TPU v7x, 128 devices: a whole 4x4x4 slice. The times are simulated.
128 devices in a mesh: tm: 4 (over x), space: 32 (over z, y, core).
Axes of the slice: x: 4, y: 4, z: 4, core: 2. Of those that a mesh axis runs over, the one named last changes fastest.
Arguments:
- initial: float32 [3, 1024, 1024], P(None, 'space'), may hold values from -6 to 6
- guess: float32 [8, 3, 1024, 1024], P('tm', None, 'space'), may hold values from -6 to 6
- depth: float32 [1024, 1024], P('space'), may hold values from 0.2 to 1
- friction: float32 [1024, 1024], P('space'), may hold values from 0.005 to 0.1
- mask: int32 [1024, 1024], P('space'), may hold values 0 or 1
- wind: float32 [8, 2, 1024, 1024], P('tm', None, 'space'), may hold values from -6 to 6
Outputs:
- corrected: float32 [8, 3, 1024, 1024], P('tm', None, 'space')
Inputs may be any that keep to these rules, and one draw needn't show every extreme that they name: `mask`: 1 marks a sea cell, 0 a land cell.
All inputs are finite; a program needn't handle non-finite values. No bound on the sum of `mask` on one device may be relied on, other than what follows from the above.
Results may differ from a plain program's by a relative error of at most 0.000039.
Values sent between devices are 32-bit elements; how exact they have to be, the bound alone decides.
No kernel may reach another device: no remote copies, remote signals or barrier semaphores. Data moves between devices by JAX's collectives and lax.ppermute only.
A program may use at most 64 MiB of HBM per device.

v0:
```python
import jax
import jax.numpy as jnp
from jax import lax
from jax.sharding import PartitionSpec as P

FACTOR = 16


delta_fine = 0.05


def with_halo(value, sides, width):
    for axis, dim in sides:
        devices, length = (lax.axis_size(axis), value.shape[dim])
        up = [(i, (i + 1) % devices) for i in range(devices - 1)]
        down = [(j, i) for i, j in up]
        last = lax.slice_in_dim(value, length - width, length, axis=dim)
        leading = lax.slice_in_dim(value, 0, width, axis=dim)
        before = lax.ppermute(last, axis, up)
        after = lax.ppermute(leading, axis, down)
        value = jnp.concatenate([before, value, after], axis=dim)
    return value


def passed_along(block, axis, distance):
    devices = range(lax.axis_size(axis))
    route = [(i - distance, i) for i in devices if i - distance in devices]
    return lax.ppermute(block, axis, route)


def diff_x(field):
    padded = jnp.pad(field, [(0, 0)] * (field.ndim - 1) + [(1, 1)])
    return (padded[..., 2:] - padded[..., :-2]) * 0.5


def step_ext(state, delta, forcing, depth_r, friction_c, mask_c, inside_r):
    flux_x = depth_r * state[..., 1, :, :]
    flux_y = depth_r * state[..., 2, :, :]
    level = state[..., 0, 1:-1, :] - delta * (
        diff_x(flux_x[..., 1:-1, :]) + (flux_y[..., 2:, :] - flux_y[..., :-2, :]) * 0.5
    )
    level = level * inside_r[1:-1]
    centre = level[..., 1:-1, :]
    grad_y = (level[..., 2:, :] - level[..., :-2, :]) * 0.5
    damping = 1.0 + delta * friction_c
    u_new = (
        mask_c
        * (state[..., 1, 2:-2, :] - delta * diff_x(centre) + delta * forcing[..., 0, :, :])
        / damping
    )
    v_new = (
        mask_c * (state[..., 2, 2:-2, :] - delta * grad_y + delta * forcing[..., 1, :, :]) / damping
    )
    return jnp.stack([centre, u_new, v_new], axis=-3)


def shards(initial, guess, depth, friction, mask, wind):
    rows = depth.shape[0]
    ncols = depth.shape[1]
    count = guess.shape[0]
    rim_width = 2
    packed = jnp.concatenate(
        [
            jnp.stack([depth, friction, mask.astype(jnp.float32)]),
            wind.reshape(count * 2, rows, ncols),
        ],
        axis=0,
    )
    packed = with_halo(packed, (("space", 1),), rim_width)
    coefficient = packed[:3]
    forcing_ext = packed[3:].reshape(count, 2, rows + 2 * rim_width, ncols)
    space_index = lax.axis_index("space")
    total_rows = rows * lax.axis_size("space")

    def window(array, reach):
        return array[..., rim_width - reach : rim_width + rows + reach, :]

    forcing_here = window(forcing_ext, 0)
    coeff_zero = window(coefficient, 0)
    coeff_two = window(coefficient, 2)

    def fine_two(state):
        depth_ext = coeff_two[0]
        velocity = with_halo(state[:, 1:3], (("space", 2),), 1)
        flux_x = depth_ext[2 : rows + 2] * state[:, 1]
        flux_y = depth_ext[1 : rows + 3] * velocity[:, 1]
        level = state[:, 0] - delta_fine * (diff_x(flux_x) + (flux_y[:, 2:] - flux_y[:, :-2]) * 0.5)
        level_ext = with_halo(level, (("space", 1),), 1)
        grad_y = (level_ext[:, 2:] - level_ext[:, :-2]) * 0.5
        damping = 1.0 + delta_fine * coeff_zero[1]
        u_new = (
            coeff_zero[2]
            * (state[:, 1] - delta_fine * diff_x(level) + delta_fine * forcing_here[:, 0])
            / damping
        )
        v_new = (
            coeff_zero[2]
            * (state[:, 2] - delta_fine * grad_y + delta_fine * forcing_here[:, 1])
            / damping
        )
        return jnp.stack([level, u_new, v_new], axis=1)

    def sweep(start):
        return lax.fori_loop(0, FACTOR, lambda i, s: fine_two(s), start)

    zero_force = jnp.zeros((2, rows, ncols), jnp.float32)
    position = space_index * rows - 2 + jnp.arange(rows + 2 * 2, dtype=jnp.int32)
    inside_two = ((position >= 0) & (position < total_rows)).astype(jnp.float32)[:, None]

    def coarse(state):
        whole = with_halo(state, (("space", 1),), 2)
        return step_ext(
            whole,
            delta_fine * FACTOR,
            zero_force,
            coeff_two[0],
            coeff_zero[1],
            coeff_zero[2],
            inside_two,
        )

    tm_index = lax.axis_index("tm")
    earlier = passed_along(guess[-1], "tm", 1)
    entry = jnp.where(tm_index == 0, initial, earlier)
    first = sweep(jnp.concatenate([entry[None], guess[:-1]], axis=0))
    earlier = passed_along(first[-1], "tm", 1)
    entry = jnp.where(tm_index == 0, initial, earlier)
    second = sweep(jnp.concatenate([entry[None], first[:-1]], axis=0))
    resid = second - first

    def local_chain(incoming):

        def link(carried, term):
            fresh = coarse(carried) + term
            return (fresh, fresh)

        _, chain = lax.scan(link, incoming, resid)
        return chain

    chain = local_chain(jnp.zeros_like(initial))

    def turn(position, chain_now):
        received = passed_along(chain_now[-1], "tm", 1)
        fresh = local_chain(received)
        return jnp.where(tm_index == position, fresh, chain_now)

    chain = lax.fori_loop(1, lax.axis_size("tm"), turn, chain)
    return first + chain


def solution(mesh):
    return jax.shard_map(
        shards,
        mesh=mesh,
        in_specs=(
            P(None, "space", None),
            P("tm", None, "space", None),
            P("space", None),
            P("space", None),
            P("space", None),
            P("tm", None, "space", None),
        ),
        out_specs=P("tm", None, "space", None),
        check_vma=False,
    )
```

profile of v0, /device:TPU:34, one launch (start us, length us, event | category | flops | bytes accessed | tf_op | source)
XLA Modules:
  0.0 890.0 jit_solution(11334994700635552410)
XLA Ops:
  6.8 5.8 collective-permute-start.15
  18.1 361.1 %while.95 = (s32[]{:T(128)}, f32[2,3,32,1024]{3,2,0,1:T(8,128)S(1)}, f32[3,36,1024]{2,1,0:T(8,128)S(1)}, f32[3,32,1024]{2,1,0:T(8,128)S(1)}, f32[2,2,32,1024]{3,2,0,1:T(8,128)S(1)}, /*index=5*/s32[]{:T(128)}) while((s32[]{:T(128)}, f32[2,3,32,1024]{3,2,0,1:T(8,128)S(1)}, f32[3,36,1024]{2,1,0:T(8,128)S(1)}, f32[3,32,1024]{2,1,0:T(8,128)S(1)}, ...), condition=%wide.region_1.2_spmd, body=%wide.region_0.1_spmd.sunk | while | flops 2109442 | bytes 9036005 | solution.py:104
  18.1 5.8 collective-permute-start
  33.3 5.8 collective-permute-start.3
  40.8 5.7 collective-permute-start
  55.9 5.8 collective-permute-start.3
  63.3 5.7 collective-permute-start
  78.5 5.8 collective-permute-start.3
  85.9 5.7 collective-permute-start
  101.0 5.8 collective-permute-start.3
  108.5 5.7 collective-permute-start
  123.6 5.8 collective-permute-start.3
  131.0 5.7 collective-permute-start
  146.2 5.8 collective-permute-start.3
  153.6 5.7 collective-permute-start
  168.7 5.8 collective-permute-start.3
  176.2 5.7 collective-permute-start
  191.3 5.8 collective-permute-start.3
  198.7 5.7 collective-permute-start
  213.8 5.8 collective-permute-start.3
  236.4 5.8 collective-permute-start.3
  243.9 5.7 collective-permute-start
  259.0 5.8 collective-permute-start.3
  281.5 5.8 collective-permute-start.3
  289.0 5.7 collective-permute-start
  304.1 5.8 collective-permute-start.3
  326.7 5.8 collective-permute-start.3
  334.1 5.7 collective-permute-start
  349.2 5.8 collective-permute-start.3
  371.8 5.8 collective-permute-start.3
  382.4 6.5 collective-permute-done.16
  389.0 360.8 %while.96 = (s32[]{:T(128)}, f32[2,3,32,1024]{3,2,0,1:T(8,128)S(1)}, f32[3,36,1024]{2,1,0:T(8,128)S(1)}, f32[3,32,1024]{2,1,0:T(8,128)S(1)}, f32[2,2,32,1024]{3,2,0,1:T(8,128)S(1)}, /*index=5*/s32[]{:T(128)}) while((s32[]{:T(128)}, f32[2,3,32,1024]{3,2,0,1:T(8,128)S(1)}, f32[3,36,1024]{2,1,0:T(8,128)S(1)}, f32[3,32,1024]{2,1,0:T(8,128)S(1)}, ...), condition=%wide.region_3.4_spmd, body=%wide.region_2.3_spmd.sunk | while | flops 2109442 | bytes 9036005 | solution.py:104
  403.7 5.8 collective-permute-start.7
  411.2 5.7 collective-permute-start.4
  426.3 5.8 collective-permute-start.7
  433.8 5.7 collective-permute-start.4
  448.9 5.8 collective-permute-start.7
  471.5 5.8 collective-permute-start.7
  478.9 5.7 collective-permute-start.4
  494.1 5.8 collective-permute-start.7
  516.6 5.8 collective-permute-start.7
  539.2 5.8 collective-permute-start.7
  546.7 5.7 collective-permute-start.4
  561.8 5.8 collective-permute-start.7
  584.4 5.8 collective-permute-start.7
  607.0 5.8 collective-permute-start.7
  614.4 5.7 collective-permute-start.4
  629.5 5.8 collective-permute-start.7
  652.1 5.8 collective-permute-start.7
  659.6 5.7 collective-permute-start.4
  674.7 5.8 collective-permute-start.7
  697.3 5.8 collective-permute-start.7
  719.9 5.8 collective-permute-start.7
  727.3 5.7 collective-permute-start.4
  742.4 5.8 collective-permute-start.7
  750.0 28.7 %while.99 = (s32[]{:T(128)}, f32[3,32,1024]{2,1,0:T(8,128)}, f32[2,3,32,1024]{3,2,1,0:T(8,128)}, f32[3,36,1024]{2,1,0:T(8,128)S(1)}, f32[36,1]{0,1:T(1,128)S(1)}...) while((s32[]{:T(128)}, f32[3,32,1024]{2,1,0:T(8,128)}, ...), condition=%wide.region_5.6_spmd.clone, body=%wide.region_4.5_spmd.clone.sunk | while | flops 1583107 | bytes 14451351 | solution.py:137
  750.1 5.7 collective-permute-start.8
  778.7 109.2 %while.98 = (s32[]{:T(128)}, f32[2,3,32,1024]{3,2,1,0:T(8,128)}, s32[]{:T(128)}, f32[3,36,1024]{2,1,0:T(8,128)S(1)}, f32[3,32,1024]{2,1,0:T(8,128)S(1)}, /*index...) while((s32[]{:T(128)}, f32[2,3,32,1024]{3,2,1,0:T(8,128)}, ...), condition=%wide.region_9.10_spmd.clone, body=%wide.region_6.9_spmd.clone.sunk | while | flops 1681593 | bytes 18383864 | solution.py:147
  782.9 6.5 collective-permute-done.12
  789.4 23.6 %while.100 = (s32[]{:T(128)}, f32[3,32,1024]{2,1,0:T(8,128)S(1)}, f32[2,3,32,1024]{3,2,1,0:T(8,128)}, f32[3,36,1024]{2,1,0:T(8,128)S(1)}, f32[36,1]{0,1:T(1,128)...) while((s32[]{:T(128)}, f32[3,32,1024]{2,1,0:T(8,128)S(1)}, ...), condition=%wide.region_8.8_spmd, body=%wide.region_7.7_spmd.sunk | while | flops 1484802 | bytes 13664901 | solution.py:137
  819.3 6.5 collective-permute-done.12
  825.8 23.6 %while.100 = (s32[]{:T(128)}, f32[3,32,1024]{2,1,0:T(8,128)S(1)}, f32[2,3,32,1024]{3,2,1,0:T(8,128)}, f32[3,36,1024]{2,1,0:T(8,128)S(1)}, f32[36,1]{0,1:T(1,128)...) while((s32[]{:T(128)}, f32[3,32,1024]{2,1,0:T(8,128)S(1)}, ...), condition=%wide.region_8.8_spmd, body=%wide.region_7.7_spmd.sunk | while | flops 1484802 | bytes 13664901 | solution.py:137
  855.7 6.5 collective-permute-done.12
  862.2 23.6 %while.100 = (s32[]{:T(128)}, f32[3,32,1024]{2,1,0:T(8,128)S(1)}, f32[2,3,32,1024]{3,2,1,0:T(8,128)}, f32[3,36,1024]{2,1,0:T(8,128)S(1)}, f32[36,1]{0,1:T(1,128)...) while((s32[]{:T(128)}, f32[3,32,1024]{2,1,0:T(8,128)S(1)}, ...), condition=%wide.region_8.8_spmd, body=%wide.region_7.7_spmd.sunk | while | flops 1484802 | bytes 13664901 | solution.py:137
  (761 shorter events, 554.4 us)
Async XLA Ops:
  1.3 14.7 %collective-permute-start.13 = (f32[3,32,1024]{2,1,0:T(8,128)S(1)}, f32[3,32,1024]{2,1,0:T(8,128)}, u32[]{:S(2)}, u32[]{:S(2)}) collective-permute-start(f32[3,32,1024]{2,1,0:T(8,128)S(1)} %get-tuple-element.747), channel_id=1, source_target_pairs={{0,32},{32,64},{64,96},{1,33},{33,65},{65,97},{2,34},{34,66},{66,9... | collective-permute-start | bytes 1179656 | tf_op jit(solution)/shard_map/ppermute | solution.py:28
  4.9 7.7 collective-permute-start.14
  18.1 7.9 collective-permute-start
  40.8 7.8 collective-permute-start
  54.0 7.7 collective-permute-start.2
  63.3 7.8 collective-permute-start
  76.5 7.7 collective-permute-start.2
  85.9 7.8 collective-permute-start
  99.1 7.7 collective-permute-start.2
  108.5 7.8 collective-permute-start
  121.7 7.7 collective-permute-start.2
  131.0 7.8 collective-permute-start
  144.2 7.7 collective-permute-start.2
  153.6 7.8 collective-permute-start
  166.8 7.7 collective-permute-start.2
  176.2 7.8 collective-permute-start
  189.4 7.7 collective-permute-start.2
  198.7 7.8 collective-permute-start
  211.9 7.7 collective-permute-start.2
  221.3 7.8 collective-permute-start
  234.5 7.7 collective-permute-start.2
  243.9 7.8 collective-permute-start
  257.0 7.7 collective-permute-start.2
  266.4 7.8 collective-permute-start
  279.6 7.7 collective-permute-start.2
  289.0 7.8 collective-permute-start
  302.2 7.7 collective-permute-start.2
  311.5 7.8 collective-permute-start
  324.7 7.7 collective-permute-start.2
  334.1 7.8 collective-permute-start
  347.3 7.7 collective-permute-start.2
  356.7 7.8 collective-permute-start
  369.9 7.7 collective-permute-start.2
  379.2 9.7 %collective-permute-start.16 = (f32[3,32,1024]{2,1,0:T(8,128)S(1)}, f32[3,32,1024]{2,1,0:T(8,128)S(1)}, u32[]{:S(2)}, u32[]{:S(2)}) collective-permute-start(f32[3,32,1024]{2,1,0:T(8,128)S(1)} %slice_bitcast_fusion.17), channel_id=1, source_target_pairs={{0,32},{32,64},{64,96},{1,33},{33,65},{65,97},{2,34},{34,66},{66,9... | collective-permute-start | bytes 1179656 | tf_op jit(solution)/shard_map/ppermute | solution.py:28
  401.8 7.7 collective-permute-start.6
  411.2 7.8 collective-permute-start.4
  424.4 7.7 collective-permute-start.6
  433.8 7.8 collective-permute-start.4
  447.0 7.7 collective-permute-start.6
  456.4 7.8 collective-permute-start.4
  469.5 7.7 collective-permute-start.6
  478.9 7.8 collective-permute-start.4
  492.1 7.7 collective-permute-start.6
  501.5 7.8 collective-permute-start.4
  514.7 7.7 collective-permute-start.6
  524.1 7.8 collective-permute-start.4
  537.3 7.7 collective-permute-start.6
  546.7 7.8 collective-permute-start.4
  569.3 7.8 collective-permute-start.4
  582.4 7.7 collective-permute-start.6
  591.8 7.8 collective-permute-start.4
  605.0 7.7 collective-permute-start.6
  614.4 7.8 collective-permute-start.4
  627.6 7.7 collective-permute-start.6
  637.0 7.8 collective-permute-start.4
  650.2 7.7 collective-permute-start.6
  659.6 7.8 collective-permute-start.4
  682.2 7.8 collective-permute-start.4
  704.7 7.8 collective-permute-start.4
  727.3 7.8 collective-permute-start.4
  750.1 7.7 collective-permute-start.8
  779.7 9.7 %collective-permute-start.12 = (f32[3,32,1024]{2,1,0:T(8,128)S(1)}, f32[3,32,1024]{2,1,0:T(8,128)S(1)}, u32[]{:S(2)}, u32[]{:S(2)}) collective-permute-start(f32[3,32,1024]{2,1,0:T(8,128)S(1)} %slice_bitcast_fusion.34), channel_id=1, source_target_pairs={{0,32},{32,64},{64,96},{1,33},{33,65},{65,97},{2,34},{34,66},{66,9... | collective-permute-start | bytes 1179656 | tf_op jit(solution)/shard_map/while/body/eval_jaxpr/ppermute | solution.py:28
  816.1 9.7 %collective-permute-start.12 = (f32[3,32,1024]{2,1,0:T(8,128)S(1)}, f32[3,32,1024]{2,1,0:T(8,128)S(1)}, u32[]{:S(2)}, u32[]{:S(2)}) collective-permute-start(f32[3,32,1024]{2,1,0:T(8,128)S(1)} %slice_bitcast_fusion.34), channel_id=1, source_target_pairs={{0,32},{32,64},{64,96},{1,33},{33,65},{65,97},{2,34},{34,66},{66,9... | collective-permute-start | bytes 1179656 | tf_op jit(solution)/shard_map/while/body/eval_jaxpr/ppermute | solution.py:28
  852.5 9.7 %collective-permute-start.12 = (f32[3,32,1024]{2,1,0:T(8,128)S(1)}, f32[3,32,1024]{2,1,0:T(8,128)S(1)}, u32[]{:S(2)}, u32[]{:S(2)}) collective-permute-start(f32[3,32,1024]{2,1,0:T(8,128)S(1)} %slice_bitcast_fusion.34), channel_id=1, source_target_pairs={{0,32},{32,64},{64,96},{1,33},{33,65},{65,97},{2,34},{34,66},{66,9... | collective-permute-start | bytes 1179656 | tf_op jit(solution)/shard_map/while/body/eval_jaxpr/ppermute | solution.py:28
  (112 other events, 645.4 us)
where the time goes:
time: 895 us; the launch traced here: 890 us
  starting transfers between devices  551 us (62%)
  waiting for transfers between devices  272 us (30%)
  other arithmetic  36.4 us (4%)
  local copies, waits for them, and re-layouts  25.5 us (3%)
    ppermute x73, starting transfers between devices, with_halo(): after = lax.ppermute(leading, axis, down)  392 us
    ppermute x73, waiting for transfers between devices, with_halo(): before = lax.ppermute(last, axis, up)  202 us
    ppermute x73, starting transfers between devices, with_halo(): before = lax.ppermute(last, axis, up)  144 us
    ppermute x73, waiting for transfers between devices, with_halo(): after = lax.ppermute(leading, axis, down)  43.5 us
    ppermute x5, waiting for transfers between devices, passed_along(): return lax.ppermute(block, axis, route)  26.1 us
  transfers between devices with their start and end apart: 151, of which 77 were waited for; matrix products, arithmetic and copies ran while one was open for 1% of the time, Pallas kernels for 0%

commit v1 on v0

v1 whole, which is shorter than its diff:
```python
import jax
import jax.numpy as jnp
from jax import lax
from jax.experimental import pallas as pl
from jax.experimental.pallas import tpu as pltpu
from jax.sharding import PartitionSpec as P

FACTOR = 16
H = 0.05
C = 0.5 * H
CHUNK = 8
PAD = 16


def ring(n, shift):
    return [(i, (i + shift) % n) for i in range(n)]


def lane_masks():
    lane = lax.broadcasted_iota(jnp.int32, (8, 128), 1)
    sub = lax.broadcasted_iota(jnp.int32, (8, 128), 0)
    return (
        lane == 0,
        lane == 127,
        (lane == 0) & (sub == 0),
        (lane == 127) & (sub == 7),
    )


def diff_cols(f, masks):
    first, last, corner_lo, corner_hi = masks
    left = pltpu.roll(f, 1, 1)
    right = pltpu.roll(f, 127, 1)
    left = jnp.where(first, pltpu.roll(left, 1, 0), left)
    right = jnp.where(last, pltpu.roll(right, 7, 0), right)
    left = jnp.where(corner_lo, 0.0, left)
    right = jnp.where(corner_hi, 0.0, right)
    return right - left


def row_at(ref, r):
    return ref[pl.ds(pl.multiple_of(r * 8, 8), 8), :]


def put_row(ref, r, value):
    ref[pl.ds(pl.multiple_of(r * 8, 8), 8), :] = value


def spread(dst, base, src, lead, rows, scale=None, start=0):
    def group(g, _):
        for j in range(8):
            val = src[lead + (pl.ds(pl.multiple_of(start + g * 8, 8), 8), pl.ds(j * 128, 128))]
            if scale is not None:
                val = val * scale
            dst[pl.ds((base + g * 8) * 8 + j, 8, stride=8), :] = val
        return 0

    lax.fori_loop(0, rows // 8, group, 0)


def gather_rows(src, base, g, j):
    return src[pl.ds((base + g * 8) * 8 + j, 8, stride=8), :]


def one_step(E, U, V, D, A, W, lo, n, top, bottom, gain, masks, write=None):
    chunks = (n + CHUNK - 1) // CHUNK

    def flux_y(r):
        return row_at(D, r) * row_at(V, r)

    def level(r, above, below):
        flux = diff_cols(row_at(D, r) * row_at(U, r), masks) + (below - above)
        if gain != 1.0:
            flux = flux * gain
        keep = jnp.where((r == top) | (r == bottom), 0.0, 1.0)
        return (row_at(E, r) - flux) * keep

    f0, f1, f2, f3 = (flux_y(lo + k) for k in (-2, -1, 0, 1))
    before = level(lo - 1, f0, f2)
    here = level(lo, f1, f3)
    put_row(E, lo, here)

    def body(k, carry):
        fa, fb, ea, eb = carry
        r = lo + k * CHUNK
        for i in range(CHUNK):
            fc = flux_y(r + i + 2)
            ec = level(r + i + 1, fa, fc)
            a = row_at(A, r + i)
            gx = diff_cols(eb, masks)
            gy = ec - ea
            if gain != 1.0:
                gx, gy = gx * gain, gy * gain
            un = a * (row_at(U, r + i) - gx)
            vn = a * (row_at(V, r + i) - gy)
            if W is not None:
                un = un + row_at(W[0], r + i)
                vn = vn + row_at(W[1], r + i)
            put_row(E, r + i + 1, ec)
            put_row(U, r + i, un)
            put_row(V, r + i, vn)
            fa, fb, ea, eb = fb, fc, eb, ec
        return fa, fb, ea, eb

    lax.fori_loop(0, chunks, body, (f2, f3, before, here))


def sweep_steps(E, U, V, D, A, W, lo0, rows0, top, bottom, masks):
    def step(s, _):
        one_step(E, U, V, D, A, W, lo0 + 2 * s, rows0 - 4 * s, top, bottom, 1.0, masks)
        return 0

    lax.fori_loop(1, FACTOR + 1, step, 0)


def edge_rows(space, top_row, bottom_row):
    size = lax.axis_size("space")
    return jnp.where(space == 0, top_row, -1), jnp.where(space == size - 1, bottom_row, -1)


def fine_kernel(n, space_ref, own, up, dn, wind, wup, wdn, coef, cup, cdn, nxt, first, delta, E, U, V, D, A, W0, W1):
    masks = lane_masks()
    space = space_ref[0]
    top, bottom = edge_rows(space, n - 1, 2 * n)
    in_up = jnp.where(space == 0, 0.0, 1.0)
    in_dn = jnp.where(space == lax.axis_size("space") - 1, 0.0, 1.0)
    for base, st, wd, cf, inside in ((0, up, wup, cup, in_up), (n, own, wind, coef, 1.0), (2 * n, dn, wdn, cdn, in_dn)):
        spread(D, base, cf, (0,), n, inside * (C * C))
        spread(A, base, cf, (1,), n, inside)
        spread(E, base, st, (0,), n, C)
        spread(U, base, st, (1,), n)
        spread(V, base, st, (2,), n)
        spread(W0, base, wd, (0,), n, H)
        spread(W1, base, wd, (1,), n, H)

    def force(r, _):
        a = row_at(A, r)
        put_row(W0, r, a * row_at(W0, r))
        put_row(W1, r, a * row_at(W1, r))
        return 0

    lax.fori_loop(0, 3 * n, force, 0)
    sweep_steps(E, U, V, D, A, (W0, W1), 0, 3 * n, top, bottom, masks)

    def out(g, _):
        rows = pl.ds(pl.multiple_of(g * 8, 8), 8)
        for f, src in enumerate((E, U, V)):
            for j in range(8):
                cols = pl.ds(j * 128, 128)
                val = gather_rows(src, n, g, j)
                if f == 0:
                    val = val * (1.0 / C)
                first[f, rows, cols] = val
                delta[f, rows, cols] = val - nxt[f, rows, cols]
        return 0

    lax.fori_loop(0, n // 8, out, 0)


def relax_kernel(n, space_ref, d1, d1u, d1d, d1uu, d1dd, d2, d2u, d2d, coef, cup, cdn, cuu, cdd, r1, c1, E, U, V, D, A, E2, U2, V2):
    masks = lane_masks()
    space = space_ref[0]
    off = n + 8
    size = lax.axis_size("space")
    top, bottom = edge_rows(space, off - 1, off + n)
    in_up = jnp.where(space == 0, 0.0, 1.0)
    in_dn = jnp.where(space == size - 1, 0.0, 1.0)
    in_uu = jnp.where(space <= 1, 0.0, 1.0)
    in_dd = jnp.where(space >= size - 2, 0.0, 1.0)
    for base, rows, cf, inside in ((0, 8, cuu, in_uu), (8, n, cup, in_up), (off, n, coef, 1.0), (off + n, n, cdn, in_dn), (off + 2 * n, 8, cdd, in_dd)):
        spread(D, base, cf, (0,), rows, inside * (C * C))
        spread(A, base, cf, (1,), rows, inside)
    for base, rows, st in ((0, 8, d1uu), (8, n, d1u), (off, n, d1), (off + n, n, d1d), (off + 2 * n, 8, d1dd)):
        spread(E, base, st, (0,), rows, C)
        spread(U, base, st, (1,), rows)
        spread(V, base, st, (2,), rows)
    for base, st in ((8, d2u), (off, d2), (off + n, d2d)):
        spread(E2, base, st, (0,), n, C)
        spread(U2, base, st, (1,), n)
        spread(V2, base, st, (2,), n)
    sweep_steps(E2, U2, V2, D, A, None, 8, 3 * n, top, bottom, masks)
    sweep_steps(E, U, V, D, A, None, 6, 3 * n + 4, top, bottom, masks)

    def out_r(g, _):
        rows = pl.ds(pl.multiple_of(g * 8, 8), 8)
        for f, src in enumerate((E, U, V)):
            for j in range(8):
                cols = pl.ds(j * 128, 128)
                r1[f, rows, cols] = gather_rows(src, off, g, j)
        return 0

    lax.fori_loop(0, n // 8, out_r, 0)

    def coarse_coef(r, _):
        a = row_at(A, off - 2 + r)
        put_row(A, off - 2 + r, a / (float(FACTOR) - (FACTOR - 1.0) * a))
        return 0

    lax.fori_loop(0, n + 4, coarse_coef, 0)
    one_step(E, U, V, D, A, None, off, n, top, bottom, float(FACTOR), masks)

    def out_c(g, _):
        rows = pl.ds(pl.multiple_of(g * 8, 8), 8)
        for f, (src, more) in enumerate(((E, E2), (U, U2), (V, V2))):
            for j in range(8):
                cols = pl.ds(j * 128, 128)
                c1[f, rows, cols] = gather_rows(src, off, g, j) + gather_rows(more, off, g, j)
        return 0

    lax.fori_loop(0, n // 8, out_c, 0)


HALO = 16


def chain_kernel(n, pos_ref, ca, cau, cad, cb, cbu, cbd, cc, ccu, ccd, coef, cup, cdn, r1, fa, fb, out, E, U, V, D, A, X, Y, Z):
    masks = lane_masks()
    tm, space = pos_ref[0], pos_ref[1]
    off = HALO
    top, bottom = edge_rows(space, off - 1, off + n)
    in_up = jnp.where(space == 0, 0.0, 1.0)
    in_dn = jnp.where(space == lax.axis_size("space") - 1, 0.0, 1.0)
    spread(D, 0, cup, (0,), HALO, in_up * (C * C), start=n - HALO)
    spread(A, 0, cup, (1,), HALO, in_up, start=n - HALO)
    spread(D, off, coef, (0,), n, C * C)
    spread(A, off, coef, (1,), n)
    spread(D, off + n, cdn, (0,), HALO, in_dn * (C * C))
    spread(A, off + n, cdn, (1,), HALO, in_dn)

    def coarse_coef(r, _):
        a = row_at(A, r)
        put_row(A, r, a / (float(FACTOR) - (FACTOR - 1.0) * a))
        return 0

    lax.fori_loop(0, n + 2 * HALO, coarse_coef, 0)

    def take(dst, f, own, u, d, use):
        spread(dst, 0, u, (f,), HALO, use)
        spread(dst, off, own, (f,), n, use)
        spread(dst, off + n, d, (f,), HALO, use)

    for f, dst in enumerate((E, U, V)):
        take(dst, f, cc, ccu, ccd, jnp.where(tm >= 3, 1.0, 0.0))

    def coarse(lo, rows):
        one_step(E, U, V, D, A, None, lo, rows, top, bottom, float(FACTOR), masks)

    def add(lo, rows):
        def body(r, _):
            for dst, src in ((E, X), (U, Y), (V, Z)):
                put_row(dst, lo + r, row_at(dst, lo + r) + row_at(src, lo + r))
            return 0

        lax.fori_loop(0, rows, body, 0)

    coarse(off - 8, n + 16)
    coarse(off - 6, n + 12)
    for f, dst in enumerate((X, Y, Z)):
        take(dst, f, cb, cbu, cbd, jnp.where(tm >= 2, 1.0, 0.0))
    add(off - 6, n + 12)
    coarse(off - 4, n + 8)
    coarse(off - 2, n + 4)
    for f, dst in enumerate((X, Y, Z)):
        take(dst, f, ca, cau, cad, jnp.where(tm >= 1, 1.0, 0.0))
    add(off - 2, n + 4)

    def write(k, first, more):
        def group(g, _):
            rows = pl.ds(pl.multiple_of(g * 8, 8), 8)
            for f, src in enumerate((E, U, V)):
                for j in range(8):
                    cols = pl.ds(j * 128, 128)
                    val = gather_rows(src, off, g, j)
                    if more is not None:
                        val = val + more[f, rows, cols]
                    if f == 0:
                        val = val * (1.0 / C)
                    out[k, f, rows, cols] = first[f, rows, cols] + val
            return 0

        lax.fori_loop(0, n // 8, group, 0)

    write(0, fa, None)
    coarse(off, n)
    write(1, fb, r1)


def call(kernel, n, rows, fields, outs, *args):
    scratch = [pltpu.VMEM(((rows + PAD) * 8, 128), jnp.float32)] * fields
    vmem = pl.BlockSpec(memory_space=pltpu.VMEM)
    return pl.pallas_call(
        lambda *refs: kernel(n, *refs),
        out_shape=outs,
        in_specs=[pl.BlockSpec(memory_space=pltpu.SMEM)] + [vmem] * (len(args) - 1),
        out_specs=jax.tree.map(lambda _: vmem, outs),
        scratch_shapes=scratch,
        compiler_params=pltpu.CompilerParams(vmem_limit_bytes=32 * 2**20),
    )(*args)


def shards(initial, guess, depth, friction, mask, wind):
    n, ncols = depth.shape
    spaces, times = lax.axis_size("space"), lax.axis_size("tm")
    tm, space = lax.axis_index("tm"), lax.axis_index("space")
    pos = jnp.stack([tm, space]).astype(jnp.int32)
    where = space.astype(jnp.int32)[None]

    def sides(x, hop=1):
        return lax.ppermute(x, "space", ring(spaces, hop)), lax.ppermute(x, "space", ring(spaces, -hop))

    def ends(x, rows, hop=1):
        up = lax.ppermute(x[:, n - rows :], "space", ring(spaces, hop))
        dn = lax.ppermute(x[:, :rows], "space", ring(spaces, -hop))
        return up, dn

    state = jax.ShapeDtypeStruct((3, n, ncols), jnp.float32)
    coef = jnp.stack([depth, mask.astype(jnp.float32) / (1.0 + H * friction)])

    earlier = lax.ppermute(guess[1], "tm", ring(times, 1))
    pack_b = jnp.concatenate([guess[0], wind[1], coef])
    bu, bd = sides(pack_b)
    entry = jnp.where(tm == 0, initial, earlier)
    pack_a = jnp.concatenate([entry, wind[0]])
    au, ad = sides(pack_a)
    cuu, cdd = ends(coef, 8, 2)

    fb, db = call(fine_kernel, n, 3 * n, 7, (state, state), where, guess[0], bu[:3], bd[:3], wind[1], bu[3:5], bd[3:5], coef, bu[5:], bd[5:], guess[1])
    dbu, dbd = sides(db)
    fa, da = call(fine_kernel, n, 3 * n, 7, (state, state), where, entry, au[:3], ad[:3], wind[0], au[3:], ad[3:], coef, bu[5:], bd[5:], guess[0])
    dau, dad = sides(da)
    dauu, dadd = ends(da, 8, 2)
    r1, c1 = call(relax_kernel, n, 3 * n + 16, 8, (state, state), where, da, dau, dad, dauu, dadd, db, dbu, dbd, coef, bu[5:], bd[5:], cuu, cdd)

    ca = lax.ppermute(c1, "tm", ring(times, 1))
    cc = lax.ppermute(c1, "tm", ring(times, -1))
    half = n // 2
    cb = jnp.concatenate(
        [lax.ppermute(ca[:, :half], "tm", ring(times, 1)), lax.ppermute(cc[:, half:], "tm", ring(times, -1))], axis=1
    )
    rim = jnp.stack([ca[:, -HALO:], cb[:, -HALO:], cc[:, -HALO:]])
    rim_up = lax.ppermute(rim, "space", ring(spaces, 1))
    rim = jnp.stack([ca[:, :HALO], cb[:, :HALO], cc[:, :HALO]])
    rim_dn = lax.ppermute(rim, "space", ring(spaces, -1))
    out = jax.ShapeDtypeStruct(guess.shape, jnp.float32)
    return call(
        chain_kernel, n, n + 2 * HALO, 8, out, pos, ca, rim_up[0], rim_dn[0], cb, rim_up[1], rim_dn[1], cc, rim_up[2], rim_dn[2],
        coef, bu[5:], bd[5:], r1, fa, fb,
    )


def solution(mesh):
    return jax.shard_map(
        shards,
        mesh=mesh,
        in_specs=(
            P(None, "space", None),
            P("tm", None, "space", None),
            P("space", None),
            P("space", None),
            P("space", None),
            P("tm", None, "space", None),
        ),
        out_specs=P("tm", None, "space", None),
        check_vma=False,
    )
```

time: 895 us -> 188 us (0.21)
  the two profiles are of different devices: /device:TPU:34 before, /device:TPU:0 now
where the time goes in v1:
time: 188 us; the launch traced here: 187 us
  Pallas kernels  105 us (56%)
  waiting for transfers between devices  38.9 us (21%)
  starting transfers between devices  30.8 us (16%)
  local copies, waits for them, and re-layouts  10.5 us (6%)
    pallas_call x4, Pallas kernels, call(): pl.pallas_call(lambda *refs: kernel(n, *refs), out_shape=outs, in_specs=[...  105 us
    ppermute x4, starting transfers between devices, sides(): lax.ppermute(x, 'space', ring(spaces, -hop))  15.3 us
    ppermute x2, waiting for transfers between devices, ends(): up = lax.ppermute(x[:, n - rows:], 'space', ring(spaces, hop))  7.93 us
    ppermute x1, waiting for transfers between devices, shards(): rim_dn = lax.ppermute(rim, 'space', ring(spaces, -1))  6.68 us
    ppermute x1, waiting for transfers between devices, shards(): ca = lax.ppermute(c1, 'tm', ring(times, 1))  6.14 us
    ppermute x1, waiting for transfers between devices, shards(): rim_up = lax.ppermute(rim, 'space', ring(spaces, 1))  5.35 us
    ppermute x2, waiting for transfers between devices, ends(): dn = lax.ppermute(x[:, :rows], 'space', ring(spaces, -hop))  4.62 us
    ppermute x2, starting transfers between devices, ends(): dn = lax.ppermute(x[:, :rows], 'space', ring(spaces, -hop))  4.51 us
  transfers between devices with their start and end apart: 19, of which 9 were waited for; matrix products, arithmetic and copies ran while one was open for 5% of the time, Pallas kernels for 26%

profile of v1, /device:TPU:0, one launch (start us, length us, event | category | flops | bytes accessed | tf_op | source)
XLA Modules:
  0.0 186.9 jit_solution(13850936089513214777)
XLA Ops:
  0.0 0.0 copy-start.1
  0.0 1.2 slice_bitcast_fusion
  1.2 0.0 copy-start.3
  1.2 0.0 copy-start.4
  1.3 1.6 collective-permute-start
  2.9 0.0 copy-done.1
  2.9 0.0 copy-done.3
  3.0 0.0 copy-done.4
  3.0 0.0 copy-start
  3.0 0.9 copy-done
  3.9 0.1 pad_maximum_fusion
  4.0 5.7 %collective-permute-start.4 = (f32[7,32,1024]{2,1,0:T(8,128)S(1)}, f32[7,32,1024]{2,1,0:T(8,128)}, u32[]{:S(2)}, u32[]{:S(2)}) collective-permute-start(f32[7,32,1024]{2,1,0:T(8,128)S(1)} %pad_maximum_fusion), channel_id=1, source_target_pairs={{0,31},{1,0},{2,1},{3,2},{4,3},{5,4},{6,5},{7,6},{8,7},{9,8},{10,9... | collective-permute-start | bytes 2752520 | tf_op jit(solution)/shard_map/ppermute | solution.py:309
  9.7 0.0 collective-permute-start.3
  9.7 3.7 %collective-permute-done = f32[3,32,1024]{2,1,0:T(8,128)} collective-permute-done((f32[3,32,1024]{2,1,0:T(8,128)S(1)}, f32[3,32,1024]{2,1,0:T(8,128)}, u32[]{:S(2)}, u32[]{:S(2)}) %collective-permute-start) | collective-permute-done | bytes 393248 | tf_op jit(solution)/shard_map/ppermute | solution.py:319
  13.4 0.0 copy-done.2
  13.4 0.1 broadcast_select_fusion.refs_1_
  13.4 0.9 pad_maximum_fusion.1
  14.3 0.0 collective-permute-start.1
  14.3 5.2 %collective-permute-start.2 = (f32[5,32,1024]{2,1,0:T(8,128)}, f32[5,32,1024]{2,1,0:T(8,128)}, u32[]{:S(2)}, u32[]{:S(2)}) collective-permute-start(f32[5,32,1024]{2,1,0:T(8,128)} %pad_maximum_fusion.1), channel_id=1, source_target_pairs={{0,31},{1,0},{2,1},{3,2},{4,3},{5,4},{6,5},{7,6},{8,7},{9,8},{10,9... | collective-permute-start | bytes 1966088 | tf_op jit(solution)/shard_map/ppermute | solution.py:309
  19.6 0.1 collective-permute-start.11
  19.7 0.9 collective-permute-done.4
  20.6 4.5 %collective-permute-start.12 = (f32[2,8,1024]{2,1,0:T(8,128)S(1)}, f32[2,8,1024]{2,1,0:T(8,128)S(1)}, u32[]{:S(2)}, u32[]{:S(2)}) collective-permute-start(f32[2,8,1024]{2,1,0:T(8,128)S(1)} %get-tuple-element.39), channel_id=1, source_target_pairs={{0,30},{1,31},{2,0},{3,1},{4,2},{5,3},{6,4},{7,5},{8,6},{9,7},{10,... | collective-permute-start | bytes 196616 | tf_op jit(solution)/shard_map/ppermute | solution.py:313
  25.1 1.1 fusion.2
  26.2 0.0 collective-permute-done.3
  26.2 1.1 fusion.3
  27.3 1.0 slice.131.refs_2_
  28.3 1.0 slice.132.refs_3_
  29.3 24.1 %shard_map.65 = (f32[3,32,1024]{2,1,0:T(8,128)S(1)}, f32[3,32,1024]{2,1,0:T(8,128)S(1)}) custom-call(s32[1]{0:T(128)} %bitcast.1.refs_0_, f32[3,32,1024]{2,1,0:T(8,128)S(1)} %get-tuple-element.21.refs_10_.refs_1_, f32[3,32,1024]{2,1,0:T(8,128)S(1)} %slice.131.refs_2_, f32[3,32,1024]{2,1,0:T(8,128)S(1)} %slice.132.refs_3_, ...), custom_call_target="tpu_custom_call" | custom-call | tf_op jit(solution)/shard_map/pallas_call | solution.py:291
  53.5 0.9 collective-permute-start.10
  54.4 0.0 collective-permute-done.1
  54.4 0.2 collective-permute-start.9
  54.6 1.0 slice.125.refs_2_
  55.6 1.0 slice.127.refs_5_
  56.6 0.0 collective-permute-done.2
  56.6 1.0 slice.126.refs_3_
  57.6 1.0 slice.128.refs_6_
  58.6 24.1 %shard_map.64 = (f32[3,32,1024]{2,1,0:T(8,128)S(1)}, f32[3,32,1024]{2,1,0:T(8,128)S(1)}) custom-call(s32[1]{0:T(128)} %bitcast.1.refs_0_, f32[3,32,1024]{2,1,0:T(8,128)S(1)} %broadcast_select_fusion.refs_1_, f32[3,32,1024]{2,1,0:T(8,128)S(1)} %slice.125.refs_2_, f32[3,32,1024]{2,1,0:T(8,128)S(1)} %slice.126.refs_3_, ...), custom_call_target="tpu_custom_call" | custom-call | tf_op jit(solution)/shard_map/pallas_call | solution.py:291
  82.7 1.7 collective-permute-start.5
  84.5 0.0 collective-permute-done.11.refs_12_
  84.5 3.4 %collective-permute-start.6 = (f32[3,32,1024]{2,1,0:T(8,128)S(1)}, f32[3,32,1024]{2,1,0:T(8,128)S(1)}, u32[]{:S(2)}, u32[]{:S(2)}) collective-permute-start(f32[3,32,1024]{2,1,0:T(8,128)S(1)} %get-tuple-element.11.refs_1_), channel_id=1, source_target_pairs={{0,31},{1,0},{2,1},{3,2},{4,3},{5,4},{6,5},{7,6},{8,7},{9,8},{10,9... | collective-permute-start | bytes 1179656 | tf_op jit(solution)/shard_map/ppermute | solution.py:309
  87.9 0.0 collective-permute-done.12.refs_13_
  87.9 0.1 collective-permute-start.7
  88.0 7.9 %collective-permute-done.7.refs_4_ = f32[3,8,1024]{2,1,0:T(8,128)S(1)} collective-permute-done((f32[3,8,1024]{2,1,0:T(8,128)S(1)}, f32[3,8,1024]{2,1,0:T(8,128)S(1)}, u32[]{:S(2)}, u32[]{:S(2)}) %collective-permute-start.7) | collective-permute-done | bytes 98336 | tf_op jit(solution)/shard_map/ppermute | solution.py:312
  95.9 0.0 collective-permute-start.8
  95.9 4.6 %collective-permute-done.8.refs_5_ = f32[3,8,1024]{2,1,0:T(8,128)S(1)} collective-permute-done((f32[3,8,1024]{2,1,0:T(8,128)S(1)}, f32[3,8,1024]{2,1,0:T(8,128)S(1)}, u32[]{:S(2)}, u32[]{:S(2)}) %collective-permute-start.8) | collective-permute-done | bytes 98336 | tf_op jit(solution)/shard_map/ppermute | solution.py:313
  100.5 0.0 collective-permute-done.10.refs_8_
  100.5 0.0 collective-permute-done.9.refs_7_
  100.5 0.0 collective-permute-done.5.refs_2_
  100.5 0.0 collective-permute-done.6.refs_3_
  100.6 48.3 %shard_map.66 = (f32[3,32,1024]{2,1,0:T(8,128)S(1)}, f32[3,32,1024]{2,1,0:T(8,128)S(1)}) custom-call(s32[1]{0:T(128)} %bitcast.1.refs_0_, f32[3,32,1024]{2,1,0:T(8,128)S(1)} %get-tuple-element.11.refs_1_, f32[3,32,1024]{2,1,0:T(8,128)S(1)} %collective-permute-done.5.refs_2_, f32[3,32,1024]{2,1,0:T(8,128)S(1)} %collective-permute-done.6.refs_3_, ...), custom_call_target="tpu_custom_call" | custom-call | tf_op jit(solution)/shard_map/pallas_call | solution.py:291
  148.8 1.6 collective-permute-start.13
  150.4 1.7 collective-permute-start.14
  152.2 6.1 %collective-permute-done.13.refs_1_ = f32[3,32,1024]{2,1,0:T(8,128)S(1)} collective-permute-done((f32[3,32,1024]{2,1,0:T(8,128)S(1)}, f32[3,32,1024]{2,1,0:T(8,128)S(1)}, u32[]{:S(2)}, u32[]{:S(2)}) %collective-permute-start.13) | collective-permute-done | bytes 393248 | tf_op jit(solution)/shard_map/ppermute | solution.py:334
  158.3 1.3 collective-permute-start.17
  159.7 0.0 collective-permute-done.14.refs_7_
  159.7 2.0 %collective-permute-start.15 = (f32[3,16,1024]{2,1,0:T(8,128)S(1)}, f32[3,16,1024]{2,1,0:T(8,128)S(1)}, u32[]{:S(2)}, u32[]{:S(2)}) collective-permute-start(f32[3,16,1024]{2,1,0:T(8,128)S(1)} %get-tuple-element.36), channel_id=1, source_target_pairs={{0,96},{32,0},{64,32},{96,64},{1,97},{33,1},{65,33},{97,65},{2,98}... | collective-permute-start | bytes 589832 | tf_op jit(solution)/shard_map/ppermute | solution.py:338
  161.8 3.5 %collective-permute-done.17 = f32[3,16,1024]{2,1,0:T(8,128)S(1)} collective-permute-done((f32[3,16,1024]{2,1,0:T(8,128)S(1)}, f32[3,16,1024]{2,1,0:T(8,128)S(1)}, u32[]{:S(2)}, u32[]{:S(2)}) %collective-permute-start.17) | collective-permute-done | bytes 196640 | tf_op jit(solution)/shard_map/ppermute | solution.py:338
  165.3 0.1 collective-permute-start.18
  165.4 0.1 collective-permute-done.15
  165.5 0.5 collective-permute-start.16
  166.0 0.1 pad_add_fusion.refs_0_
  166.1 6.7 %collective-permute-done.18 = f32[3,3,16,1024]{3,2,1,0:T(8,128)S(1)} collective-permute-done((f32[3,3,16,1024]{3,2,1,0:T(8,128)S(1)}, f32[3,3,16,1024]{3,2,1,0:T(8,128)S(1)}, u32[]{:S(2)}, u32[]{:S(2)}) %collective-permute-start.18) | collective-permute-done | bytes 589856 | tf_op jit(solution)/shard_map/ppermute | solution.py:343
  172.9 5.3 %collective-permute-done.16 = f32[3,3,16,1024]{3,2,1,0:T(8,128)S(1)} collective-permute-done((f32[3,3,16,1024]{3,2,1,0:T(8,128)S(1)}, f32[3,3,16,1024]{3,2,1,0:T(8,128)S(1)}, u32[]{:S(2)}, u32[]{:S(2)}) %collective-permute-start.16) | collective-permute-done | bytes 589856 | tf_op jit(solution)/shard_map/ppermute | solution.py:341
  178.3 8.7 %shard_map.67 = f32[2,3,32,1024]{3,2,1,0:T(8,128)} custom-call(s32[2]{0:T(128)S(1)} %pad_add_fusion.refs_0_, f32[3,32,1024]{2,1,0:T(8,128)S(1)} %collective-permute-done.13.refs_1_, f32[3,16,1024]{2,1,0:T(8,128)S(1)} %get-tuple-element.28.refs_2_, f32[3,16,1024]{2,1,0:T(8,128)S(1)} %get-tuple-element.25.refs_3_, ...), custom_call_target="tpu_custom_call" | custom-call | tf_op jit(solution)/shard_map/pallas_call | solution.py:291
  (13 shorter events, 0.4 us)
Async XLA Ops:
  0.0 2.9 %copy-start.1 = (f32[2,2,32,1024]{3,2,1,0:T(8,128)S(1)}, f32[2,2,32,1024]{3,2,1,0:T(8,128)}, u32[]{:S(2)}) copy-start(f32[2,2,32,1024]{3,2,1,0:T(8,128)} %param.11) | copy-start | bytes 1572868
  1.2 1.7 copy-start.3
  1.2 1.7 copy-start.4
  1.3 12.1 %collective-permute-start = (f32[3,32,1024]{2,1,0:T(8,128)S(1)}, f32[3,32,1024]{2,1,0:T(8,128)}, u32[]{:S(2)}, u32[]{:S(2)}) collective-permute-start(f32[3,32,1024]{2,1,0:T(8,128)S(1)} %get-tuple-element.22.refs_10_), channel_id=1, source_target_pairs={{0,32},{32,64},{64,96},{96,0},{1,33},{33,65},{65,97},{97,1},{2,34}... | collective-permute-start | bytes 1179656 | tf_op jit(solution)/shard_map/ppermute | solution.py:319
  3.0 0.9 copy-start
  3.9 9.5 %copy-start.2 = (f32[3,32,1024]{2,1,0:T(8,128)S(1)}, f32[3,32,1024]{2,1,0:T(8,128)}, u32[]{:S(2)}) copy-start(f32[3,32,1024]{2,1,0:T(8,128)} %param.6) | copy-start | bytes 1179652
  4.0 16.6 %collective-permute-start.4 = (f32[7,32,1024]{2,1,0:T(8,128)S(1)}, f32[7,32,1024]{2,1,0:T(8,128)}, u32[]{:S(2)}, u32[]{:S(2)}) collective-permute-start(f32[7,32,1024]{2,1,0:T(8,128)S(1)} %pad_maximum_fusion), channel_id=1, source_target_pairs={{0,31},{1,0},{2,1},{3,2},{4,3},{5,4},{6,5},{7,6},{8,7},{9,8},{10,9... | collective-permute-start | bytes 2752520 | tf_op jit(solution)/shard_map/ppermute | solution.py:309
  9.7 16.5 %collective-permute-start.3 = (f32[7,32,1024]{2,1,0:T(8,128)S(1)}, f32[7,32,1024]{2,1,0:T(8,128)}, u32[]{:S(2)}, u32[]{:S(2)}) collective-permute-start(f32[7,32,1024]{2,1,0:T(8,128)S(1)} %pad_maximum_fusion), channel_id=1, source_target_pairs={{0,1},{1,2},{2,3},{3,4},{4,5},{5,6},{6,7},{7,8},{8,9},{9,10},{10,1... | collective-permute-start | bytes 2752520 | tf_op jit(solution)/shard_map/ppermute | solution.py:309
  14.3 40.1 %collective-permute-start.1 = (f32[5,32,1024]{2,1,0:T(8,128)}, f32[5,32,1024]{2,1,0:T(8,128)}, u32[]{:S(2)}, u32[]{:S(2)}) collective-permute-start(f32[5,32,1024]{2,1,0:T(8,128)} %pad_maximum_fusion.1), channel_id=1, source_target_pairs={{0,1},{1,2},{2,3},{3,4},{4,5},{5,6},{6,7},{7,8},{8,9},{9,10},{10,1... | collective-permute-start | bytes 1966088 | tf_op jit(solution)/shard_map/ppermute | solution.py:309
  14.3 42.3 %collective-permute-start.2 = (f32[5,32,1024]{2,1,0:T(8,128)}, f32[5,32,1024]{2,1,0:T(8,128)}, u32[]{:S(2)}, u32[]{:S(2)}) collective-permute-start(f32[5,32,1024]{2,1,0:T(8,128)} %pad_maximum_fusion.1), channel_id=1, source_target_pairs={{0,31},{1,0},{2,1},{3,2},{4,3},{5,4},{6,5},{7,6},{8,7},{9,8},{10,9... | collective-permute-start | bytes 1966088 | tf_op jit(solution)/shard_map/ppermute | solution.py:309
  19.6 64.9 %collective-permute-start.11 = (f32[2,8,1024]{2,1,0:T(8,128)S(1)}, f32[2,8,1024]{2,1,0:T(8,128)S(1)}, u32[]{:S(2)}, u32[]{:S(2)}) collective-permute-start(f32[2,8,1024]{2,1,0:T(8,128)S(1)} %get-tuple-element.40), channel_id=1, source_target_pairs={{0,2},{1,3},{2,4},{3,5},{4,6},{5,7},{6,8},{7,9},{8,10},{9,11},{10,... | collective-permute-start | bytes 196616 | tf_op jit(solution)/shard_map/ppermute | solution.py:312
  20.6 67.3 %collective-permute-start.12 = (f32[2,8,1024]{2,1,0:T(8,128)S(1)}, f32[2,8,1024]{2,1,0:T(8,128)S(1)}, u32[]{:S(2)}, u32[]{:S(2)}) collective-permute-start(f32[2,8,1024]{2,1,0:T(8,128)S(1)} %get-tuple-element.39), channel_id=1, source_target_pairs={{0,30},{1,31},{2,0},{3,1},{4,2},{5,3},{6,4},{7,5},{8,6},{9,7},{10,... | collective-permute-start | bytes 196616 | tf_op jit(solution)/shard_map/ppermute | solution.py:313
  53.5 47.1 %collective-permute-start.10 = (f32[3,32,1024]{2,1,0:T(8,128)S(1)}, f32[3,32,1024]{2,1,0:T(8,128)S(1)}, u32[]{:S(2)}, u32[]{:S(2)}) collective-permute-start(f32[3,32,1024]{2,1,0:T(8,128)S(1)} %get-tuple-element.12.refs_6_), channel_id=1, source_target_pairs={{0,31},{1,0},{2,1},{3,2},{4,3},{5,4},{6,5},{7,6},{8,7},{9,8},{10,9... | collective-permute-start | bytes 1179656 | tf_op jit(solution)/shard_map/ppermute | solution.py:309
  54.4 46.2 %collective-permute-start.9 = (f32[3,32,1024]{2,1,0:T(8,128)S(1)}, f32[3,32,1024]{2,1,0:T(8,128)S(1)}, u32[]{:S(2)}, u32[]{:S(2)}) collective-permute-start(f32[3,32,1024]{2,1,0:T(8,128)S(1)} %get-tuple-element.12.refs_6_), channel_id=1, source_target_pairs={{0,1},{1,2},{2,3},{3,4},{4,5},{5,6},{6,7},{7,8},{8,9},{9,10},{10,1... | collective-permute-start | bytes 1179656 | tf_op jit(solution)/shard_map/ppermute | solution.py:309
  82.7 17.8 %collective-permute-start.5 = (f32[3,32,1024]{2,1,0:T(8,128)S(1)}, f32[3,32,1024]{2,1,0:T(8,128)S(1)}, u32[]{:S(2)}, u32[]{:S(2)}) collective-permute-start(f32[3,32,1024]{2,1,0:T(8,128)S(1)} %get-tuple-element.11.refs_1_), channel_id=1, source_target_pairs={{0,1},{1,2},{2,3},{3,4},{4,5},{5,6},{6,7},{7,8},{8,9},{9,10},{10,1... | collective-permute-start | bytes 1179656 | tf_op jit(solution)/shard_map/ppermute | solution.py:309
  84.5 16.1 %collective-permute-start.6 = (f32[3,32,1024]{2,1,0:T(8,128)S(1)}, f32[3,32,1024]{2,1,0:T(8,128)S(1)}, u32[]{:S(2)}, u32[]{:S(2)}) collective-permute-start(f32[3,32,1024]{2,1,0:T(8,128)S(1)} %get-tuple-element.11.refs_1_), channel_id=1, source_target_pairs={{0,31},{1,0},{2,1},{3,2},{4,3},{5,4},{6,5},{7,6},{8,7},{9,8},{10,9... | collective-permute-start | bytes 1179656 | tf_op jit(solution)/shard_map/ppermute | solution.py:309
  87.9 8.0 %collective-permute-start.7 = (f32[3,8,1024]{2,1,0:T(8,128)S(1)}, f32[3,8,1024]{2,1,0:T(8,128)S(1)}, u32[]{:S(2)}, u32[]{:S(2)}) collective-permute-start(f32[3,8,1024]{2,1,0:T(8,128)S(1)} %get-tuple-element.38), channel_id=1, source_target_pairs={{0,2},{1,3},{2,4},{3,5},{4,6},{5,7},{6,8},{7,9},{8,10},{9,11},{10,... | collective-permute-start | bytes 294920 | tf_op jit(solution)/shard_map/ppermute | solution.py:312
  95.9 4.6 %collective-permute-start.8 = (f32[3,8,1024]{2,1,0:T(8,128)S(1)}, f32[3,8,1024]{2,1,0:T(8,128)S(1)}, u32[]{:S(2)}, u32[]{:S(2)}) collective-permute-start(f32[3,8,1024]{2,1,0:T(8,128)S(1)} %get-tuple-element.37), channel_id=1, source_target_pairs={{0,30},{1,31},{2,0},{3,1},{4,2},{5,3},{6,4},{7,5},{8,6},{9,7},{10,... | collective-permute-start | bytes 294920 | tf_op jit(solution)/shard_map/ppermute | solution.py:313
  148.8 9.4 %collective-permute-start.13 = (f32[3,32,1024]{2,1,0:T(8,128)S(1)}, f32[3,32,1024]{2,1,0:T(8,128)S(1)}, u32[]{:S(2)}, u32[]{:S(2)}) collective-permute-start(f32[3,32,1024]{2,1,0:T(8,128)S(1)} %get-tuple-element.13), channel_id=1, source_target_pairs={{0,32},{32,64},{64,96},{96,0},{1,33},{33,65},{65,97},{97,1},{2,34}... | collective-permute-start | bytes 1179656 | tf_op jit(solution)/shard_map/ppermute | solution.py:334
  150.4 9.3 %collective-permute-start.14 = (f32[3,32,1024]{2,1,0:T(8,128)S(1)}, f32[3,32,1024]{2,1,0:T(8,128)S(1)}, u32[]{:S(2)}, u32[]{:S(2)}) collective-permute-start(f32[3,32,1024]{2,1,0:T(8,128)S(1)} %get-tuple-element.13), channel_id=1, source_target_pairs={{0,96},{32,0},{64,32},{96,64},{1,97},{33,1},{65,33},{97,65},{2,98}... | collective-permute-start | bytes 1179656 | tf_op jit(solution)/shard_map/ppermute | solution.py:335
  158.3 6.9 %collective-permute-start.17 = (f32[3,16,1024]{2,1,0:T(8,128)S(1)}, f32[3,16,1024]{2,1,0:T(8,128)S(1)}, u32[]{:S(2)}, u32[]{:S(2)}) collective-permute-start(f32[3,16,1024]{2,1,0:T(8,128)S(1)} %get-tuple-element.32), channel_id=1, source_target_pairs={{0,32},{32,64},{64,96},{96,0},{1,33},{33,65},{65,97},{97,1},{2,34}... | collective-permute-start | bytes 589832 | tf_op jit(solution)/shard_map/ppermute | solution.py:338
  159.7 5.7 %collective-permute-start.15 = (f32[3,16,1024]{2,1,0:T(8,128)S(1)}, f32[3,16,1024]{2,1,0:T(8,128)S(1)}, u32[]{:S(2)}, u32[]{:S(2)}) collective-permute-start(f32[3,16,1024]{2,1,0:T(8,128)S(1)} %get-tuple-element.36), channel_id=1, source_target_pairs={{0,96},{32,0},{64,32},{96,64},{1,97},{33,1},{65,33},{97,65},{2,98}... | collective-permute-start | bytes 589832 | tf_op jit(solution)/shard_map/ppermute | solution.py:338
  165.3 7.5 %collective-permute-start.18 = (f32[3,3,16,1024]{3,2,1,0:T(8,128)S(1)}, f32[3,3,16,1024]{3,2,1,0:T(8,128)S(1)}, u32[]{:S(2)}, u32[]{:S(2)}) collective-permute-start(f32[3,3,16,1024]{3,2,1,0:T(8,128)S(1)} %pad_maximum_fusion.3), channel_id=1, source_target_pairs={{0,31},{1,0},{2,1},{3,2},{4,3},{5,4},{6,5},{7,6},{8,7},{9,8},{10,9... | collective-permute-start | bytes 1769480 | tf_op jit(solution)/shard_map/ppermute | solution.py:343
  165.5 12.7 %collective-permute-start.16 = (f32[3,3,16,1024]{3,2,1,0:T(8,128)S(1)}, f32[3,3,16,1024]{3,2,1,0:T(8,128)S(1)}, u32[]{:S(2)}, u32[]{:S(2)}) collective-permute-start(f32[3,3,16,1024]{3,2,1,0:T(8,128)S(1)} %pad_maximum_fusion.2), channel_id=1, source_target_pairs={{0,1},{1,2},{2,3},{3,4},{4,5},{5,6},{6,7},{7,8},{8,9},{9,10},{10,1... | collective-permute-start | bytes 1769480 | tf_op jit(solution)/shard_map/ppermute | solution.py:341

commit v2 on v0

v2 whole, which is shorter than its diff:
```python
import functools

import jax
import jax.numpy as jnp
from jax import lax
from jax.experimental import pallas as pl
from jax.experimental.pallas import tpu as pltpu
from jax.sharding import PartitionSpec as P

FACTOR = 16
H = 0.05
C = 0.5 * H
LANES = 128


def ring(n, shift):
    return [(i, (i + shift) % n) for i in range(n)]


def at(r, rows=8):
    return pl.ds(r, rows)


def diff_cols(chunks):
    lane = lax.broadcasted_iota(jnp.int32, (8, LANES), 1)
    first, last = lane == 0, lane == LANES - 1
    left = [pltpu.roll(f, 1, 1) for f in chunks]
    right = [pltpu.roll(f, LANES - 1, 1) for f in chunks]
    out = []
    for c in range(len(chunks)):
        lo = jnp.where(first, left[c - 1] if c > 0 else 0.0, left[c])
        hi = jnp.where(last, right[c + 1] if c + 1 < len(chunks) else 0.0, right[c])
        out.append(hi - lo)
    return out


def copy_in(dst, base, src, lead, start, rows, scale=None):
    for g in range(0, rows, 8):
        for c in range(dst.shape[0]):
            val = src[lead + (at(start + g), pl.ds(c * LANES, LANES))]
            dst[c, at(base + g), :] = val if scale is None else val * scale


def each(fields, base, rows, f):
    def group(g, _):
        for c in range(fields[0].shape[0]):
            f((c, at(base + g * 8), slice(None)))
        return 0

    lax.fori_loop(0, rows // 8, group, 0)


def flux_rows(FY, V, D, base, rows):
    def put(s):
        FY[s] = D[s] * V[s]

    each((FY,), base, rows, put)


def level_pass(E, U, FY, D, r):
    cs = range(E.shape[0])
    dx = diff_cols([D[c, at(r), :] * U[c, at(r), :] for c in cs])
    for c in cs:
        E[c, at(r), :] = E[c, at(r), :] - (dx[c] + (FY[c, at(r + 1), :] - FY[c, at(r - 1), :]))


def velocity_pass(E, U, V, FY, D, A, W, r, gain=None):
    cs = range(E.shape[0])
    dx = diff_cols([E[c, at(r), :] for c in cs])
    for c in cs:
        s = (c, at(r), slice(None))
        dy = E[c, at(r + 1), :] - E[c, at(r - 1), :]
        gx = dx[c]
        if gain is not None:
            gx, dy = gx * gain, dy * gain
        u = A[s] * (U[s] - gx)
        v = A[s] * (V[s] - dy)
        if W is not None:
            u, v = u + W[0][s], v + W[1][s]
        U[s] = u
        V[s] = v
        FY[s] = D[s] * v


def keep_rim(E, base, n, keep):
    for r, k in ((base - 1, keep[0]), (base + n, keep[1])):
        for c in range(E.shape[0]):
            E[c, at(r, 1), :] = E[c, at(r, 1), :] * k


def sweep(E, U, V, FY, D, A, W, base, n, keep, wide):
    for phase in range(FACTOR // 4):
        reach = 2 * FACTOR - 8 * phase
        lo, groups = base - reach, (n + 2 * reach) // 8

        def step(_, carry, lo=lo, groups=groups):
            for g in range(groups + wide):
                level_pass(E, U, FY, D, lo - wide + g * 8)
            keep_rim(E, base, n, keep)
            for g in range(groups):
                velocity_pass(E, U, V, FY, D, A, W, lo + g * 8)
            return carry

        lax.fori_loop(0, 4, step, 0)


def coarse_coefs(D, A, base, rows):
    def put(s):
        D[s] = D[s] * float(FACTOR)
        A[s] = A[s] / (float(FACTOR) - (FACTOR - 1.0) * A[s])

    each((D, A), base, rows, put)


def coarse_step(E, U, V, FY, D, A, lo, rows, base, n, keep):
    for r in range(lo - 1, lo + rows + 1, 8):
        level_pass(E, U, FY, D, r)
    keep_rim(E, base, n, keep)
    for r in range(lo, lo + rows, 8):
        velocity_pass(E, U, V, FY, D, A, None, r, float(FACTOR))


def rim_flags(space):
    size = lax.axis_size("space")
    return tuple(jnp.where(x, 1.0, 0.0) for x in (space > 0, space < size - 1, space > 1, space < size - 2))


def read_own(src, base, g, c):
    return src[c, at(base + g), :]


def fine_kernel(k, pack, n, space_ref, own, up, dn, wind, wup, wdn, coef, cup, cdn, guess, first, delta, E, U, V, FY, D, A, W0, W1):
    in_up, in_dn, _, _ = rim_flags(space_ref[0])
    lead, ws, cs = pack
    base = 40
    parts = ((base - n, up, wup, cup, in_up, (), ws, cs), (base, own, wind, coef, 1.0, lead, None, 0), (base + n, dn, wdn, cdn, in_dn, (), ws, cs))
    for row, st, wd, cf, inside, ld, w, c in parts:
        copy_in(D, row, cf, (c,), 0, n, inside * (C * C))
        copy_in(A, row, cf, (c + 1,), 0, n, inside)
        copy_in(E, row, st, ld + (0,), 0, n, C)
        copy_in(U, row, st, ld + (1,), 0, n)
        copy_in(V, row, st, ld + (2,), 0, n)
        for f, dst in enumerate((W0, W1)):
            copy_in(dst, row, wd, (k, f) if w is None else (w + f,), 0, n, H)

    def prepare(s):
        W0[s] = W0[s] * A[s]
        W1[s] = W1[s] * A[s]
        FY[s] = D[s] * V[s]

    each((E,), base - n, 3 * n, prepare)
    sweep(E, U, V, FY, D, A, (W0, W1), base, n, (in_up, in_dn), 0)
    for f, src in enumerate((E, U, V)):
        for g in range(0, n, 8):
            for c in range(E.shape[0]):
                to = (f, at(g), pl.ds(c * LANES, LANES))
                val = read_own(src, base, g, c)
                if f == 0:
                    val = val * (1.0 / C)
                first[to] = val
                delta[to] = val - guess[(k,) + to]


def relax_b_kernel(n, space_ref, d, up, dn, coef, cup, cdn, res, E, U, V, FY, D, A):
    in_up, in_dn, _, _ = rim_flags(space_ref[0])
    base = 40
    for row, st, cf, inside, c in ((base - n, up, cup, in_up, 5), (base, d, coef, 1.0, 0), (base + n, dn, cdn, in_dn, 5)):
        copy_in(D, row, cf, (c,), 0, n, inside * (C * C))
        copy_in(A, row, cf, (c + 1,), 0, n, inside)
        copy_in(E, row, st, (0,), 0, n, C)
        copy_in(U, row, st, (1,), 0, n)
        copy_in(V, row, st, (2,), 0, n)
    flux_rows(FY, V, D, base - n, 3 * n)
    sweep(E, U, V, FY, D, A, None, base, n, (in_up, in_dn), 0)
    for f, src in enumerate((E, U, V)):
        for g in range(0, n, 8):
            for c in range(E.shape[0]):
                res[f, at(g), pl.ds(c * LANES, LANES)] = read_own(src, base, g, c)


def relax_a_kernel(n, space_ref, d, up, dn, uup, ddn, coef, cup, cdn, cuu, cdd, more, res, total, E, U, V, FY, D, A):
    in_up, in_dn, in_uu, in_dd = rim_flags(space_ref[0])
    base = 48
    for row, rows, st, cf, inside, c in (
        (base - n - 8, 8, uup, cuu, in_uu, 0),
        (base - n, n, up, cup, in_up, 5),
        (base, n, d, coef, 1.0, 0),
        (base + n, n, dn, cdn, in_dn, 5),
        (base + 2 * n, 8, ddn, cdd, in_dd, 0),
    ):
        copy_in(D, row, cf, (c,), 0, rows, inside * (C * C))
        copy_in(A, row, cf, (c + 1,), 0, rows, inside)
        copy_in(E, row, st, (0,), 0, rows, C)
        copy_in(U, row, st, (1,), 0, rows)
        copy_in(V, row, st, (2,), 0, rows)
    flux_rows(FY, V, D, base - n - 8, 3 * n + 16)
    sweep(E, U, V, FY, D, A, None, base, n, (in_up, in_dn), 1)
    for f, src in enumerate((E, U, V)):
        for g in range(0, n, 8):
            for c in range(E.shape[0]):
                res[f, at(g), pl.ds(c * LANES, LANES)] = read_own(src, base, g, c)
    coarse_coefs(D, A, base - 8, n + 16)
    flux_rows(FY, V, D, base - 8, n + 16)
    coarse_step(E, U, V, FY, D, A, base, n, base, n, (in_up, in_dn))
    for f, src in enumerate((E, U, V)):
        for g in range(0, n, 8):
            for c in range(E.shape[0]):
                to = (f, at(g), pl.ds(c * LANES, LANES))
                total[to] = read_own(src, base, g, c) + more[to]


HALO = 16


def chain_kernel(n, pos_ref, ca, cb, cc, rup, rdn, coef, cup, cdn, r1, fa, fb, out, E, U, V, FY, D, A, X, Y, Z):
    tm, space = pos_ref[0], pos_ref[1]
    base = HALO + 8
    in_up, in_dn, _, _ = rim_flags(space)
    keep = (in_up, in_dn)
    for row, cf, c, start, rows, inside in (
        (base - HALO, cup, 5, n - HALO, HALO, in_up),
        (base, coef, 0, 0, n, 1.0),
        (base + n, cdn, 5, 0, HALO, in_dn),
    ):
        copy_in(D, row, cf, (c,), start, rows, inside * (C * C))
        copy_in(A, row, cf, (c + 1,), start, rows, inside)
    coarse_coefs(D, A, base - HALO, n + 2 * HALO)

    def take(fields, k, own, use):
        for f, dst in enumerate(fields):
            copy_in(dst, base - HALO, rup, (k, f), 0, HALO, use)
            copy_in(dst, base, own, (f,), 0, n, use)
            copy_in(dst, base + n, rdn, (k, f), 0, HALO, use)

    def add(lo, rows):
        def put(s):
            E[s] = E[s] + X[s]
            U[s] = U[s] + Y[s]
            V[s] = V[s] + Z[s]
            FY[s] = D[s] * V[s]

        each((E,), lo, rows, put)

    def coarse(reach):
        coarse_step(E, U, V, FY, D, A, base - reach, n + 2 * reach, base, n, keep)

    take((E, U, V), 2, cc, jnp.where(tm >= 3, 1.0, 0.0))
    flux_rows(FY, V, D, base - HALO, n + 2 * HALO)
    coarse(8)
    coarse(6)
    take((X, Y, Z), 1, cb, jnp.where(tm >= 2, 1.0, 0.0))
    add(base - 8, n + 16)
    coarse(4)
    coarse(2)
    take((X, Y, Z), 0, ca, jnp.where(tm >= 1, 1.0, 0.0))
    add(base - 8, n + 16)

    def write(k, first, more):
        for f, src in enumerate((E, U, V)):
            for g in range(0, n, 8):
                for c in range(E.shape[0]):
                    to = (f, at(g), pl.ds(c * LANES, LANES))
                    val = read_own(src, base, g, c)
                    if more is not None:
                        val = val + more[to]
                    if f == 0:
                        val = val * (1.0 / C)
                    out[(k,) + to] = first[to] + val

    write(0, fa, None)
    coarse(0)
    write(1, fb, r1)


def call(kernel, n, ncols, rows, fields, outs, *args):
    scratch = [pltpu.VMEM((ncols // LANES, rows, LANES), jnp.float32)] * fields
    vmem = pl.BlockSpec(memory_space=pltpu.VMEM)
    return pl.pallas_call(
        lambda *refs: kernel(n, *refs),
        out_shape=outs,
        in_specs=[pl.BlockSpec(memory_space=pltpu.SMEM)] + [vmem] * (len(args) - 1),
        out_specs=jax.tree.map(lambda _: vmem, outs),
        scratch_shapes=scratch,
        compiler_params=pltpu.CompilerParams(vmem_limit_bytes=32 * 2**20),
    )(*args)


def shards(initial, guess, depth, friction, mask, wind):
    n, ncols = depth.shape
    spaces, times = lax.axis_size("space"), lax.axis_size("tm")
    tm, space = lax.axis_index("tm"), lax.axis_index("space")
    pos = jnp.stack([tm, space]).astype(jnp.int32)
    where = space.astype(jnp.int32)[None]

    def sides(x, hop=1):
        return lax.ppermute(x, "space", ring(spaces, hop)), lax.ppermute(x, "space", ring(spaces, -hop))

    def ends(x, rows, hop=1):
        up = lax.ppermute(x[..., n - rows :, :], "space", ring(spaces, hop))
        dn = lax.ppermute(x[..., :rows, :], "space", ring(spaces, -hop))
        return up, dn

    state = jax.ShapeDtypeStruct((3, n, ncols), jnp.float32)
    coef = jnp.stack([depth, mask.astype(jnp.float32) / (1.0 + H * friction)])

    earlier = lax.ppermute(guess[1], "tm", ring(times, 1))
    bu, bd = sides(jnp.concatenate([guess[0], wind[1], coef]))
    entry = jnp.where(tm == 0, initial, earlier)
    au, ad = sides(jnp.concatenate([entry, wind[0]]))
    cuu, cdd = ends(coef, 8, 2)

    fine_b = functools.partial(fine_kernel, 1, ((0,), 3, 5))
    fb, db = call(fine_b, n, ncols, 120, 8, (state, state), where, guess, bu, bd, wind, bu, bd, coef, bu, bd, guess)
    dbu, dbd = sides(db)
    fine_a = functools.partial(fine_kernel, 0, ((), 3, 5))
    fa, da = call(fine_a, n, ncols, 120, 8, (state, state), where, entry, au, ad, wind, au, ad, coef, bu, bd, guess)
    dau, dad = sides(da)
    dauu, dadd = ends(da, 8, 2)
    rb = call(relax_b_kernel, n, ncols, 120, 6, state, where, db, dbu, dbd, coef, bu, bd)
    ra, c1 = call(relax_a_kernel, n, ncols, 144, 6, (state, state), where, da, dau, dad, dauu, dadd, coef, bu, bd, cuu, cdd, rb)

    ca = lax.ppermute(c1, "tm", ring(times, 1))
    cc = lax.ppermute(c1, "tm", ring(times, -1))
    half = n // 2
    cb = jnp.concatenate(
        [lax.ppermute(ca[:, :half], "tm", ring(times, 1)), lax.ppermute(cc[:, half:], "tm", ring(times, -1))], axis=1
    )
    rup, rdn = ends(jnp.stack([ca, cb, cc]), HALO)
    out = jax.ShapeDtypeStruct(guess.shape, jnp.float32)
    return call(chain_kernel, n, ncols, 88, 9, out, pos, ca, cb, cc, rup, rdn, coef, bu, bd, ra, fa, fb)


def solution(mesh):
    return jax.shard_map(
        shards,
        mesh=mesh,
        in_specs=(
            P(None, "space", None),
            P("tm", None, "space", None),
            P("space", None),
            P("space", None),
            P("space", None),
            P("tm", None, "space", None),
        ),
        out_specs=P("tm", None, "space", None),
        check_vma=False,
    )
```

time: 895 us -> 113 us (0.13)
  the two profiles are of different devices: /device:TPU:34 before, /device:TPU:0 now
where the time goes in v2:
time: 113 us
  waiting for transfers between devices  40.3 us (36%)
  Pallas kernels  33.8 us (30%)
  starting transfers between devices  32.1 us (28%)
  other arithmetic  4.21 us (4%)
  local copies, waits for them, and re-layouts  2.21 us (2%)
    pallas_call x5, Pallas kernels, call(): pl.pallas_call(lambda *refs: kernel(n, *refs), out_shape=outs, in_specs=[...  33.8 us
    ppermute x4, starting transfers between devices, sides(): lax.ppermute(x, 'space', ring(spaces, -hop))  15.7 us
    ppermute x3, waiting for transfers between devices, ends(): dn = lax.ppermute(x[..., :rows, :], 'space', ring(spaces, -hop))  13 us
    ppermute x1, waiting for transfers between devices, shards(): ca = lax.ppermute(c1, 'tm', ring(times, 1))  8.12 us
    ppermute x3, waiting for transfers between devices, ends(): up = lax.ppermute(x[..., n - rows:, :], 'space', ring(spaces, hop))  7.44 us
    ppermute x3, starting transfers between devices, ends(): dn = lax.ppermute(x[..., :rows, :], 'space', ring(spaces, -hop))  7.37 us
    ppermute x4, waiting for transfers between devices, sides(): lax.ppermute(x, 'space', ring(spaces, hop))  5.13 us
    ppermute x1, waiting for transfers between devices, shards(): lax.ppermute(ca[:, :half], 'tm', ring(times, 1))  3.55 us
  transfers between devices with their start and end apart: 19, of which 9 were waited for; matrix products, arithmetic and copies ran while one was open for 4% of the time, Pallas kernels for 20%

profile of v2, /device:TPU:0, one launch (start us, length us, event | category | flops | bytes accessed | tf_op | source)
XLA Modules:
  0.0 112.9 jit_solution(950964640667092519)
XLA Ops:
  0.0 1.3 %slice_bitcast_fusion = (f32[3,32,1024]{2,1,0:T(8,128)S(1)}, f32[3,32,1024]{2,1,0:T(8,128)S(1)}) fusion(f32[2,3,32,1024]{3,2,1,0:T(8,128)} %refs_10_.3), kind=kLoop, calls=%fused_computation.3 | loop fusion | bytes 1572864 | tf_op jit(solution)/shard_map/squeeze | solution.py:307
  1.3 1.7 %collective-permute-start = (f32[3,32,1024]{2,1,0:T(8,128)S(1)}, f32[3,32,1024]{2,1,0:T(8,128)S(1)}, u32[]{:S(2)}, u32[]{:S(2)}) collective-permute-start(f32[3,32,1024]{2,1,0:T(8,128)S(1)} %get-tuple-element.20), channel_id=1, source_target_pairs={{0,32},{32,64},{64,96},{96,0},{1,33},{33,65},{65,97},{97,1},{2,34}... | collective-permute-start | bytes 1179656 | tf_op jit(solution)/shard_map/ppermute | solution.py:306
  2.9 0.0 copy-done.8
  2.9 0.0 copy-done.7
  3.0 0.0 copy-done.1
  3.0 0.0 copy-start.2
  3.0 0.7 slice_bitcast_fusion.2
  3.7 0.0 copy-done.2
  3.7 0.0 copy-done.4
  3.7 1.0 pad_maximum_fusion.1
  4.8 5.6 %collective-permute-start.4 = (f32[7,32,1024]{2,1,0:T(8,128)}, f32[7,32,1024]{2,1,0:T(8,128)S(1)}, u32[]{:S(2)}, u32[]{:S(2)}) collective-permute-start(f32[7,32,1024]{2,1,0:T(8,128)} %pad_maximum_fusion.1), channel_id=1, source_target_pairs={{0,31},{1,0},{2,1},{3,2},{4,3},{5,4},{6,5},{7,6},{8,7},{9,8},{10,9... | collective-permute-start | bytes 2752520 | tf_op jit(solution)/shard_map/ppermute | solution.py:296
  10.4 0.0 collective-permute-start.3
  10.4 2.9 %collective-permute-done = f32[3,32,1024]{2,1,0:T(8,128)S(1)} collective-permute-done((f32[3,32,1024]{2,1,0:T(8,128)S(1)}, f32[3,32,1024]{2,1,0:T(8,128)S(1)}, u32[]{:S(2)}, u32[]{:S(2)}) %collective-permute-start) | collective-permute-done | bytes 393248 | tf_op jit(solution)/shard_map/ppermute | solution.py:306
  13.3 0.0 copy-done.6
  13.4 0.0 copy-start
  13.4 1.9 %pad_maximum_fusion.2 = f32[5,32,1024]{2,1,0:T(8,128)} fusion(f32[2,32,1024]{2,1,0:T(8,128)} %get-tuple-element.22, f32[3,32,1024]{2,1,0:T(8,128)S(1)} %broadcast_select_fusion.refs_1_), kind=kLoop, calls=%fused_computation.2 | loop fusion | flops 163840 | bytes 1310720 | tf_op jit(solution)/shard_map/concatenate | solution.py:309
  15.3 5.2 %collective-permute-start.2 = (f32[5,32,1024]{2,1,0:T(8,128)}, f32[5,32,1024]{2,1,0:T(8,128)}, u32[]{:S(2)}, u32[]{:S(2)}) collective-permute-start(f32[5,32,1024]{2,1,0:T(8,128)} %pad_maximum_fusion.2), channel_id=1, source_target_pairs={{0,31},{1,0},{2,1},{3,2},{4,3},{5,4},{6,5},{7,6},{8,7},{9,8},{10,9... | collective-permute-start | bytes 1966088 | tf_op jit(solution)/shard_map/ppermute | solution.py:296
  20.5 0.0 collective-permute-start.1
  20.5 1.0 pad_maximum_fusion.3.refs_7_.refs_4_.refs_6_
  21.5 0.1 collective-permute-done.4.refs_9_.refs_3_.refs_6_.refs_8_
  21.6 5.1 %collective-permute-done.3.refs_8_.refs_2_.refs_5_.refs_7_ = f32[7,32,1024]{2,1,0:T(8,128)S(1)} collective-permute-done((f32[7,32,1024]{2,1,0:T(8,128)}, f32[7,32,1024]{2,1,0:T(8,128)S(1)}, u32[]{:S(2)}, u32[]{:S(2)}) %collective-permute-start.3) | collective-permute-done | bytes 917536 | tf_op jit(solution)/shard_map/ppermute | solution.py:296
  26.8 0.0 copy-done
  26.8 7.1 %shard_map.65 = (f32[3,32,1024]{2,1,0:T(8,128)S(1)}, f32[3,32,1024]{2,1,0:T(8,128)S(1)}) custom-call(s32[1]{0:T(128)} %bitcast.1.refs_0_, f32[2,3,32,1024]{3,2,1,0:T(8,128)S(1)} %copy-done, f32[7,32,1024]{2,1,0:T(8,128)S(1)} %collective-permute-done.3.refs_8_.refs_2_.refs_5_.refs_7_, ...), custom_call_target="tpu_custom_call" | custom-call | tf_op jit(solution)/shard_map/pallas_call | solution.py:278
  33.9 0.0 copy-start.3
  33.9 0.0 copy-start.5
  33.9 0.1 collective-permute-start.12
  34.0 0.5 collective-permute-start.11
  34.5 0.0 collective-permute-done.2.refs_3_.refs_6_
  34.5 0.0 collective-permute-done.1.refs_2_.refs_5_
  34.5 8.8 %shard_map.64 = (f32[3,32,1024]{2,1,0:T(8,128)S(1)}, f32[3,32,1024]{2,1,0:T(8,128)S(1)}) custom-call(s32[1]{0:T(128)} %bitcast.1.refs_0_, f32[3,32,1024]{2,1,0:T(8,128)S(1)} %broadcast_select_fusion.refs_1_, f32[5,32,1024]{2,1,0:T(8,128)} %collective-permute-done.1.refs_2_.refs_5_, f32[5,32,1024]{2,1,0:T(8,128)} %collective-permute-done.2.refs_3_.refs_6_, ...), custom_call_target="tpu_custom_call" | custom-call | tf_op jit(solution)/shard_map/pallas_call | solution.py:278
  43.4 4.7 %collective-permute-start.6 = (f32[3,32,1024]{2,1,0:T(8,128)S(1)}, f32[3,32,1024]{2,1,0:T(8,128)S(1)}, u32[]{:S(2)}, u32[]{:S(2)}) collective-permute-start(f32[3,32,1024]{2,1,0:T(8,128)S(1)} %get-tuple-element.11.refs_1_), channel_id=1, source_target_pairs={{0,31},{1,0},{2,1},{3,2},{4,3},{5,4},{6,5},{7,6},{8,7},{9,8},{10,9... | collective-permute-start | bytes 1179656 | tf_op jit(solution)/shard_map/ppermute | solution.py:296
  48.1 0.0 collective-permute-start.5
  48.1 0.0 copy-done.3
  48.1 0.0 copy-done.5
  48.1 0.5 collective-permute-start.10
  48.7 5.7 %collective-permute-done.10.refs_10_ = f32[2,8,1024]{2,1,0:T(8,128)S(1)} collective-permute-done((f32[2,8,1024]{2,1,0:T(8,128)S(1)}, f32[2,8,1024]{2,1,0:T(8,128)S(1)}, u32[]{:S(2)}, u32[]{:S(2)}) %collective-permute-start.10) | collective-permute-done | bytes 65568 | tf_op jit(solution)/shard_map/ppermute | solution.py:300
  54.3 5.8 %collective-permute-start.8 = (f32[3,8,1024]{2,1,0:T(8,128)S(1)}, f32[3,8,1024]{2,1,0:T(8,128)S(1)}, u32[]{:S(2)}, u32[]{:S(2)}) collective-permute-start(f32[3,8,1024]{2,1,0:T(8,128)S(1)} %get-tuple-element.23), channel_id=1, source_target_pairs={{0,30},{1,31},{2,0},{3,1},{4,2},{5,3},{6,4},{7,5},{8,6},{9,7},{10,... | collective-permute-start | bytes 294920 | tf_op jit(solution)/shard_map/ppermute | solution.py:300
  60.1 0.0 collective-permute-done.12.refs_3_
  60.1 0.0 collective-permute-start.7
  60.1 0.0 collective-permute-done.11.refs_2_
  60.2 0.3 collective-permute-start.9
  60.4 6.9 %shard_map.66.refs_11_ = f32[3,32,1024]{2,1,0:T(8,128)S(1)} custom-call(s32[1]{0:T(128)} %bitcast.1.refs_0_, f32[3,32,1024]{2,1,0:T(8,128)S(1)} %get-tuple-element.12.refs_1_, f32[3,32,1024]{2,1,0:T(8,128)S(1)} %collective-permute-done.11.refs_2_, f32[3,32,1024]{2,1,0:T(8,128)S(1)} %collective-permute-done.12.refs_3_, ...), custom_call_target="tpu_custom_call" | custom-call | tf_op jit(solution)/shard_map/pallas_call | solution.py:278
  67.3 2.2 %collective-permute-done.9.refs_9_ = f32[2,8,1024]{2,1,0:T(8,128)S(1)} collective-permute-done((f32[2,8,1024]{2,1,0:T(8,128)S(1)}, f32[2,8,1024]{2,1,0:T(8,128)S(1)}, u32[]{:S(2)}, u32[]{:S(2)}) %collective-permute-start.9) | collective-permute-done | bytes 65568 | tf_op jit(solution)/shard_map/ppermute | solution.py:299
  69.5 0.0 collective-permute-done.8.refs_5_
  69.5 0.0 collective-permute-done.7.refs_4_
  69.5 0.0 collective-permute-done.6.refs_3_
  69.6 0.0 collective-permute-done.5.refs_2_
  69.6 7.7 %shard_map.67 = (f32[3,32,1024]{2,1,0:T(8,128)S(1)}, f32[3,32,1024]{2,1,0:T(8,128)S(1)}) custom-call(s32[1]{0:T(128)} %bitcast.1.refs_0_, f32[3,32,1024]{2,1,0:T(8,128)S(1)} %get-tuple-element.11.refs_1_, f32[3,32,1024]{2,1,0:T(8,128)S(1)} %collective-permute-done.5.refs_2_, f32[3,32,1024]{2,1,0:T(8,128)S(1)} %collective-permute-done.6.refs_3_, ...), custom_call_target="tpu_custom_call" | custom-call | tf_op jit(solution)/shard_map/pallas_call | solution.py:278
  77.2 1.6 %collective-permute-start.13 = (f32[3,32,1024]{2,1,0:T(8,128)S(1)}, f32[3,32,1024]{2,1,0:T(8,128)S(1)}, u32[]{:S(2)}, u32[]{:S(2)}) collective-permute-start(f32[3,32,1024]{2,1,0:T(8,128)S(1)} %get-tuple-element.13), channel_id=1, source_target_pairs={{0,32},{32,64},{64,96},{96,0},{1,33},{33,65},{65,97},{97,1},{2,34}... | collective-permute-start | bytes 1179656 | tf_op jit(solution)/shard_map/ppermute | solution.py:322
  78.8 1.7 %collective-permute-start.15 = (f32[3,32,1024]{2,1,0:T(8,128)S(1)}, f32[3,32,1024]{2,1,0:T(8,128)S(1)}, u32[]{:S(2)}, u32[]{:S(2)}) collective-permute-start(f32[3,32,1024]{2,1,0:T(8,128)S(1)} %get-tuple-element.13), channel_id=1, source_target_pairs={{0,96},{32,0},{64,32},{96,64},{1,97},{33,1},{65,33},{97,65},{2,98}... | collective-permute-start | bytes 1179656 | tf_op jit(solution)/shard_map/ppermute | solution.py:323
  80.5 8.1 %collective-permute-done.13.refs_1_ = f32[3,32,1024]{2,1,0:T(8,128)S(1)} collective-permute-done((f32[3,32,1024]{2,1,0:T(8,128)S(1)}, f32[3,32,1024]{2,1,0:T(8,128)S(1)}, u32[]{:S(2)}, u32[]{:S(2)}) %collective-permute-start.13) | collective-permute-done | bytes 393248 | tf_op jit(solution)/shard_map/ppermute | solution.py:322
  88.7 0.3 collective-permute-start.14
  89.0 0.0 collective-permute-done.15.refs_3_
  89.0 3.0 %collective-permute-start.16 = (f32[3,16,1024]{2,1,0:T(8,128)S(1)}, f32[3,16,1024]{2,1,0:T(8,128)S(1)}, u32[]{:S(2)}, u32[]{:S(2)}) collective-permute-start(f32[3,16,1024]{2,1,0:T(8,128)S(1)} %slice.53), channel_id=1, source_target_pairs={{0,96},{32,0},{64,32},{96,64},{1,97},{33,1},{65,33},{97,65},{2,98}... | collective-permute-start | bytes 589832 | tf_op jit(solution)/shard_map/ppermute | solution.py:326
  92.1 3.6 %collective-permute-done.14 = f32[3,16,1024]{2,1,0:T(8,128)S(1)} collective-permute-done((f32[3,16,1024]{2,1,0:T(8,128)S(1)}, f32[3,16,1024]{2,1,0:T(8,128)S(1)}, u32[]{:S(2)}, u32[]{:S(2)}) %collective-permute-start.14) | collective-permute-done | bytes 196640 | tf_op jit(solution)/shard_map/ppermute | solution.py:326
  95.6 0.0 collective-permute-done.16
  95.7 0.1 pad_maximum_fusion
  95.8 0.1 fusion.2
  95.9 1.0 collective-permute-start.18
  96.9 0.0 collective-permute-start.17
  97.0 0.1 pad_add_fusion.refs_0_
  97.0 7.3 %collective-permute-done.18.refs_5_ = f32[3,3,16,1024]{3,2,1,0:T(8,128)S(1)} collective-permute-done((f32[3,3,16,1024]{3,2,1,0:T(8,128)S(1)}, f32[3,3,16,1024]{3,2,1,0:T(8,128)S(1)}, u32[]{:S(2)}, u32[]{:S(2)}) %collective-permute-start.18) | collective-permute-done | bytes 589856 | tf_op jit(solution)/shard_map/ppermute | solution.py:300
  104.4 5.2 %collective-permute-done.17.refs_4_ = f32[3,3,16,1024]{3,2,1,0:T(8,128)S(1)} collective-permute-done((f32[3,3,16,1024]{3,2,1,0:T(8,128)S(1)}, f32[3,3,16,1024]{3,2,1,0:T(8,128)S(1)}, u32[]{:S(2)}, u32[]{:S(2)}) %collective-permute-start.17) | collective-permute-done | bytes 589856 | tf_op jit(solution)/shard_map/ppermute | solution.py:299
  109.6 3.3 %shard_map.68 = f32[2,3,32,1024]{3,2,1,0:T(8,128)} custom-call(s32[2]{0:T(128)S(1)} %pad_add_fusion.refs_0_, f32[3,32,1024]{2,1,0:T(8,128)S(1)} %collective-permute-done.13.refs_1_, f32[3,32,1024]{2,1,0:T(8,128)S(1)} %constant_dynamic-update-slice_fusion.refs_2_, f32[3,32,1024]{2,1,0:T(8,128)S(1)} %collective-permute-done.15.refs_3_, ...), custom_call_target="tpu_custom_call" | custom-call | tf_op jit(solution)/shard_map/pallas_call | solution.py:278
  (13 shorter events, 0.2 us)
Async XLA Ops:
  0.0 2.9 %copy-start.8 = (s32[32,1024]{1,0:T(8,128)S(1)}, s32[32,1024]{1,0:T(8,128)}, u32[]{:S(2)}) copy-start(s32[32,1024]{1,0:T(8,128)} %param.10) | copy-start | bytes 393220
  0.0 2.9 %copy-start.7 = (f32[32,1024]{1,0:T(8,128)S(1)}, f32[32,1024]{1,0:T(8,128)}, u32[]{:S(2)}) copy-start(f32[32,1024]{1,0:T(8,128)} %param.9) | copy-start | bytes 393220
  0.0 3.0 %copy-start.1 = (f32[2,2,32,1024]{3,2,1,0:T(8,128)S(1)}, f32[2,2,32,1024]{3,2,1,0:T(8,128)}, u32[]{:S(2)}) copy-start(f32[2,2,32,1024]{3,2,1,0:T(8,128)} %refs_4_.3) | copy-start | bytes 1572868
  0.0 3.7 %copy-start.4 = (f32[32,1024]{1,0:T(8,128)S(1)}, f32[32,1024]{1,0:T(8,128)}, u32[]{:S(2)}) copy-start(f32[32,1024]{1,0:T(8,128)} %param.8) | copy-start | bytes 393220
  1.3 12.0 %collective-permute-start = (f32[3,32,1024]{2,1,0:T(8,128)S(1)}, f32[3,32,1024]{2,1,0:T(8,128)S(1)}, u32[]{:S(2)}, u32[]{:S(2)}) collective-permute-start(f32[3,32,1024]{2,1,0:T(8,128)S(1)} %get-tuple-element.20), channel_id=1, source_target_pairs={{0,32},{32,64},{64,96},{96,0},{1,33},{33,65},{65,97},{97,1},{2,34}... | collective-permute-start | bytes 1179656 | tf_op jit(solution)/shard_map/ppermute | solution.py:306
  3.0 0.7 copy-start.2
  3.7 9.6 %copy-start.6 = (f32[3,32,1024]{2,1,0:T(8,128)S(1)}, f32[3,32,1024]{2,1,0:T(8,128)}, u32[]{:S(2)}) copy-start(f32[3,32,1024]{2,1,0:T(8,128)} %param.6) | copy-start | bytes 1179652
  4.8 16.9 %collective-permute-start.4 = (f32[7,32,1024]{2,1,0:T(8,128)}, f32[7,32,1024]{2,1,0:T(8,128)S(1)}, u32[]{:S(2)}, u32[]{:S(2)}) collective-permute-start(f32[7,32,1024]{2,1,0:T(8,128)} %pad_maximum_fusion.1), channel_id=1, source_target_pairs={{0,31},{1,0},{2,1},{3,2},{4,3},{5,4},{6,5},{7,6},{8,7},{9,8},{10,9... | collective-permute-start | bytes 2752520 | tf_op jit(solution)/shard_map/ppermute | solution.py:296
  10.4 16.4 %collective-permute-start.3 = (f32[7,32,1024]{2,1,0:T(8,128)}, f32[7,32,1024]{2,1,0:T(8,128)S(1)}, u32[]{:S(2)}, u32[]{:S(2)}) collective-permute-start(f32[7,32,1024]{2,1,0:T(8,128)} %pad_maximum_fusion.1), channel_id=1, source_target_pairs={{0,1},{1,2},{2,3},{3,4},{4,5},{5,6},{6,7},{7,8},{8,9},{9,10},{10,1... | collective-permute-start | bytes 2752520 | tf_op jit(solution)/shard_map/ppermute | solution.py:296
  13.4 13.4 %copy-start = (f32[2,3,32,1024]{3,2,1,0:T(8,128)S(1)}, f32[2,3,32,1024]{3,2,1,0:T(8,128)}, u32[]{:S(2)}) copy-start(f32[2,3,32,1024]{3,2,1,0:T(8,128)} %refs_10_.3) | copy-start | bytes 2359300
  15.3 19.2 %collective-permute-start.2 = (f32[5,32,1024]{2,1,0:T(8,128)}, f32[5,32,1024]{2,1,0:T(8,128)}, u32[]{:S(2)}, u32[]{:S(2)}) collective-permute-start(f32[5,32,1024]{2,1,0:T(8,128)} %pad_maximum_fusion.2), channel_id=1, source_target_pairs={{0,31},{1,0},{2,1},{3,2},{4,3},{5,4},{6,5},{7,6},{8,7},{9,8},{10,9... | collective-permute-start | bytes 1966088 | tf_op jit(solution)/shard_map/ppermute | solution.py:296
  20.5 14.0 %collective-permute-start.1 = (f32[5,32,1024]{2,1,0:T(8,128)}, f32[5,32,1024]{2,1,0:T(8,128)}, u32[]{:S(2)}, u32[]{:S(2)}) collective-permute-start(f32[5,32,1024]{2,1,0:T(8,128)} %pad_maximum_fusion.2), channel_id=1, source_target_pairs={{0,1},{1,2},{2,3},{3,4},{4,5},{5,6},{6,7},{7,8},{8,9},{9,10},{10,1... | collective-permute-start | bytes 1966088 | tf_op jit(solution)/shard_map/ppermute | solution.py:296
  33.9 14.2 %copy-start.3 = (f32[1,32,1024]{2,1,0:T(8,128)S(1)}, f32[1,32,1024]{2,1,0:T(8,128)}, u32[]{:S(2)}) copy-start(f32[1,32,1024]{2,1,0:T(8,128)} %copy-done.2) | copy-start | bytes 393220
  33.9 14.2 %copy-start.5 = (f32[32,1024]{1,0:T(8,128)S(1)}, f32[32,1024]{1,0:T(8,128)}, u32[]{:S(2)}) copy-start(f32[32,1024]{1,0:T(8,128)} %param.8) | copy-start | bytes 393220
  33.9 26.2 %collective-permute-start.12 = (f32[3,32,1024]{2,1,0:T(8,128)S(1)}, f32[3,32,1024]{2,1,0:T(8,128)S(1)}, u32[]{:S(2)}, u32[]{:S(2)}) collective-permute-start(f32[3,32,1024]{2,1,0:T(8,128)S(1)} %get-tuple-element.12.refs_1_), channel_id=1, source_target_pairs={{0,31},{1,0},{2,1},{3,2},{4,3},{5,4},{6,5},{7,6},{8,7},{9,8},{10,9... | collective-permute-start | bytes 1179656 | tf_op jit(solution)/shard_map/ppermute | solution.py:296
  34.0 26.1 %collective-permute-start.11 = (f32[3,32,1024]{2,1,0:T(8,128)S(1)}, f32[3,32,1024]{2,1,0:T(8,128)S(1)}, u32[]{:S(2)}, u32[]{:S(2)}) collective-permute-start(f32[3,32,1024]{2,1,0:T(8,128)S(1)} %get-tuple-element.12.refs_1_), channel_id=1, source_target_pairs={{0,1},{1,2},{2,3},{3,4},{4,5},{5,6},{6,7},{7,8},{8,9},{9,10},{10,1... | collective-permute-start | bytes 1179656 | tf_op jit(solution)/shard_map/ppermute | solution.py:296
  43.4 26.2 %collective-permute-start.6 = (f32[3,32,1024]{2,1,0:T(8,128)S(1)}, f32[3,32,1024]{2,1,0:T(8,128)S(1)}, u32[]{:S(2)}, u32[]{:S(2)}) collective-permute-start(f32[3,32,1024]{2,1,0:T(8,128)S(1)} %get-tuple-element.11.refs_1_), channel_id=1, source_target_pairs={{0,31},{1,0},{2,1},{3,2},{4,3},{5,4},{6,5},{7,6},{8,7},{9,8},{10,9... | collective-permute-start | bytes 1179656 | tf_op jit(solution)/shard_map/ppermute | solution.py:296
  48.1 21.5 %collective-permute-start.5 = (f32[3,32,1024]{2,1,0:T(8,128)S(1)}, f32[3,32,1024]{2,1,0:T(8,128)S(1)}, u32[]{:S(2)}, u32[]{:S(2)}) collective-permute-start(f32[3,32,1024]{2,1,0:T(8,128)S(1)} %get-tuple-element.11.refs_1_), channel_id=1, source_target_pairs={{0,1},{1,2},{2,3},{3,4},{4,5},{5,6},{6,7},{7,8},{8,9},{9,10},{10,1... | collective-permute-start | bytes 1179656 | tf_op jit(solution)/shard_map/ppermute | solution.py:296
  48.1 6.2 %collective-permute-start.10 = (f32[2,8,1024]{2,1,0:T(8,128)S(1)}, f32[2,8,1024]{2,1,0:T(8,128)S(1)}, u32[]{:S(2)}, u32[]{:S(2)}) collective-permute-start(f32[2,8,1024]{2,1,0:T(8,128)S(1)} %get-tuple-element.25), channel_id=1, source_target_pairs={{0,30},{1,31},{2,0},{3,1},{4,2},{5,3},{6,4},{7,5},{8,6},{9,7},{10,... | collective-permute-start | bytes 196616 | tf_op jit(solution)/shard_map/ppermute | solution.py:300
  54.3 15.2 %collective-permute-start.8 = (f32[3,8,1024]{2,1,0:T(8,128)S(1)}, f32[3,8,1024]{2,1,0:T(8,128)S(1)}, u32[]{:S(2)}, u32[]{:S(2)}) collective-permute-start(f32[3,8,1024]{2,1,0:T(8,128)S(1)} %get-tuple-element.23), channel_id=1, source_target_pairs={{0,30},{1,31},{2,0},{3,1},{4,2},{5,3},{6,4},{7,5},{8,6},{9,7},{10,... | collective-permute-start | bytes 294920 | tf_op jit(solution)/shard_map/ppermute | solution.py:300
  60.1 9.4 %collective-permute-start.7 = (f32[3,8,1024]{2,1,0:T(8,128)S(1)}, f32[3,8,1024]{2,1,0:T(8,128)S(1)}, u32[]{:S(2)}, u32[]{:S(2)}) collective-permute-start(f32[3,8,1024]{2,1,0:T(8,128)S(1)} %get-tuple-element.24), channel_id=1, source_target_pairs={{0,2},{1,3},{2,4},{3,5},{4,6},{5,7},{6,8},{7,9},{8,10},{9,11},{10,... | collective-permute-start | bytes 294920 | tf_op jit(solution)/shard_map/ppermute | solution.py:299
  60.2 9.4 %collective-permute-start.9 = (f32[2,8,1024]{2,1,0:T(8,128)S(1)}, f32[2,8,1024]{2,1,0:T(8,128)S(1)}, u32[]{:S(2)}, u32[]{:S(2)}) collective-permute-start(f32[2,8,1024]{2,1,0:T(8,128)S(1)} %get-tuple-element.26), channel_id=1, source_target_pairs={{0,2},{1,3},{2,4},{3,5},{4,6},{5,7},{6,8},{7,9},{8,10},{9,11},{10,... | collective-permute-start | bytes 196616 | tf_op jit(solution)/shard_map/ppermute | solution.py:299
  77.2 11.4 %collective-permute-start.13 = (f32[3,32,1024]{2,1,0:T(8,128)S(1)}, f32[3,32,1024]{2,1,0:T(8,128)S(1)}, u32[]{:S(2)}, u32[]{:S(2)}) collective-permute-start(f32[3,32,1024]{2,1,0:T(8,128)S(1)} %get-tuple-element.13), channel_id=1, source_target_pairs={{0,32},{32,64},{64,96},{96,0},{1,33},{33,65},{65,97},{97,1},{2,34}... | collective-permute-start | bytes 1179656 | tf_op jit(solution)/shard_map/ppermute | solution.py:322
  78.8 10.2 %collective-permute-start.15 = (f32[3,32,1024]{2,1,0:T(8,128)S(1)}, f32[3,32,1024]{2,1,0:T(8,128)S(1)}, u32[]{:S(2)}, u32[]{:S(2)}) collective-permute-start(f32[3,32,1024]{2,1,0:T(8,128)S(1)} %get-tuple-element.13), channel_id=1, source_target_pairs={{0,96},{32,0},{64,32},{96,64},{1,97},{33,1},{65,33},{97,65},{2,98}... | collective-permute-start | bytes 1179656 | tf_op jit(solution)/shard_map/ppermute | solution.py:323
  88.7 6.9 %collective-permute-start.14 = (f32[3,16,1024]{2,1,0:T(8,128)S(1)}, f32[3,16,1024]{2,1,0:T(8,128)S(1)}, u32[]{:S(2)}, u32[]{:S(2)}) collective-permute-start(f32[3,16,1024]{2,1,0:T(8,128)S(1)} %slice.52), channel_id=1, source_target_pairs={{0,32},{32,64},{64,96},{96,0},{1,33},{33,65},{65,97},{97,1},{2,34}... | collective-permute-start | bytes 589832 | tf_op jit(solution)/shard_map/ppermute | solution.py:326
  89.0 6.6 %collective-permute-start.16 = (f32[3,16,1024]{2,1,0:T(8,128)S(1)}, f32[3,16,1024]{2,1,0:T(8,128)S(1)}, u32[]{:S(2)}, u32[]{:S(2)}) collective-permute-start(f32[3,16,1024]{2,1,0:T(8,128)S(1)} %slice.53), channel_id=1, source_target_pairs={{0,96},{32,0},{64,32},{96,64},{1,97},{33,1},{65,33},{97,65},{2,98}... | collective-permute-start | bytes 589832 | tf_op jit(solution)/shard_map/ppermute | solution.py:326
  95.9 8.4 %collective-permute-start.18 = (f32[3,3,16,1024]{3,2,1,0:T(8,128)S(1)}, f32[3,3,16,1024]{3,2,1,0:T(8,128)S(1)}, u32[]{:S(2)}, u32[]{:S(2)}) collective-permute-start(f32[3,3,16,1024]{3,2,1,0:T(8,128)S(1)} %get-tuple-element.17), channel_id=1, source_target_pairs={{0,31},{1,0},{2,1},{3,2},{4,3},{5,4},{6,5},{7,6},{8,7},{9,8},{10,9... | collective-permute-start | bytes 1769480 | tf_op jit(solution)/shard_map/ppermute | solution.py:300
  96.9 12.6 %collective-permute-start.17 = (f32[3,3,16,1024]{3,2,1,0:T(8,128)S(1)}, f32[3,3,16,1024]{3,2,1,0:T(8,128)S(1)}, u32[]{:S(2)}, u32[]{:S(2)}) collective-permute-start(f32[3,3,16,1024]{3,2,1,0:T(8,128)S(1)} %get-tuple-element.18), channel_id=1, source_target_pairs={{0,1},{1,2},{2,3},{3,4},{4,5},{5,6},{6,7},{7,8},{8,9},{9,10},{10,1... | collective-permute-start | bytes 1769480 | tf_op jit(solution)/shard_map/ppermute | solution.py:299

commit v3 on v2

--- a/solution.py
+++ b/solution.py
@@ -36,9 +36,10 @@
 
 def copy_in(dst, base, src, lead, start, rows, scale=None):
     for g in range(0, rows, 8):
+        count = min(8, rows - g)
         for c in range(dst.shape[0]):
-            val = src[lead + (at(start + g), pl.ds(c * LANES, LANES))]
-            dst[c, at(base + g), :] = val if scale is None else val * scale
+            val = src[lead + (at(start + g, count), pl.ds(c * LANES, LANES))]
+            dst[c, at(base + g, count), :] = val if scale is None else val * scale
 
 
 def each(fields, base, rows, f):
@@ -182,11 +183,11 @@
     in_up, in_dn, in_uu, in_dd = rim_flags(space_ref[0])
     base = 48
     for row, rows, st, cf, inside, c in (
-        (base - n - 8, 8, uup, cuu, in_uu, 0),
+        (base - n - 2, 2, uup, cuu, in_uu, 0),
         (base - n, n, up, cup, in_up, 5),
         (base, n, d, coef, 1.0, 0),
         (base + n, n, dn, cdn, in_dn, 5),
-        (base + 2 * n, 8, ddn, cdd, in_dd, 0),
+        (base + 2 * n, 2, ddn, cdd, in_dd, 0),
     ):
         copy_in(D, row, cf, (c,), 0, rows, inside * (C * C))
         copy_in(A, row, cf, (c + 1,), 0, rows, inside)
@@ -209,28 +210,19 @@
                 total[to] = read_own(src, base, g, c) + more[to]
 
 
-HALO = 16
-
-
-def chain_kernel(n, pos_ref, ca, cb, cc, rup, rdn, coef, cup, cdn, r1, fa, fb, out, E, U, V, FY, D, A, X, Y, Z):
+def chain_kernel(n, pos_ref, ca, cb0, cb1, cc, yup, ydn, zup, zdn, coef, cup, cdn, r1, fa, fb, out, E, U, V, FY, D, A, X, Y, Z):
     tm, space = pos_ref[0], pos_ref[1]
-    base = HALO + 8
+    base, halo, half = 24, 16, cb0.shape[1]
     in_up, in_dn, _, _ = rim_flags(space)
     keep = (in_up, in_dn)
     for row, cf, c, start, rows, inside in (
-        (base - HALO, cup, 5, n - HALO, HALO, in_up),
+        (base - halo, cup, 5, n - halo, halo, in_up),
         (base, coef, 0, 0, n, 1.0),
-        (base + n, cdn, 5, 0, HALO, in_dn),
+        (base + n, cdn, 5, 0, halo, in_dn),
     ):
         copy_in(D, row, cf, (c,), start, rows, inside * (C * C))
         copy_in(A, row, cf, (c + 1,), start, rows, inside)
-    coarse_coefs(D, A, base - HALO, n + 2 * HALO)
-
-    def take(fields, k, own, use):
-        for f, dst in enumerate(fields):
-            copy_in(dst, base - HALO, rup, (k, f), 0, HALO, use)
-            copy_in(dst, base, own, (f,), 0, n, use)
-            copy_in(dst, base + n, rdn, (k, f), 0, HALO, use)
+    coarse_coefs(D, A, base - halo, n + 2 * halo)
 
     def add(lo, rows):
         def put(s):
@@ -244,15 +236,28 @@
     def coarse(reach):
         coarse_step(E, U, V, FY, D, A, base - reach, n + 2 * reach, base, n, keep)
 
-    take((E, U, V), 2, cc, jnp.where(tm >= 3, 1.0, 0.0))
-    flux_rows(FY, V, D, base - HALO, n + 2 * HALO)
+    use = jnp.where(tm >= 3, 1.0, 0.0)
+    for f, dst in enumerate((E, U, V)):
+        copy_in(dst, base - 10, yup, (f,), 2, 10, use)
+        copy_in(dst, base, cc, (f,), 0, n, use)
+        copy_in(dst, base + n, ydn, (f,), 2, 10, use)
+    flux_rows(FY, V, D, base - halo, n + 2 * halo)
     coarse(8)
     coarse(6)
-    take((X, Y, Z), 1, cb, jnp.where(tm >= 2, 1.0, 0.0))
+    use = jnp.where(tm >= 2, 1.0, 0.0)
+    for f, dst in enumerate((X, Y, Z)):
+        copy_in(dst, base - 6, zup, (f,), 0, 6, use)
+        copy_in(dst, base, cb0, (f,), 0, half, use)
+        copy_in(dst, base + half, cb1, (f,), 0, n - half, use)
+        copy_in(dst, base + n, zdn, (f,), 0, 6, use)
     add(base - 8, n + 16)
     coarse(4)
     coarse(2)
-    take((X, Y, Z), 0, ca, jnp.where(tm >= 1, 1.0, 0.0))
+    use = jnp.where(tm >= 1, 1.0, 0.0)
+    for f, dst in enumerate((X, Y, Z)):
+        copy_in(dst, base - 2, yup, (f,), 0, 2, use)
+        copy_in(dst, base, ca, (f,), 0, n, use)
+        copy_in(dst, base + n, ydn, (f,), 0, 2, use)
     add(base - 8, n + 16)
 
     def write(k, first, more):
@@ -272,7 +277,7 @@
     write(1, fb, r1)
 
 
-def call(kernel, n, ncols, rows, fields, outs, *args):
+def call(kernel, n, ncols, rows, fields, cost, outs, *args):
     scratch = [pltpu.VMEM((ncols // LANES, rows, LANES), jnp.float32)] * fields
     vmem = pl.BlockSpec(memory_space=pltpu.VMEM)
     return pl.pallas_call(
@@ -281,7 +286,8 @@
         in_specs=[pl.BlockSpec(memory_space=pltpu.SMEM)] + [vmem] * (len(args) - 1),
         out_specs=jax.tree.map(lambda _: vmem, outs),
         scratch_shapes=scratch,
-        compiler_params=pltpu.CompilerParams(vmem_limit_bytes=32 * 2**20),
+        compiler_params=pltpu.CompilerParams(vmem_limit_bytes=(ncols * rows * fields) * 4 + 2**21),
+        cost_estimate=pl.CostEstimate(flops=cost * 10**6, bytes_accessed=0, transcendentals=0),
     )(*args)
 
 
@@ -303,31 +309,43 @@
     state = jax.ShapeDtypeStruct((3, n, ncols), jnp.float32)
     coef = jnp.stack([depth, mask.astype(jnp.float32) / (1.0 + H * friction)])
 
-    earlier = lax.ppermute(guess[1], "tm", ring(times, 1))
-    bu, bd = sides(jnp.concatenate([guess[0], wind[1], coef]))
+    pack = jnp.concatenate([guess[0], wind[1], coef])
+    bu, bd = sides(pack)
+    last, _ = lax.optimization_barrier((guess[1], pack))
+    earlier = lax.ppermute(last, "tm", ring(times, 1))
+    wu, wd = sides(wind[0])
+    cuu, cdd = ends(coef, 2, 2)
     entry = jnp.where(tm == 0, initial, earlier)
-    au, ad = sides(jnp.concatenate([entry, wind[0]]))
-    cuu, cdd = ends(coef, 8, 2)
+    au, ad = sides(entry)
+    bu, bd, cuu, cdd = lax.optimization_barrier((bu, bd, cuu, cdd))
 
     fine_b = functools.partial(fine_kernel, 1, ((0,), 3, 5))
-    fb, db = call(fine_b, n, ncols, 120, 8, (state, state), where, guess, bu, bd, wind, bu, bd, coef, bu, bd, guess)
+    fb, db = call(fine_b, n, ncols, 120, 8, 60, (state, state), where, guess, bu, bd, wind, bu, bd, coef, bu, bd, guess)
     dbu, dbd = sides(db)
-    fine_a = functools.partial(fine_kernel, 0, ((), 3, 5))
-    fa, da = call(fine_a, n, ncols, 120, 8, (state, state), where, entry, au, ad, wind, au, ad, coef, bu, bd, guess)
+    fine_a = functools.partial(fine_kernel, 0, ((), 0, 5))
+    fa, da = call(fine_a, n, ncols, 120, 8, 60, (state, state), where, entry, au, ad, wind, wu, wd, coef, bu, bd, guess)
     dau, dad = sides(da)
-    dauu, dadd = ends(da, 8, 2)
-    rb = call(relax_b_kernel, n, ncols, 120, 6, state, where, db, dbu, dbd, coef, bu, bd)
-    ra, c1 = call(relax_a_kernel, n, ncols, 144, 6, (state, state), where, da, dau, dad, dauu, dadd, coef, bu, bd, cuu, cdd, rb)
+    dauu, dadd = ends(da, 2, 2)
+    rb = call(relax_b_kernel, n, ncols, 120, 6, 60, state, where, db, dbu, dbd, coef, bu, bd)
+    ra, c1 = call(relax_a_kernel, n, ncols, 144, 6, 60, (state, state), where, da, dau, dad, dauu, dadd, coef, bu, bd, cuu, cdd, rb)
 
     ca = lax.ppermute(c1, "tm", ring(times, 1))
     cc = lax.ppermute(c1, "tm", ring(times, -1))
     half = n // 2
-    cb = jnp.concatenate(
-        [lax.ppermute(ca[:, :half], "tm", ring(times, 1)), lax.ppermute(cc[:, half:], "tm", ring(times, -1))], axis=1
+    cb0 = lax.ppermute(ca[:, :half], "tm", ring(times, 1))
+    cb1 = lax.ppermute(cc[:, half:], "tm", ring(times, -1))
+
+    def skew(x, hop):
+        pairs = [(t * spaces + p, (t + 1) % times * spaces + (p + hop) % spaces) for t in range(times) for p in range(spaces)]
+        return lax.ppermute(x, ("tm", "space"), pairs)
+
+    zup, zdn = skew(ca[:, -6:], 1), skew(ca[:, :6], -1)
+    yup = lax.ppermute(jnp.concatenate([ca[:, -2:], cc[:, -10:]], axis=1), "space", ring(spaces, 1))
+    ydn = lax.ppermute(jnp.concatenate([ca[:, :2], cc[:, :10]], axis=1), "space", ring(spaces, -1))
+    out = jax.ShapeDtypeStruct(guess.shape, jnp.float32)
+    return call(
+        chain_kernel, n, ncols, 88, 9, 20, out, pos, ca, cb0, cb1, cc, yup, ydn, zup, zdn, coef, bu, bd, ra, fa, fb
     )
-    rup, rdn = ends(jnp.stack([ca, cb, cc]), HALO)
-    out = jax.ShapeDtypeStruct(guess.shape, jnp.float32)
-    return call(chain_kernel, n, ncols, 88, 9, out, pos, ca, cb, cc, rup, rdn, coef, bu, bd, ra, fa, fb)
 
 
 def solution(mesh):

time: 113 us -> 119 us (1.053)
  starting transfers between devices: 32.1 us -> 38.2 us
  local copies, waits for them, and re-layouts: 2.21 us -> 4.44 us
  other arithmetic: 4.21 us -> 2.25 us
    ppermute x3 -> x7, waiting for transfers between devices: 6.45 us -> 17 us  [the longest x2 9.4 us: skew(): return lax.ppermute(x, ('tm', 'space'), pairs)]
    ppermute x1, waiting for transfers between devices: 0.01 us -> 9.07 us  [shards(): cc = lax.ppermute(c1, 'tm', ring(times, -1))]
    ppermute x3 -> x2, waiting for transfers between devices: 13 us -> 4 us  [ends(): dn = lax.ppermute(x[..., :rows, :], 'space', ring(spaces, -hop))]
    ppermute x1, waiting for transfers between devices: 8.12 us -> 0.12 us  [shards(): ca = lax.ppermute(c1, 'tm', ring(times, 1))]
    ppermute x3 -> x7, starting transfers between devices: 5.03 us -> 11.6 us  [the longest x1 5.12 us: shards(): lax.ppermute(jnp.concatenate([ca[:, :2], cc[:, :10]], axis=1), 'space', r...]
    ppermute x3 -> x2, starting transfers between devices: 7.37 us -> 1.98 us  [ends(): dn = lax.ppermute(x[..., :rows, :], 'space', ring(spaces, -hop))]
    ppermute x4 -> x5, starting transfers between devices: 15.7 us -> 20.4 us  [sides(): lax.ppermute(x, 'space', ring(spaces, -hop))]
    ppermute x4 -> x5, waiting for transfers between devices: 5.13 us -> 1.73 us  [sides(): lax.ppermute(x, 'space', ring(spaces, hop))]
  transfers between devices with their start and end apart: 19 -> 23, of which waited for: 9 -> 7; matrix products, arithmetic and copies ran while one was open for 4% -> 1% of each run, Pallas kernels for 20% -> 19%
where the time goes in v3:
time: 119 us; the launch traced here: 118 us
  waiting for transfers between devices  39.4 us (33%)
  starting transfers between devices  38.2 us (32%)
  Pallas kernels  33.5 us (28%)
  local copies, waits for them, and re-layouts  4.44 us (4%)
  other arithmetic  2.25 us (2%)
    pallas_call x5, Pallas kernels, call(): pl.pallas_call(lambda *refs: kernel(n, *refs), out_shape=outs, in_specs=[...  33.5 us
    ppermute x5, starting transfers between devices, sides(): lax.ppermute(x, 'space', ring(spaces, -hop))  20.4 us
    ppermute x2, waiting for transfers between devices, skew(): return lax.ppermute(x, ('tm', 'space'), pairs)  9.4 us
    ppermute x1, waiting for transfers between devices, shards(): cc = lax.ppermute(c1, 'tm', ring(times, -1))  9.07 us
    ppermute x1, waiting for transfers between devices, shards(): earlier = lax.ppermute(last, 'tm', ring(times, 1))  7.59 us
    ppermute x2, waiting for transfers between devices, ends(): up = lax.ppermute(x[..., n - rows:, :], 'space', ring(spaces, hop))  7.52 us
    ppermute x1, starting transfers between devices, shards(): lax.ppermute(jnp.concatenate([ca[:, :2], cc[:, :10]], axis=1), 'space', r...  5.12 us
    ppermute x2, waiting for transfers between devices, ends(): dn = lax.ppermute(x[..., :rows, :], 'space', ring(spaces, -hop))  4 us
  transfers between devices with their start and end apart: 23, of which 7 were waited for; matrix products, arithmetic and copies ran while one was open for 1% of the time, Pallas kernels for 19%

profile of v3, /device:TPU:0, one launch (start us, length us, event | category | flops | bytes accessed | tf_op | source)
XLA Modules:
  0.0 118.0 jit_solution(13721653861142900895)
XLA Ops:
  0.0 1.9 %slice_bitcast_fusion.2 = (f32[2,32,1024]{2,1,0:T(8,128)}, f32[2,32,1024]{2,1,0:T(8,128)S(1)}) fusion(f32[2,2,32,1024]{3,2,1,0:T(8,128)} %refs_4_.3), kind=kLoop, calls=%fused_computation.8 | loop fusion | bytes 1048576 | tf_op jit(solution)/shard_map/squeeze | solution.py:316
  1.9 0.1 slice_bitcast_fusion
  1.9 0.8 copy-done.9
  2.8 0.1 copy-done.10
  2.9 0.0 copy-start.4
  2.9 0.9 copy-done.6
  3.8 1.0 pad_maximum_fusion
  4.8 6.0 %collective-permute-start.6 = (f32[7,32,1024]{2,1,0:T(8,128)}, f32[7,32,1024]{2,1,0:T(8,128)S(1)}, u32[]{:S(2)}, u32[]{:S(2)}) collective-permute-start(f32[7,32,1024]{2,1,0:T(8,128)} %pad_maximum_fusion), channel_id=1, source_target_pairs={{0,31},{1,0},{2,1},{3,2},{4,3},{5,4},{6,5},{7,6},{8,7},{9,8},{10,9... | collective-permute-start | bytes 2752520 | tf_op jit(solution)/shard_map/ppermute | solution.py:302
  10.8 1.5 %collective-permute-start = (f32[3,32,1024]{2,1,0:T(8,128)S(1)}, f32[3,32,1024]{2,1,0:T(8,128)}, u32[]{:S(2)}, u32[]{:S(2)}) collective-permute-start(f32[3,32,1024]{2,1,0:T(8,128)S(1)} %get-tuple-element.16), channel_id=1, source_target_pairs={{0,32},{32,64},{64,96},{96,0},{1,33},{33,65},{65,97},{97,1},{2,34}... | collective-permute-start | bytes 1179656 | tf_op jit(solution)/shard_map/ppermute | solution.py:315
  12.3 0.0 collective-permute-start.5
  12.3 7.6 %collective-permute-done = f32[3,32,1024]{2,1,0:T(8,128)} collective-permute-done((f32[3,32,1024]{2,1,0:T(8,128)S(1)}, f32[3,32,1024]{2,1,0:T(8,128)}, u32[]{:S(2)}, u32[]{:S(2)}) %collective-permute-start) | collective-permute-done | bytes 393248 | tf_op jit(solution)/shard_map/ppermute | solution.py:315
  19.9 0.1 broadcast_select_fusion.refs_1_
  20.0 0.0 copy-start.1
  20.0 3.5 %collective-permute-start.2 = (f32[3,32,1024]{2,1,0:T(8,128)S(1)}, f32[3,32,1024]{2,1,0:T(8,128)}, u32[]{:S(2)}, u32[]{:S(2)}) collective-permute-start(f32[3,32,1024]{2,1,0:T(8,128)S(1)} %broadcast_select_fusion.refs_1_), channel_id=1, source_target_pairs={{0,31},{1,0},{2,1},{3,2},{4,3},{5,4},{6,5},{7,6},{8,7},{9,8},{10,9... | collective-permute-start | bytes 1179656 | tf_op jit(solution)/shard_map/ppermute | solution.py:302
  23.5 0.0 collective-permute-start.1
  23.5 0.0 copy-done.5
  23.5 1.4 %collective-permute-start.8 = (f32[2,2,1024]{2,1,0:T(2,128)S(1)}, f32[2,2,1024]{2,1,0:T(2,128)S(1)}, u32[]{:S(2)}, u32[]{:S(2)}) collective-permute-start(f32[2,2,1024]{2,1,0:T(2,128)S(1)} %get-tuple-element.39), channel_id=1, source_target_pairs={{0,30},{1,31},{2,0},{3,1},{4,2},{5,3},{6,4},{7,5},{8,6},{9,7},{10,... | collective-permute-start | bytes 49160 | tf_op jit(solution)/shard_map/ppermute | solution.py:306
  25.0 4.0 %collective-permute-done.8.refs_10_ = f32[2,2,1024]{2,1,0:T(2,128)S(1)} collective-permute-done((f32[2,2,1024]{2,1,0:T(2,128)S(1)}, f32[2,2,1024]{2,1,0:T(2,128)S(1)}, u32[]{:S(2)}, u32[]{:S(2)}) %collective-permute-start.8) | collective-permute-done | bytes 16416 | tf_op jit(solution)/shard_map/ppermute | solution.py:306
  29.0 0.0 collective-permute-start.7
  29.0 7.5 %collective-permute-done.7.refs_9_ = f32[2,2,1024]{2,1,0:T(2,128)S(1)} collective-permute-done((f32[2,2,1024]{2,1,0:T(2,128)S(1)}, f32[2,2,1024]{2,1,0:T(2,128)S(1)}, u32[]{:S(2)}, u32[]{:S(2)}) %collective-permute-start.7) | collective-permute-done | bytes 16416 | tf_op jit(solution)/shard_map/ppermute | solution.py:305
  36.5 0.6 copy-done.2
  37.1 0.7 collective-permute-start.4
  37.7 0.0 collective-permute-done.6.refs_9_.refs_3_.refs_6_.refs_8_.refs_11_
  37.7 0.0 collective-permute-start.3
  37.7 1.0 pad_maximum_fusion.1.refs_7_.refs_4_.refs_6_.refs_9_
  38.7 0.0 collective-permute-done.5.refs_8_.refs_2_.refs_5_.refs_7_.refs_10_
  38.8 7.2 %shard_map.65 = (f32[3,32,1024]{2,1,0:T(8,128)S(1)}, f32[3,32,1024]{2,1,0:T(8,128)S(1)}) custom-call(s32[1]{0:T(128)} %bitcast.1.refs_0_, f32[2,3,32,1024]{3,2,1,0:T(8,128)S(1)} %copy-done, f32[7,32,1024]{2,1,0:T(8,128)S(1)} %collective-permute-done.5.refs_8_.refs_2_.refs_5_.refs_7_.refs_10_, ...), custom_call_target="tpu_custom_call" | custom-call | flops 60000000 | tf_op jit(solution)/shard_map/pallas_call | solution.py:283
  45.9 5.1 %collective-permute-start.14 = (f32[3,32,1024]{2,1,0:T(8,128)S(1)}, f32[3,32,1024]{2,1,0:T(8,128)S(1)}, u32[]{:S(2)}, u32[]{:S(2)}) collective-permute-start(f32[3,32,1024]{2,1,0:T(8,128)S(1)} %get-tuple-element.22.refs_1_), channel_id=1, source_target_pairs={{0,31},{1,0},{2,1},{3,2},{4,3},{5,4},{6,5},{7,6},{8,7},{9,8},{10,9... | collective-permute-start | bytes 1179656 | tf_op jit(solution)/shard_map/ppermute | solution.py:302
  51.1 0.0 collective-permute-done.4.refs_6_
  51.1 0.0 collective-permute-start.13
  51.1 0.0 collective-permute-done.3.refs_5_
  51.1 0.0 collective-permute-done.2.refs_3_
  51.1 0.0 collective-permute-done.1.refs_2_
  51.1 8.4 %shard_map.64 = (f32[3,32,1024]{2,1,0:T(8,128)S(1)}, f32[3,32,1024]{2,1,0:T(8,128)S(1)}) custom-call(s32[1]{0:T(128)} %bitcast.1.refs_0_, f32[3,32,1024]{2,1,0:T(8,128)S(1)} %broadcast_select_fusion.refs_1_, f32[3,32,1024]{2,1,0:T(8,128)} %collective-permute-done.1.refs_2_, f32[3,32,1024]{2,1,0:T(8,128)} %collective-permute-done.2.refs_3_, ...), custom_call_target="tpu_custom_call" | custom-call | flops 60000000 | tf_op jit(solution)/shard_map/pallas_call | solution.py:283
  59.5 5.1 %collective-permute-start.10 = (f32[3,32,1024]{2,1,0:T(8,128)S(1)}, f32[3,32,1024]{2,1,0:T(8,128)S(1)}, u32[]{:S(2)}, u32[]{:S(2)}) collective-permute-start(f32[3,32,1024]{2,1,0:T(8,128)S(1)} %get-tuple-element.19.refs_1_), channel_id=1, source_target_pairs={{0,31},{1,0},{2,1},{3,2},{4,3},{5,4},{6,5},{7,6},{8,7},{9,8},{10,9... | collective-permute-start | bytes 1179656 | tf_op jit(solution)/shard_map/ppermute | solution.py:302
  64.6 0.0 collective-permute-start.9
  64.7 0.5 collective-permute-start.12
  65.2 0.0 collective-permute-done.14.refs_3_
  65.2 1.6 %collective-permute-start.11 = (f32[3,2,1024]{2,1,0:T(2,128)S(1)}, f32[3,2,1024]{2,1,0:T(2,128)S(1)}, u32[]{:S(2)}, u32[]{:S(2)}) collective-permute-start(f32[3,2,1024]{2,1,0:T(2,128)S(1)} %get-tuple-element.38), channel_id=1, source_target_pairs={{0,2},{1,3},{2,4},{3,5},{4,6},{5,7},{6,8},{7,9},{8,10},{9,11},{10,... | collective-permute-start | bytes 73736 | tf_op jit(solution)/shard_map/ppermute | solution.py:305
  66.8 0.0 collective-permute-done.13.refs_2_
  66.8 6.9 %shard_map.66.refs_11_ = f32[3,32,1024]{2,1,0:T(8,128)S(1)} custom-call(s32[1]{0:T(128)} %bitcast.1.refs_0_, f32[3,32,1024]{2,1,0:T(8,128)S(1)} %get-tuple-element.22.refs_1_, f32[3,32,1024]{2,1,0:T(8,128)S(1)} %collective-permute-done.13.refs_2_, f32[3,32,1024]{2,1,0:T(8,128)S(1)} %collective-permute-done.14.refs_3_, ...), custom_call_target="tpu_custom_call" | custom-call | flops 60000000 | tf_op jit(solution)/shard_map/pallas_call | solution.py:283
  73.7 0.0 collective-permute-done.12.refs_5_
  73.7 0.0 collective-permute-done.11.refs_4_
  73.7 0.0 collective-permute-done.10.refs_3_
  73.7 1.7 %collective-permute-done.9.refs_2_ = f32[3,32,1024]{2,1,0:T(8,128)S(1)} collective-permute-done((f32[3,32,1024]{2,1,0:T(8,128)S(1)}, f32[3,32,1024]{2,1,0:T(8,128)S(1)}, u32[]{:S(2)}, u32[]{:S(2)}) %collective-permute-start.9) | collective-permute-done | bytes 393248 | tf_op jit(solution)/shard_map/ppermute | solution.py:302
  75.4 7.7 %shard_map.67 = (f32[3,32,1024]{2,1,0:T(8,128)S(1)}, f32[3,32,1024]{2,1,0:T(8,128)S(1)}) custom-call(s32[1]{0:T(128)} %bitcast.1.refs_0_, f32[3,32,1024]{2,1,0:T(8,128)S(1)} %get-tuple-element.19.refs_1_, f32[3,32,1024]{2,1,0:T(8,128)S(1)} %collective-permute-done.9.refs_2_, f32[3,32,1024]{2,1,0:T(8,128)S(1)} %collective-permute-done.10.refs_3_, ...), custom_call_target="tpu_custom_call" | custom-call | flops 60000000 | tf_op jit(solution)/shard_map/pallas_call | solution.py:283
  83.1 2.6 %collective-permute-start.17 = (f32[3,32,1024]{2,1,0:T(8,128)S(1)}, f32[3,32,1024]{2,1,0:T(8,128)S(1)}, u32[]{:S(2)}, u32[]{:S(2)}) collective-permute-start(f32[3,32,1024]{2,1,0:T(8,128)S(1)} %get-tuple-element.23), channel_id=1, source_target_pairs={{0,96},{32,0},{64,32},{96,64},{1,97},{33,1},{65,33},{97,65},{2,98}... | collective-permute-start | bytes 1179656 | tf_op jit(solution)/shard_map/ppermute | solution.py:333
  85.7 0.0 collective-permute-start.15
  85.7 9.1 %collective-permute-done.17.refs_4_ = f32[3,32,1024]{2,1,0:T(8,128)S(1)} collective-permute-done((f32[3,32,1024]{2,1,0:T(8,128)S(1)}, f32[3,32,1024]{2,1,0:T(8,128)S(1)}, u32[]{:S(2)}, u32[]{:S(2)}) %collective-permute-start.17) | collective-permute-done | bytes 393248 | tf_op jit(solution)/shard_map/ppermute | solution.py:333
  94.8 3.8 %collective-permute-start.18 = (f32[3,16,1024]{2,1,0:T(8,128)S(1)}, f32[3,16,1024]{2,1,0:T(8,128)S(1)}, u32[]{:S(2)}, u32[]{:S(2)}) collective-permute-start(f32[3,16,1024]{2,1,0:T(8,128)S(1)} %slice.69), channel_id=1, source_target_pairs={{0,96},{32,0},{64,32},{96,64},{1,97},{33,1},{65,33},{97,65},{2,98}... | collective-permute-start | bytes 589832 | tf_op jit(solution)/shard_map/ppermute | solution.py:336
  98.5 0.1 collective-permute-done.15.refs_1_
  98.7 0.3 collective-permute-start.22
  99.1 0.8 collective-permute-start.16
  100.0 0.1 collective-permute-start.19
  100.1 5.1 %collective-permute-start.20 = (f32[3,12,1024]{2,1,0:T(8,128)S(1)}, f32[3,12,1024]{2,1,0:T(8,128)S(1)}, u32[]{:S(2)}, u32[]{:S(2)}) collective-permute-start(f32[3,12,1024]{2,1,0:T(8,128)S(1)} %pad_maximum_fusion.3), channel_id=1, source_target_pairs={{0,31},{1,0},{2,1},{3,2},{4,3},{5,4},{6,5},{7,6},{8,7},{9,8},{10,9... | collective-permute-start | bytes 442376 | tf_op jit(solution)/shard_map/ppermute | solution.py:344
  105.2 0.0 collective-permute-done.22.refs_8_
  105.2 0.0 collective-permute-start.21
  105.2 0.1 pad_add_fusion.refs_0_
  105.3 9.4 %collective-permute-done.21.refs_7_ = f32[3,6,1024]{2,1,0:T(8,128)S(1)} collective-permute-done((f32[3,6,1024]{2,1,0:T(8,128)S(1)}, f32[3,6,1024]{2,1,0:T(8,128)S(1)}, u32[]{:S(2)}, u32[]{:S(2)}) %collective-permute-start.21) | collective-permute-done | bytes 73760 | tf_op jit(solution)/shard_map/ppermute | solution.py:340
  114.7 0.0 collective-permute-done.19.refs_5_
  114.7 0.0 collective-permute-done.20.refs_6_
  114.7 0.0 collective-permute-done.18.refs_3_
  114.7 0.0 collective-permute-done.16.refs_2_
  114.7 3.3 %shard_map.68 = f32[2,3,32,1024]{3,2,1,0:T(8,128)} custom-call(s32[2]{0:T(128)S(1)} %pad_add_fusion.refs_0_, f32[3,32,1024]{2,1,0:T(8,128)S(1)} %collective-permute-done.15.refs_1_, f32[3,16,1024]{2,1,0:T(8,128)S(1)} %collective-permute-done.16.refs_2_, f32[3,16,1024]{2,1,0:T(8,128)S(1)} %collective-permute-done.18.refs_3_, ...), custom_call_target="tpu_custom_call" | custom-call | flops 20000000 | tf_op jit(solution)/shard_map/pallas_call | solution.py:283
  (25 shorter events, 0.2 us)
Async XLA Ops:
  0.0 1.9 %copy-start = (f32[2,3,32,1024]{3,2,1,0:T(8,128)S(1)}, f32[2,3,32,1024]{3,2,1,0:T(8,128)}, u32[]{:S(2)}) copy-start(f32[2,3,32,1024]{3,2,1,0:T(8,128)} %refs_10_.3) | copy-start | bytes 2359300
  1.9 0.9 copy-start.9
  1.9 1.0 copy-start.10
  2.8 0.9 copy-start.6
  2.9 1.9 %copy-start.4 = (f32[1,32,1024]{2,1,0:T(8,128)}, f32[1,32,1024]{2,1,0:T(8,128)S(1)}, u32[]{:S(2)}) copy-start(f32[1,32,1024]{2,1,0:T(8,128)S(1)} %divide_bitcast_fusion) | copy-start | bytes 393220
  3.8 16.1 %copy-start.8 = (f32[3,32,1024]{2,1,0:T(8,128)S(1)}, f32[3,32,1024]{2,1,0:T(8,128)}, u32[]{:S(2)}) copy-start(f32[3,32,1024]{2,1,0:T(8,128)} %param.6) | copy-start | bytes 1179652
  4.8 32.9 %collective-permute-start.6 = (f32[7,32,1024]{2,1,0:T(8,128)}, f32[7,32,1024]{2,1,0:T(8,128)S(1)}, u32[]{:S(2)}, u32[]{:S(2)}) collective-permute-start(f32[7,32,1024]{2,1,0:T(8,128)} %pad_maximum_fusion), channel_id=1, source_target_pairs={{0,31},{1,0},{2,1},{3,2},{4,3},{5,4},{6,5},{7,6},{8,7},{9,8},{10,9... | collective-permute-start | bytes 2752520 | tf_op jit(solution)/shard_map/ppermute | solution.py:302
  10.8 9.1 %collective-permute-start = (f32[3,32,1024]{2,1,0:T(8,128)S(1)}, f32[3,32,1024]{2,1,0:T(8,128)}, u32[]{:S(2)}, u32[]{:S(2)}) collective-permute-start(f32[3,32,1024]{2,1,0:T(8,128)S(1)} %get-tuple-element.16), channel_id=1, source_target_pairs={{0,32},{32,64},{64,96},{96,0},{1,33},{33,65},{65,97},{97,1},{2,34}... | collective-permute-start | bytes 1179656 | tf_op jit(solution)/shard_map/ppermute | solution.py:315
  12.3 26.4 %collective-permute-start.5 = (f32[7,32,1024]{2,1,0:T(8,128)}, f32[7,32,1024]{2,1,0:T(8,128)S(1)}, u32[]{:S(2)}, u32[]{:S(2)}) collective-permute-start(f32[7,32,1024]{2,1,0:T(8,128)} %pad_maximum_fusion), channel_id=1, source_target_pairs={{0,1},{1,2},{2,3},{3,4},{4,5},{5,6},{6,7},{7,8},{8,9},{9,10},{10,1... | collective-permute-start | bytes 2752520 | tf_op jit(solution)/shard_map/ppermute | solution.py:302
  12.3 11.2 %copy-start.5 = (f32[1,32,1024]{2,1,0:T(8,128)S(1)}, f32[1,32,1024]{2,1,0:T(8,128)}, u32[]{:S(2)}) copy-start(f32[1,32,1024]{2,1,0:T(8,128)} %copy-done.4) | copy-start | bytes 393220
  12.3 11.2 %copy-start.7 = (f32[32,1024]{1,0:T(8,128)S(1)}, f32[32,1024]{1,0:T(8,128)}, u32[]{:S(2)}) copy-start(f32[32,1024]{1,0:T(8,128)} %param.8) | copy-start | bytes 393220
  20.0 18.8 %copy-start.1 = (f32[2,2,32,1024]{3,2,1,0:T(8,128)S(1)}, f32[2,2,32,1024]{3,2,1,0:T(8,128)}, u32[]{:S(2)}) copy-start(f32[2,2,32,1024]{3,2,1,0:T(8,128)} %refs_4_.3) | copy-start | bytes 1572868
  20.0 31.1 %collective-permute-start.2 = (f32[3,32,1024]{2,1,0:T(8,128)S(1)}, f32[3,32,1024]{2,1,0:T(8,128)}, u32[]{:S(2)}, u32[]{:S(2)}) collective-permute-start(f32[3,32,1024]{2,1,0:T(8,128)S(1)} %broadcast_select_fusion.refs_1_), channel_id=1, source_target_pairs={{0,31},{1,0},{2,1},{3,2},{4,3},{5,4},{6,5},{7,6},{8,7},{9,8},{10,9... | collective-permute-start | bytes 1179656 | tf_op jit(solution)/shard_map/ppermute | solution.py:302
  23.5 27.6 %collective-permute-start.1 = (f32[3,32,1024]{2,1,0:T(8,128)S(1)}, f32[3,32,1024]{2,1,0:T(8,128)}, u32[]{:S(2)}, u32[]{:S(2)}) collective-permute-start(f32[3,32,1024]{2,1,0:T(8,128)S(1)} %broadcast_select_fusion.refs_1_), channel_id=1, source_target_pairs={{0,1},{1,2},{2,3},{3,4},{4,5},{5,6},{6,7},{7,8},{8,9},{9,10},{10,1... | collective-permute-start | bytes 1179656 | tf_op jit(solution)/shard_map/ppermute | solution.py:302
  23.5 5.4 %collective-permute-start.8 = (f32[2,2,1024]{2,1,0:T(2,128)S(1)}, f32[2,2,1024]{2,1,0:T(2,128)S(1)}, u32[]{:S(2)}, u32[]{:S(2)}) collective-permute-start(f32[2,2,1024]{2,1,0:T(2,128)S(1)} %get-tuple-element.39), channel_id=1, source_target_pairs={{0,30},{1,31},{2,0},{3,1},{4,2},{5,3},{6,4},{7,5},{8,6},{9,7},{10,... | collective-permute-start | bytes 49160 | tf_op jit(solution)/shard_map/ppermute | solution.py:306
  29.0 7.5 %collective-permute-start.7 = (f32[2,2,1024]{2,1,0:T(2,128)S(1)}, f32[2,2,1024]{2,1,0:T(2,128)S(1)}, u32[]{:S(2)}, u32[]{:S(2)}) collective-permute-start(f32[2,2,1024]{2,1,0:T(2,128)S(1)} %get-tuple-element.40), channel_id=1, source_target_pairs={{0,2},{1,3},{2,4},{3,5},{4,6},{5,7},{6,8},{7,9},{8,10},{9,11},{10,... | collective-permute-start | bytes 49160 | tf_op jit(solution)/shard_map/ppermute | solution.py:305
  36.5 0.6 copy-start.2
  37.1 14.0 %collective-permute-start.4 = (f32[2,32,1024]{2,1,0:T(8,128)}, f32[2,32,1024]{2,1,0:T(8,128)}, u32[]{:S(2)}, u32[]{:S(2)}) collective-permute-start(f32[2,32,1024]{2,1,0:T(8,128)} %get-tuple-element.29), channel_id=1, source_target_pairs={{0,31},{1,0},{2,1},{3,2},{4,3},{5,4},{6,5},{7,6},{8,7},{9,8},{10,9... | collective-permute-start | bytes 786440 | tf_op jit(solution)/shard_map/ppermute | solution.py:302
  37.7 13.3 %collective-permute-start.3 = (f32[2,32,1024]{2,1,0:T(8,128)}, f32[2,32,1024]{2,1,0:T(8,128)}, u32[]{:S(2)}, u32[]{:S(2)}) collective-permute-start(f32[2,32,1024]{2,1,0:T(8,128)} %get-tuple-element.29), channel_id=1, source_target_pairs={{0,1},{1,2},{2,3},{3,4},{4,5},{5,6},{6,7},{7,8},{8,9},{9,10},{10,1... | collective-permute-start | bytes 786440 | tf_op jit(solution)/shard_map/ppermute | solution.py:302
  45.9 19.3 %collective-permute-start.14 = (f32[3,32,1024]{2,1,0:T(8,128)S(1)}, f32[3,32,1024]{2,1,0:T(8,128)S(1)}, u32[]{:S(2)}, u32[]{:S(2)}) collective-permute-start(f32[3,32,1024]{2,1,0:T(8,128)S(1)} %get-tuple-element.22.refs_1_), channel_id=1, source_target_pairs={{0,31},{1,0},{2,1},{3,2},{4,3},{5,4},{6,5},{7,6},{8,7},{9,8},{10,9... | collective-permute-start | bytes 1179656 | tf_op jit(solution)/shard_map/ppermute | solution.py:302
  51.1 15.7 %collective-permute-start.13 = (f32[3,32,1024]{2,1,0:T(8,128)S(1)}, f32[3,32,1024]{2,1,0:T(8,128)S(1)}, u32[]{:S(2)}, u32[]{:S(2)}) collective-permute-start(f32[3,32,1024]{2,1,0:T(8,128)S(1)} %get-tuple-element.22.refs_1_), channel_id=1, source_target_pairs={{0,1},{1,2},{2,3},{3,4},{4,5},{5,6},{6,7},{7,8},{8,9},{9,10},{10,1... | collective-permute-start | bytes 1179656 | tf_op jit(solution)/shard_map/ppermute | solution.py:302
  59.5 14.2 %collective-permute-start.10 = (f32[3,32,1024]{2,1,0:T(8,128)S(1)}, f32[3,32,1024]{2,1,0:T(8,128)S(1)}, u32[]{:S(2)}, u32[]{:S(2)}) collective-permute-start(f32[3,32,1024]{2,1,0:T(8,128)S(1)} %get-tuple-element.19.refs_1_), channel_id=1, source_target_pairs={{0,31},{1,0},{2,1},{3,2},{4,3},{5,4},{6,5},{7,6},{8,7},{9,8},{10,9... | collective-permute-start | bytes 1179656 | tf_op jit(solution)/shard_map/ppermute | solution.py:302
  64.6 10.8 %collective-permute-start.9 = (f32[3,32,1024]{2,1,0:T(8,128)S(1)}, f32[3,32,1024]{2,1,0:T(8,128)S(1)}, u32[]{:S(2)}, u32[]{:S(2)}) collective-permute-start(f32[3,32,1024]{2,1,0:T(8,128)S(1)} %get-tuple-element.19.refs_1_), channel_id=1, source_target_pairs={{0,1},{1,2},{2,3},{3,4},{4,5},{5,6},{6,7},{7,8},{8,9},{9,10},{10,1... | collective-permute-start | bytes 1179656 | tf_op jit(solution)/shard_map/ppermute | solution.py:302
  64.7 9.0 %collective-permute-start.12 = (f32[3,2,1024]{2,1,0:T(2,128)S(1)}, f32[3,2,1024]{2,1,0:T(2,128)S(1)}, u32[]{:S(2)}, u32[]{:S(2)}) collective-permute-start(f32[3,2,1024]{2,1,0:T(2,128)S(1)} %get-tuple-element.37), channel_id=1, source_target_pairs={{0,30},{1,31},{2,0},{3,1},{4,2},{5,3},{6,4},{7,5},{8,6},{9,7},{10,... | collective-permute-start | bytes 73736 | tf_op jit(solution)/shard_map/ppermute | solution.py:306
  65.2 10.2 %copy-start.3 = (f32[2,2,1024]{2,1,0:T(2,128)S(1)}, f32[2,2,1024]{2,1,0:T(2,128)}, u32[]{:S(2)}) copy-start(f32[2,2,1024]{2,1,0:T(2,128)} %copy-done.2) | copy-start | bytes 49156
  65.2 8.5 %collective-permute-start.11 = (f32[3,2,1024]{2,1,0:T(2,128)S(1)}, f32[3,2,1024]{2,1,0:T(2,128)S(1)}, u32[]{:S(2)}, u32[]{:S(2)}) collective-permute-start(f32[3,2,1024]{2,1,0:T(2,128)S(1)} %get-tuple-element.38), channel_id=1, source_target_pairs={{0,2},{1,3},{2,4},{3,5},{4,6},{5,7},{6,8},{7,9},{8,10},{9,11},{10,... | collective-permute-start | bytes 73736 | tf_op jit(solution)/shard_map/ppermute | solution.py:305
  83.1 11.7 %collective-permute-start.17 = (f32[3,32,1024]{2,1,0:T(8,128)S(1)}, f32[3,32,1024]{2,1,0:T(8,128)S(1)}, u32[]{:S(2)}, u32[]{:S(2)}) collective-permute-start(f32[3,32,1024]{2,1,0:T(8,128)S(1)} %get-tuple-element.23), channel_id=1, source_target_pairs={{0,96},{32,0},{64,32},{96,64},{1,97},{33,1},{65,33},{97,65},{2,98}... | collective-permute-start | bytes 1179656 | tf_op jit(solution)/shard_map/ppermute | solution.py:333
  85.7 13.0 %collective-permute-start.15 = (f32[3,32,1024]{2,1,0:T(8,128)S(1)}, f32[3,32,1024]{2,1,0:T(8,128)S(1)}, u32[]{:S(2)}, u32[]{:S(2)}) collective-permute-start(f32[3,32,1024]{2,1,0:T(8,128)S(1)} %get-tuple-element.23), channel_id=1, source_target_pairs={{0,32},{32,64},{64,96},{96,0},{1,33},{33,65},{65,97},{97,1},{2,34}... | collective-permute-start | bytes 1179656 | tf_op jit(solution)/shard_map/ppermute | solution.py:332
  94.8 19.9 %collective-permute-start.18 = (f32[3,16,1024]{2,1,0:T(8,128)S(1)}, f32[3,16,1024]{2,1,0:T(8,128)S(1)}, u32[]{:S(2)}, u32[]{:S(2)}) collective-permute-start(f32[3,16,1024]{2,1,0:T(8,128)S(1)} %slice.69), channel_id=1, source_target_pairs={{0,96},{32,0},{64,32},{96,64},{1,97},{33,1},{65,33},{97,65},{2,98}... | collective-permute-start | bytes 589832 | tf_op jit(solution)/shard_map/ppermute | solution.py:336
  98.7 6.5 %collective-permute-start.22 = (f32[3,6,1024]{2,1,0:T(8,128)S(1)}, f32[3,6,1024]{2,1,0:T(8,128)S(1)}, u32[]{:S(2)}, u32[]{:S(2)}) collective-permute-start(f32[3,6,1024]{2,1,0:T(8,128)S(1)} %get-tuple-element.31), channel_id=1, source_target_pairs={{0,63},{1,32},{2,33},{3,34},{4,35},{5,36},{6,37},{7,38},{8,39},{9,... | collective-permute-start | bytes 221192 | tf_op jit(solution)/shard_map/ppermute | solution.py:340
  99.1 15.7 %collective-permute-start.16 = (f32[3,16,1024]{2,1,0:T(8,128)S(1)}, f32[3,16,1024]{2,1,0:T(8,128)S(1)}, u32[]{:S(2)}, u32[]{:S(2)}) collective-permute-start(f32[3,16,1024]{2,1,0:T(8,128)S(1)} %slice.68), channel_id=1, source_target_pairs={{0,32},{32,64},{64,96},{96,0},{1,33},{33,65},{65,97},{97,1},{2,34}... | collective-permute-start | bytes 589832 | tf_op jit(solution)/shard_map/ppermute | solution.py:335
  100.0 14.7 %collective-permute-start.19 = (f32[3,12,1024]{2,1,0:T(8,128)S(1)}, f32[3,12,1024]{2,1,0:T(8,128)S(1)}, u32[]{:S(2)}, u32[]{:S(2)}) collective-permute-start(f32[3,12,1024]{2,1,0:T(8,128)S(1)} %pad_maximum_fusion.2), channel_id=1, source_target_pairs={{0,1},{1,2},{2,3},{3,4},{4,5},{5,6},{6,7},{7,8},{8,9},{9,10},{10,1... | collective-permute-start | bytes 442376 | tf_op jit(solution)/shard_map/ppermute | solution.py:343
  100.1 14.6 %collective-permute-start.20 = (f32[3,12,1024]{2,1,0:T(8,128)S(1)}, f32[3,12,1024]{2,1,0:T(8,128)S(1)}, u32[]{:S(2)}, u32[]{:S(2)}) collective-permute-start(f32[3,12,1024]{2,1,0:T(8,128)S(1)} %pad_maximum_fusion.3), channel_id=1, source_target_pairs={{0,31},{1,0},{2,1},{3,2},{4,3},{5,4},{6,5},{7,6},{8,7},{9,8},{10,9... | collective-permute-start | bytes 442376 | tf_op jit(solution)/shard_map/ppermute | solution.py:344
  105.2 9.5 %collective-permute-start.21 = (f32[3,6,1024]{2,1,0:T(8,128)S(1)}, f32[3,6,1024]{2,1,0:T(8,128)S(1)}, u32[]{:S(2)}, u32[]{:S(2)}) collective-permute-start(f32[3,6,1024]{2,1,0:T(8,128)S(1)} %get-tuple-element.32), channel_id=1, source_target_pairs={{0,33},{1,34},{2,35},{3,36},{4,37},{5,38},{6,39},{7,40},{8,41},{9,... | collective-permute-start | bytes 221192 | tf_op jit(solution)/shard_map/ppermute | solution.py:340

commit v4 on v3

v4 whole, which is shorter than its diff:
```python
import functools

import jax
import jax.numpy as jnp
from jax import lax
from jax.experimental import pallas as pl
from jax.experimental.pallas import tpu as pltpu
from jax.sharding import PartitionSpec as P

FACTOR = 16
H = 0.05
C = 0.5 * H
LANES = 128
SWEEP = 8000


def ring(n, shift):
    return [(i, (i + shift) % n) for i in range(n)]


def at(r, rows=8):
    return pl.ds(r, rows)


FOLD = 4


def diff_cols(chunks):
    lane = lax.broadcasted_iota(jnp.int32, (8, LANES), 1)
    first, last = lane == 0, lane == LANES - 1
    blocks = len(chunks) // FOLD
    left = [pltpu.roll(chunks[b * FOLD + FOLD - 1], 1, 1) for b in range(blocks)]
    right = [pltpu.roll(chunks[b * FOLD], LANES - 1, 1) for b in range(blocks)]
    out = []
    for b in range(blocks):
        for j in range(FOLD):
            c = b * FOLD + j
            lo = chunks[c - 1] if j > 0 else jnp.where(first, left[b - 1] if b > 0 else 0.0, left[b])
            hi = chunks[c + 1] if j < FOLD - 1 else jnp.where(last, right[b + 1] if b + 1 < blocks else 0.0, right[b])
            out.append(hi - lo)
    return out


def fold(chunks):
    lane = lax.broadcasted_iota(jnp.int32, (8, LANES), 1)
    width = LANES // FOLD
    out = []
    for b in range(0, len(chunks), FOLD):
        for j in range(FOLD):
            index = lane * FOLD % LANES + j
            val = jnp.take_along_axis(chunks[b], index, axis=1)
            for k in range(1, FOLD):
                val = jnp.where(lane >= k * width, jnp.take_along_axis(chunks[b + k], index, axis=1), val)
            out.append(val)
    return out


def unfold(chunks):
    lane = lax.broadcasted_iota(jnp.int32, (8, LANES), 1)
    width = LANES // FOLD
    out = []
    for b in range(0, len(chunks), FOLD):
        for k in range(FOLD):
            index = lane // FOLD + k * width
            val = jnp.take_along_axis(chunks[b], index, axis=1)
            for j in range(1, FOLD):
                val = jnp.where(lane % FOLD == j, jnp.take_along_axis(chunks[b + j], index, axis=1), val)
            out.append(val)
    return out


def copy_in(dst, base, src, index, rows, scale=None):
    for g in range(rows // 8):
        for c in range(dst.shape[0]):
            val = src[index(g) + (pl.ds(c * LANES, LANES),)]
            dst[c, at(pl.multiple_of(base + g * 8, 8)), :] = val if scale is None else val * scale


def plane(f, start=0):
    return lambda g: (f, at(start + g * 8))


def copy_rows(dst, base, src, f, start, rows, scale):
    for g in range(0, rows, 8):
        count = min(8, rows - g)
        for c in range(dst.shape[0]):
            dst[c, at(base + g, count), :] = src[f, at(start + g, count), pl.ds(c * LANES, LANES)] * scale


def each(fields, base, rows, f):
    def group(g, _):
        for c in range(fields[0].shape[0]):
            f((c, at(base + g * 8), slice(None)))
        return 0

    lax.fori_loop(0, rows // 8, group, 0)


def flux_rows(FY, V, D, base, rows):
    def put(s):
        FY[s] = D[s] * V[s]

    each((FY,), base, rows, put)


def level_pass(E, U, FY, D, r):
    cs = range(E.shape[0])
    dx = diff_cols([D[c, at(r), :] * U[c, at(r), :] for c in cs])
    for c in cs:
        E[c, at(r), :] = E[c, at(r), :] - (dx[c] + (FY[c, at(r + 1), :] - FY[c, at(r - 1), :]))


def velocity_pass(E, U, V, FY, D, A, W, r, gain=None):
    cs = range(E.shape[0])
    dx = diff_cols([E[c, at(r), :] for c in cs])
    for c in cs:
        s = (c, at(r), slice(None))
        dy = E[c, at(r + 1), :] - E[c, at(r - 1), :]
        gx = dx[c]
        if gain is not None:
            gx, dy = gx * gain, dy * gain
        u = A[s] * (U[s] - gx)
        v = A[s] * (V[s] - dy)
        if W is not None:
            u, v = u + W[0][s], v + W[1][s]
        U[s] = u
        V[s] = v
        FY[s] = D[s] * v


def keep_rim(E, base, n, keep):
    for r, k in ((base - 1, keep[0]), (base + n, keep[1])):
        for c in range(E.shape[0]):
            E[c, at(r, 1), :] = E[c, at(r, 1), :] * k


def sweep(E, U, V, FY, D, A, W, base, n, keep, wide):
    for phase in range(FACTOR // 4):
        reach = 2 * FACTOR - 8 * phase
        lo, groups = base - reach, (n + 2 * reach) // 8

        def step(_, carry, lo=lo, groups=groups):
            for g in range(groups + wide):
                level_pass(E, U, FY, D, lo - wide + g * 8)
            keep_rim(E, base, n, keep)
            for g in range(groups):
                velocity_pass(E, U, V, FY, D, A, W, lo + g * 8)
            return carry

        lax.fori_loop(0, 4, step, 0)


def coarse_coefs(D, A, base, rows):
    def put(s):
        D[s] = D[s] * float(FACTOR)
        A[s] = A[s] / (float(FACTOR) - (FACTOR - 1.0) * A[s])

    each((D, A), base, rows, put)


def coarse_step(E, U, V, FY, D, A, lo, rows, base, n, keep):
    for r in range(lo - 1, lo + rows + 1, 8):
        level_pass(E, U, FY, D, r)
    keep_rim(E, base, n, keep)
    for r in range(lo, lo + rows, 8):
        velocity_pass(E, U, V, FY, D, A, None, r, float(FACTOR))


def place(space):
    size = lax.axis_size("space")
    even = lax.rem(space, 2) == 0
    keep = tuple(jnp.where(x, 1.0, 0.0) for x in (space > 0, space < size - 1))
    return even, keep, keep[0] * keep[1]


def read_own(src, base, g, c):
    return src[c, at(base + g), :]


def sides_of(even, base, n):
    return jnp.where(even, base - n, base + n), jnp.where(even, base + n, base - n)


def folded(raw, k, out, f, n):
    def group(g, _):
        rows = at(pl.multiple_of(g * 8, 8))
        cs = range(raw.shape[2] // LANES)
        for c, val in enumerate(fold([raw[k, rows, pl.ds(c * LANES, LANES)] for c in cs])):
            out[f, rows, pl.ds(c * LANES, LANES)] = val
        return 0

    lax.fori_loop(0, n // 8, group, 0)


def main_kernel(n, guess, wind, depth, friction, mask, out, raw, land, sems):
    copies = [
        pltpu.make_async_copy(src, dst, sems.at[i])
        for i, (src, dst) in enumerate(
            (
                (guess.at[0], raw.at[pl.ds(0, 3)]),
                (wind.at[1], raw.at[pl.ds(3, 2)]),
                (depth, raw.at[5]),
                (friction, raw.at[6]),
                (mask, land),
            )
        )
    ]
    for copy in copies:
        copy.start()
    for copy in copies:
        copy.wait()
    raw[6] = land[...].astype(jnp.float32) / (1.0 + H * raw[6])
    for f in range(7):
        folded(raw, f, out, f, n)


def late_kernel(n, guess, wind, initial, _, last, late, raw, sems):
    copies = [
        pltpu.make_async_copy(src, dst, sems.at[i])
        for i, (src, dst) in enumerate(
            ((guess.at[1], raw.at[pl.ds(0, 3)]), (initial, raw.at[pl.ds(3, 3)]), (wind.at[0], raw.at[pl.ds(6, 2)]))
        )
    ]
    for copy in copies:
        copy.start()
    for copy in copies:
        copy.wait()
    for f in range(8):
        folded(raw, f, last if f < 3 else late, f if f < 3 else f - 3, n)


def fine_kernel(n, space_ref, own, across, beside, coef, coef_a, coef_b, nxt, *refs):
    outs, (E, U, V, FY, D, A, W0, W1) = refs[:-8], refs[-8:]
    first, delta = outs[:2]
    even, keep, inside = place(space_ref[0])
    base = 40
    row_a, row_b = sides_of(even, base, n)
    for row, st, cf, ok in ((row_a, across, coef_a, inside), (base, own, coef, 1.0), (row_b, beside, coef_b, 1.0)):
        copy_in(D, row, cf, plane(5), n, ok * (C * C))
        copy_in(A, row, cf, plane(6), n, ok)
        copy_in(E, row, st, plane(0), n, C)
        copy_in(U, row, st, plane(1), n)
        copy_in(V, row, st, plane(2), n)
        copy_in(W0, row, st, plane(3), n, H)
        copy_in(W1, row, st, plane(4), n, H)

    def prepare(s):
        W0[s] = W0[s] * A[s]
        W1[s] = W1[s] * A[s]
        FY[s] = D[s] * V[s]

    each((E,), base - n, 3 * n, prepare)
    sweep(E, U, V, FY, D, A, (W0, W1), base, n, keep, 0)
    for f, src in enumerate((E, U, V)):
        for g in range(0, n, 8):
            for c in range(E.shape[0]):
                to = (f, at(g), pl.ds(c * LANES, LANES))
                val = read_own(src, base, g, c)
                if f == 0:
                    val = val * (1.0 / C)
                first[to] = val
                val = val - nxt[to]
                delta[to] = val
                if len(outs) > 2:
                    outs[2][f * (n // 8) + g // 8, :, pl.ds(c * LANES, LANES)] = val
    if len(outs) > 2:
        for f in range(2):
            outs[2][3 * (n // 8) + f] = jnp.where(even, coef_a[5 + f, at(n - 8), :], coef_a[5 + f, at(0), :])


def relax_b_kernel(n, space_ref, d, across, beside, coef, coef_a, coef_b, res, E, U, V, FY, D, A):
    even, keep, inside = place(space_ref[0])
    base = 40
    row_a, row_b = sides_of(even, base, n)

    def grouped(f):
        return lambda g: (f * (n // 8) + g, slice(None))

    for row, st, cf, ok, index in (
        (row_a, across, coef_a, inside, plane),
        (base, d, coef, 1.0, plane),
        (row_b, beside, coef_b, 1.0, grouped),
    ):
        copy_in(D, row, cf, plane(5), n, ok * (C * C))
        copy_in(A, row, cf, plane(6), n, ok)
        copy_in(E, row, st, index(0), n, C)
        copy_in(U, row, st, index(1), n)
        copy_in(V, row, st, index(2), n)
    flux_rows(FY, V, D, base - n, 3 * n)
    sweep(E, U, V, FY, D, A, None, base, n, keep, 0)
    for f, src in enumerate((E, U, V)):
        for g in range(0, n, 8):
            for c in range(E.shape[0]):
                res[f, at(g), pl.ds(c * LANES, LANES)] = read_own(src, base, g, c)


def relay_kernel(n, space_ref, d, across, out):
    even, _, _ = place(space_ref[0])
    groups = n // 8
    for f in range(3):
        for g in range(groups):
            out[f * groups + g] = d[f, at(g * 8), :]
        out[3 * groups + f] = jnp.where(even, across[f, at(n - 8), :], across[f, at(0), :])


def relax_a_kernel(n, space_ref, d, across, beside, coef, coef_a, coef_b, relay, more, res, total, E, U, V, FY, D, A):
    space = space_ref[0]
    even, keep, inside = place(space)
    base = 48
    row_a, row_b = sides_of(even, base, n)
    row_c = jnp.where(even, base + 2 * n, base - n - 8)
    inside_c = jnp.where(even, jnp.where(space < lax.axis_size("space") - 2, 1.0, 0.0), jnp.where(space > 1, 1.0, 0.0))
    groups = n // 8

    def grouped(f):
        return lambda g: (f * groups + g, slice(None))

    for row, st, cf, ok, index in (
        (row_a, across, coef_a, inside, plane),
        (base, d, coef, 1.0, plane),
        (row_b, beside, coef_b, 1.0, grouped),
    ):
        copy_in(D, row, cf, plane(5), n, ok * (C * C))
        copy_in(A, row, cf, plane(6), n, ok)
        copy_in(E, row, st, index(0), n, C)
        copy_in(U, row, st, index(1), n)
        copy_in(V, row, st, index(2), n)

    def one(k):
        return lambda g: (k, slice(None))

    copy_in(D, row_c, relay, one(3 * groups), 8, inside_c * (C * C))
    copy_in(A, row_c, relay, one(3 * groups + 1), 8, inside_c)
    copy_in(E, row_c, beside, one(3 * groups), 8, C)
    copy_in(U, row_c, beside, one(3 * groups + 1), 8)
    copy_in(V, row_c, beside, one(3 * groups + 2), 8)
    flux_rows(FY, V, D, base - n - 8, 3 * n + 16)
    sweep(E, U, V, FY, D, A, None, base, n, keep, 1)
    for f, src in enumerate((E, U, V)):
        for g in range(0, n, 8):
            for c in range(E.shape[0]):
                res[f, at(g), pl.ds(c * LANES, LANES)] = read_own(src, base, g, c)
    coarse_coefs(D, A, base - 8, n + 16)
    flux_rows(FY, V, D, base - 8, n + 16)
    coarse_step(E, U, V, FY, D, A, base, n, base, n, keep)
    for f, src in enumerate((E, U, V)):
        for g in range(0, n, 8):
            for c in range(E.shape[0]):
                to = (f, at(g), pl.ds(c * LANES, LANES))
                total[to] = read_own(src, base, g, c) + more[to]


RIMS = (2, 6, 10)


def chain_kernel(n, pos_ref, ca, cc, p1, p2, p3, coef, coef_a, coef_b, r1, fa, fb, out, E, U, V, FY, D, A, X, Y, Z):
    tm, space = pos_ref[0], pos_ref[1]
    base, halo = 24, 16
    main, rest = p1.shape[1] - 2 * RIMS[0], p2.shape[1] - 2 * RIMS[2]
    even, keep, inside = place(space)
    odd = jnp.logical_not(even)
    for cond, up, dn, ok_up, ok_dn in ((even, coef_a, coef_b, inside, 1.0), (odd, coef_b, coef_a, 1.0, inside)):

        @pl.when(cond)
        def _(up=up, dn=dn, ok_up=ok_up, ok_dn=ok_dn):
            for f, dst, k in ((5, D, C * C), (6, A, 1.0)):
                copy_in(dst, base - halo, up, plane(f, n - halo), halo, ok_up * k)
                copy_in(dst, base + n, dn, plane(f), halo, ok_dn * k)

    copy_in(D, base, coef, plane(5), n, C * C)
    copy_in(A, base, coef, plane(6), n)
    coarse_coefs(D, A, base - halo, n + 2 * halo)

    def rims(fields, k, src, start, use):
        rows = RIMS[k]
        for f, dst in enumerate(fields):
            copy_rows(dst, base - rows, src, f, start, rows, use)
            copy_rows(dst, base + n, src, f, start + rows, rows, use)

    def add(lo, rows):
        def put(s):
            E[s] = E[s] + X[s]
            U[s] = U[s] + Y[s]
            V[s] = V[s] + Z[s]
            FY[s] = D[s] * V[s]

        each((E,), lo, rows, put)

    def coarse(reach):
        coarse_step(E, U, V, FY, D, A, base - reach, n + 2 * reach, base, n, keep)

    use = jnp.where(tm >= 3, 1.0, 0.0)
    rims((E, U, V), 2, p2, rest, use)
    for f, dst in enumerate((E, U, V)):
        copy_in(dst, base, cc, plane(f), n, use)
    flux_rows(FY, V, D, base - halo, n + 2 * halo)
    coarse(8)
    coarse(6)
    use = jnp.where(tm >= 2, 1.0, 0.0)
    rims((X, Y, Z), 1, p3, 0, use)
    for f, dst in enumerate((X, Y, Z)):
        copy_in(dst, base, p1, plane(f), main, use)
        copy_in(dst, base + main, p2, plane(f), rest, use)
    add(base - 8, n + 16)
    coarse(4)
    coarse(2)
    use = jnp.where(tm >= 1, 1.0, 0.0)
    rims((X, Y, Z), 0, p1, main, use)
    for f, dst in enumerate((X, Y, Z)):
        copy_in(dst, base, ca, plane(f), n, use)
    add(base - 8, n + 16)

    def write(k, first, more):
        for f, src in enumerate((E, U, V)):

            def group(g, carry, f=f, src=src):
                rows = pl.multiple_of(g * 8, 8)
                vals = []
                for c in range(E.shape[0]):
                    to = (f, at(rows), pl.ds(c * LANES, LANES))
                    val = read_own(src, base, rows, c)
                    if more is not None:
                        val = val + more[to]
                    if f == 0:
                        val = val * (1.0 / C)
                    vals.append(first[to] + val)
                for c, val in enumerate(unfold(vals)):
                    out[k, f, at(rows), pl.ds(c * LANES, LANES)] = val
                return carry

            lax.fori_loop(0, n // 8, group, 0)

    write(0, fa, None)
    coarse(0)
    write(1, fb, r1)


def call(kernel, n, ncols, rows, fields, cost, outs, *args, after=()):
    scratch = [pltpu.VMEM((ncols // LANES, rows, LANES), jnp.float32)] * fields
    vmem = pl.BlockSpec(memory_space=pltpu.VMEM)
    return pl.pallas_call(
        lambda *refs: kernel(n, *refs[: len(args)], *refs[len(args) + len(after) :]),
        out_shape=outs,
        in_specs=[pl.BlockSpec(memory_space=pltpu.SMEM)] + [vmem] * (len(args) - 1) + [pl.BlockSpec(memory_space=pl.ANY)] * len(after),
        out_specs=jax.tree.map(lambda _: vmem, outs),
        scratch_shapes=scratch,
        compiler_params=pltpu.CompilerParams(vmem_limit_bytes=(ncols * rows * fields) * 4 + 2**21),
        cost_estimate=pl.CostEstimate(flops=cost * 10**6, bytes_accessed=0, transcendentals=0),
    )(*args, *after)


def packed(kernel, n, ncols, fields, scratch, *args):
    def block(k):
        return jax.ShapeDtypeStruct((k, n, ncols), jnp.float32)

    return pl.pallas_call(
        functools.partial(kernel, n),
        out_shape=[block(k) for k in fields],
        in_specs=[pl.BlockSpec(memory_space=pl.ANY)] * len(args),
        out_specs=[pl.BlockSpec(memory_space=pltpu.VMEM)] * len(fields),
        scratch_shapes=[pltpu.VMEM(x.shape, x.dtype) for x in scratch] + [pltpu.SemaphoreType.DMA((len(args),))],
        compiler_params=pltpu.CompilerParams(vmem_limit_bytes=4 * 2**20),
    )(*args)


def shards(initial, guess, depth, friction, mask, wind):
    n, ncols = depth.shape
    spaces, times = lax.axis_size("space"), lax.axis_size("tm")
    tm, space = lax.axis_index("tm"), lax.axis_index("space")
    pos = jnp.stack([tm, space]).astype(jnp.int32)
    where = space.astype(jnp.int32)[None]
    even = space % 2 == 0

    def across(x):
        return lax.ppermute(x, "space", [(i, (i - 1 if i % 2 == 0 else i + 1) % spaces) for i in range(spaces)])

    def beside(x):
        return lax.ppermute(x, "space", [(i, i ^ 1) for i in range(spaces)])

    state = jax.ShapeDtypeStruct((3, n, ncols), jnp.float32)
    both = jax.ShapeDtypeStruct((3 * (n // 8) + 2, 8, ncols), jnp.float32)
    raw = jax.ShapeDtypeStruct((8, n, ncols), jnp.float32)
    (b_own,) = packed(main_kernel, n, ncols, (7,), (raw, mask), guess, wind, depth, friction, mask)
    b_a, b_b = across(b_own), beside(b_own)
    last, late = packed(late_kernel, n, ncols, (3, 5), (raw,), guess, wind, initial, b_own)
    earlier = lax.ppermute(last, "tm", ring(times, 1))
    a_own = jnp.concatenate([jnp.where(tm == 0, late[:3], earlier), late[3:]])
    a_a, a_b = across(a_own), beside(a_own)

    fb, db, db_pack = call(fine_kernel, n, ncols, 120, 8, SWEEP, (state, state, both), where, b_own, b_a, b_b, b_own, b_a, b_b, last)
    db_a, db_b = across(db), beside(db_pack)
    fa, da = call(fine_kernel, n, ncols, 120, 8, SWEEP, (state, state), where, a_own, a_a, a_b, b_own, b_a, b_b, b_own, after=(db,))
    da_a = across(da)
    rb = call(relax_b_kernel, n, ncols, 120, 6, SWEEP, state, where, db, db_a, db_b, b_own, b_a, b_b, after=(da,))
    more = jax.ShapeDtypeStruct((3 * (n // 8) + 3, 8, ncols), jnp.float32)
    da_b = beside(call(relay_kernel, n, ncols, 8, 0, 1, more, where, da, da_a, after=(rb,)))
    ra, c1 = call(relax_a_kernel, n, ncols, 144, 6, SWEEP, (state, state), where, da, da_a, da_b, b_own, b_a, b_b, db_b, rb)

    ca = lax.ppermute(c1, "tm", ring(times, 1))
    cc = lax.ppermute(c1, "tm", ring(times, -1))
    rim_a = across(jnp.where(even, c1[:, : RIMS[2]], c1[:, -RIMS[2] :]))
    rim_b = beside(jnp.where(even, c1[:, -RIMS[2] :], c1[:, : RIMS[2]]))
    up, dn = jnp.where(even, rim_a, rim_b), jnp.where(even, rim_b, rim_a)
    main = n - 8
    p1 = jnp.concatenate([ca[:, :main], up[:, -RIMS[0] :], dn[:, : RIMS[0]]], axis=1)
    p2 = jnp.concatenate([cc[:, main:], up, dn], axis=1)
    p3 = jnp.concatenate([up[:, -RIMS[1] :], dn[:, : RIMS[1]]], axis=1)
    p1 = lax.ppermute(p1, "tm", ring(times, 1))
    p2 = lax.ppermute(p2, "tm", ring(times, -1))
    p3 = lax.ppermute(p3, "tm", ring(times, 2))
    out = jax.ShapeDtypeStruct(guess.shape, jnp.float32)
    return call(
        chain_kernel, n, ncols, 88, 9, SWEEP // 2, out, pos, ca, cc, p1, p2, p3, b_own, b_a, b_b, ra, fa, fb
    )


def solution(mesh):
    return jax.shard_map(
        shards,
        mesh=mesh,
        in_specs=(
            P(None, "space", None),
            P("tm", None, "space", None),
            P("space", None),
            P("space", None),
            P("space", None),
            P("tm", None, "space", None),
        ),
        out_specs=P("tm", None, "space", None),
        check_vma=False,
    )
```

time: 119 us -> 114 us (0.958)
  starting transfers between devices: 38.2 us -> 20.8 us
  local copies, waits for them, and re-layouts: 4.44 us -> 10.6 us
  waiting for transfers between devices: 39.4 us -> 44.3 us
  Pallas kernels: 33.5 us -> 36.8 us
  other arithmetic: 2.25 us -> 0.35 us
    ppermute x20 -> x13, starting transfers between devices: 34.1 us -> 16.5 us  [the longest x5 11.4 us: across(): lax.ppermute(x, 'space', [(i, (i - 1 if i % 2 == 0 else i + 1) % spaces)...]
    ppermute x20 -> x13, waiting for transfers between devices: 22.7 us -> 33 us  [the longest x5 16.2 us: across(): lax.ppermute(x, 'space', [(i, (i - 1 if i % 2 == 0 else i + 1) % spaces)...]
    ppermute x1, waiting for transfers between devices: 9.07 us -> 0.07 us  [shards(): cc = lax.ppermute(c1, 'tm', ring(times, -1))]
    unnamed x22 -> x34, local copies, waits for them, and re-layouts: 2.41 us -> 9.82 us
    pallas_call x5 -> x8, Pallas kernels: 33.5 us -> 36.8 us  [the longest x6 26.6 us: call(): pl.pallas_call(lambda *refs: kernel(n, *refs[:len(args)], *refs[len(args)...]
    ppermute x1, waiting for transfers between devices: 7.59 us -> 10.8 us  [shards(): earlier = lax.ppermute(last, 'tm', ring(times, 1))]
    squeeze x2 -> x0, local copies, waits for them, and re-layouts: 1.91 us -> none  [the longest x1 1.85 us: shards(): wu, wd = sides(wind[0])]
  transfers between devices with their start and end apart: 23 -> 16, of which waited for: 7 -> 9; matrix products, arithmetic and copies ran while one was open for 1% -> 1% of each run, Pallas kernels for 19% -> 18%
where the time goes in v4:
time: 114 us; the launch traced here: 113 us
  waiting for transfers between devices  44.3 us (39%)
  Pallas kernels  36.8 us (32%)
  starting transfers between devices  20.8 us (18%)
  local copies, waits for them, and re-layouts  10.6 us (9%)
    pallas_call x6, Pallas kernels, call(): pl.pallas_call(lambda *refs: kernel(n, *refs[:len(args)], *refs[len(args)...  26.6 us
    ppermute x5, waiting for transfers between devices, across(): lax.ppermute(x, 'space', [(i, (i - 1 if i % 2 == 0 else i + 1) % spaces)...  16.2 us
    ppermute x1, waiting for transfers between devices, shards(): p3 = lax.ppermute(p3, 'tm', ring(times, 2))  12.7 us
    ppermute x5, starting transfers between devices, across(): lax.ppermute(x, 'space', [(i, (i - 1 if i % 2 == 0 else i + 1) % spaces)...  11.4 us
    ppermute x1, waiting for transfers between devices, shards(): earlier = lax.ppermute(last, 'tm', ring(times, 1))  10.8 us
    pallas_call x2, Pallas kernels, packed(): pl.pallas_call(functools.partial(kernel, n), out_shape=[block(k) for k in...  10.2 us
    unnamed x34, local copies, waits for them, and re-layouts  9.82 us
    ppermute x1, starting transfers between devices, shards(): p2 = lax.ppermute(p2, 'tm', ring(times, -1))  3.76 us
  transfers between devices with their start and end apart: 16, of which 9 were waited for; matrix products, arithmetic and copies ran while one was open for 1% of the time, Pallas kernels for 18%

profile of v4, /device:TPU:0, one launch (start us, length us, event | category | flops | bytes accessed | tf_op | source)
XLA Modules:
  0.0 113.1 jit_solution(6534266991855359675)
XLA Ops:
  0.0 1.1 copy-done
  1.1 1.0 copy-done.1
  2.2 0.9 copy-done.3
  3.1 0.9 copy-done.4
  4.0 0.9 copy-done.5
  4.9 4.7 %shard_map.64._.refs_1_.refs_4_.refs_7_.refs_6_ = f32[7,32,1024]{2,1,0:T(8,128)S(1)} custom-call(f32[2,3,32,1024]{3,2,1,0:T(8,128)S(1)} %copy-done, f32[2,2,32,1024]{3,2,1,0:T(8,128)S(1)} %copy-done.1, f32[32,1024]{1,0:T(8,128)S(1)} %copy-done.3, f32[32,1024]{1,0:T(8,128)S(1)} %copy-done.4, s32[32,1024]{1,0:T(8,128)S(1)} %copy-done.5), custom_call_target="tpu_custom_call" | custom-call | tf_op jit(solution)/shard_map/pallas_call | solution.py:456
  9.6 6.1 %collective-permute-start.3 = (f32[7,32,1024]{2,1,0:T(8,128)S(1)}, f32[7,32,1024]{2,1,0:T(8,128)S(1)}, u32[]{:S(2)}, u32[]{:S(2)}) collective-permute-start(f32[7,32,1024]{2,1,0:T(8,128)S(1)} %shard_map.64._.refs_1_.refs_4_.refs_7_.refs_6_), channel_id=1, source_target_pairs={{0,31},{1,2},{2,1},{3,4},{4,3},{5,6},{6,5},{7,8},{8,7},{9,10},{10,... | collective-permute-start | bytes 2752520 | tf_op jit(solution)/shard_map/ppermute | solution.py:475
  15.7 0.0 collective-permute-start.4
  15.7 0.0 copy-done.2
  15.7 5.5 %shard_map.65 = (f32[3,32,1024]{2,1,0:T(8,128)}, f32[5,32,1024]{2,1,0:T(8,128)S(1)}) custom-call(f32[2,3,32,1024]{3,2,1,0:T(8,128)S(1)} %copy-done, f32[2,2,32,1024]{3,2,1,0:T(8,128)S(1)} %copy-done.1, f32[3,32,1024]{2,1,0:T(8,128)S(1)} %copy-done.2, f32[7,32,1024]{2,1,0:T(8,128)S(1)} %shard_map.64._.refs_1_.refs_4_.refs_7_.refs_6_), custom_call_target="tpu_custom_call" | custom-call | tf_op jit(solution)/shard_map/pallas_call | solution.py:456
  21.2 1.6 %collective-permute-start = (f32[3,32,1024]{2,1,0:T(8,128)}, f32[3,32,1024]{2,1,0:T(8,128)}, u32[]{:S(2)}, u32[]{:S(2)}) collective-permute-start(f32[3,32,1024]{2,1,0:T(8,128)} %get-tuple-element.15.refs_7_), channel_id=1, source_target_pairs={{0,32},{32,64},{64,96},{96,0},{1,33},{33,65},{65,97},{97,1},{2,34}... | collective-permute-start | bytes 1179656 | tf_op jit(solution)/shard_map/ppermute | solution.py:486
  22.8 0.7 slice.33
  23.5 10.8 %collective-permute-done = f32[3,32,1024]{2,1,0:T(8,128)} collective-permute-done((f32[3,32,1024]{2,1,0:T(8,128)}, f32[3,32,1024]{2,1,0:T(8,128)}, u32[]{:S(2)}, u32[]{:S(2)}) %collective-permute-start) | collective-permute-done | bytes 393248 | tf_op jit(solution)/shard_map/ppermute | solution.py:486
  34.3 0.1 slice_select_fusion
  34.4 0.0 copy-done.16
  34.4 0.1 pad_maximum_fusion.refs_1_
  34.4 0.2 collective-permute-start.1
  34.6 0.0 collective-permute-start.2
  34.6 0.0 collective-permute-done.3.refs_2_.refs_5_.refs_7_
  34.6 0.0 collective-permute-done.4.refs_3_.refs_6_.refs_8_
  34.6 0.0 copy-start.6
  34.7 5.8 %shard_map.66 = (f32[3,32,1024]{2,1,0:T(8,128)S(1)}, f32[3,32,1024]{2,1,0:T(8,128)S(1)}, f32[14,8,1024]{2,1,0:T(8,128)S(1)}) custom-call(s32[1]{0:T(128)} %bitcast.1.refs_0_, f32[7,32,1024]{2,1,0:T(8,128)S(1)} %shard_map.64._.refs_1_.refs_4_.refs_7_.refs_6_, f32[7,32,1024]{2,1,0:T(8,128)S(1)} %collective-permute-done.3.refs_2_.refs_5_.refs_7_, ...), custom_call_target="tpu_custom_call" | custom-call | flops 8000000000 | tf_op jit(solution)/shard_map/pallas_call | solution.py:441
  40.5 0.0 copy-done.6
  40.5 0.0 copy-start.12
  40.5 0.7 copy-done.12
  41.3 5.0 %collective-permute-start.6 = (f32[3,32,1024]{2,1,0:T(8,128)S(1)}, f32[3,32,1024]{2,1,0:T(8,128)S(1)}, u32[]{:S(2)}, u32[]{:S(2)}) collective-permute-start(f32[3,32,1024]{2,1,0:T(8,128)S(1)} %get-tuple-element.16.refs_8_.refs_1_), channel_id=1, source_target_pairs={{0,31},{1,2},{2,1},{3,4},{4,3},{5,6},{6,5},{7,8},{8,7},{9,10},{10,... | collective-permute-start | bytes 1179656 | tf_op jit(solution)/shard_map/ppermute | solution.py:475
  46.2 0.0 collective-permute-start.7
  46.2 1.6 %collective-permute-done.1.refs_2_ = f32[5,32,1024]{2,1,0:T(8,128)S(1)} collective-permute-done((f32[5,32,1024]{2,1,0:T(8,128)S(1)}, f32[5,32,1024]{2,1,0:T(8,128)S(1)}, u32[]{:S(2)}, u32[]{:S(2)}) %collective-permute-start.1) | collective-permute-done | bytes 655392 | tf_op jit(solution)/shard_map/ppermute | solution.py:475
  47.9 0.0 collective-permute-done.2.refs_3_
  47.9 1.2 %copy-done.7 = f32[7,32,1024]{2,1,0:T(8,128)S(1)} copy-done((f32[7,32,1024]{2,1,0:T(8,128)S(1)}, f32[7,32,1024]{2,1,0:T(8,128)}, u32[]{:S(2)}) %copy-start.7) | copy-done | bytes 917528
  49.0 4.5 %shard_map.67 = (f32[3,32,1024]{2,1,0:T(8,128)S(1)}, f32[3,32,1024]{2,1,0:T(8,128)S(1)}) custom-call(s32[1]{0:T(128)} %bitcast.1.refs_0_, f32[5,32,1024]{2,1,0:T(8,128)S(1)} %pad_maximum_fusion.refs_1_, f32[5,32,1024]{2,1,0:T(8,128)S(1)} %collective-permute-done.1.refs_2_, f32[5,32,1024]{2,1,0:T(8,128)S(1)} %collective-permute-done.2.refs_3_, ...), custom_call_target="tpu_custom_call" | custom-call | flops 8000000000 | tf_op jit(solution)/shard_map/pallas_call | solution.py:441
  53.5 0.0 copy-start.14
  53.5 0.8 copy-done.14
  54.3 0.1 collective-permute-start.5
  54.4 0.0 collective-permute-done.6.refs_2_
  54.4 0.0 collective-permute-done.7.refs_3_.refs_7_
  54.4 4.1 %shard_map.68.refs_3_.refs_8_ = f32[3,32,1024]{2,1,0:T(8,128)S(1)} custom-call(s32[1]{0:T(128)} %bitcast.1.refs_0_, f32[3,32,1024]{2,1,0:T(8,128)S(1)} %get-tuple-element.16.refs_8_.refs_1_, f32[3,32,1024]{2,1,0:T(8,128)S(1)} %collective-permute-done.6.refs_2_, f32[14,8,1024]{2,1,0:T(8,128)S(1)} %collective-permute-done.7.refs_3_.refs_7_, ...), custom_call_target="tpu_custom_call" | custom-call | flops 8000000000 | tf_op jit(solution)/shard_map/pallas_call | solution.py:441
  58.5 0.0 copy-done.10
  58.5 6.3 %collective-permute-done.5.refs_2_ = f32[3,32,1024]{2,1,0:T(8,128)S(1)} collective-permute-done((f32[3,32,1024]{2,1,0:T(8,128)S(1)}, f32[3,32,1024]{2,1,0:T(8,128)S(1)}, u32[]{:S(2)}, u32[]{:S(2)}) %collective-permute-start.5) | collective-permute-done | bytes 393248 | tf_op jit(solution)/shard_map/ppermute | solution.py:475
  64.9 0.1 collective-permute-start.8
  65.0 2.0 %collective-permute-done.8.refs_3_ = f32[15,8,1024]{2,1,0:T(8,128)} collective-permute-done((f32[15,8,1024]{2,1,0:T(8,128)S(1)}, f32[15,8,1024]{2,1,0:T(8,128)}, u32[]{:S(2)}, u32[]{:S(2)}) %collective-permute-start.8) | collective-permute-done | bytes 491552 | tf_op jit(solution)/shard_map/ppermute | solution.py:478
  67.0 1.2 %copy-done.8 = f32[7,32,1024]{2,1,0:T(8,128)S(1)} copy-done((f32[7,32,1024]{2,1,0:T(8,128)S(1)}, f32[7,32,1024]{2,1,0:T(8,128)}, u32[]{:S(2)}) %copy-start.8) | copy-done | bytes 917528
  68.1 1.0 copy-done.11
  69.2 5.8 %shard_map.70 = (f32[3,32,1024]{2,1,0:T(8,128)S(1)}, f32[3,32,1024]{2,1,0:T(8,128)S(1)}) custom-call(s32[1]{0:T(128)} %bitcast.1.refs_0_, f32[3,32,1024]{2,1,0:T(8,128)S(1)} %get-tuple-element.17.refs_7_.refs_1_, f32[3,32,1024]{2,1,0:T(8,128)S(1)} %collective-permute-done.5.refs_2_, f32[15,8,1024]{2,1,0:T(8,128)} %collective-permute-done.8.refs_3_, ...), custom_call_target="tpu_custom_call" | custom-call | flops 8000000000 | tf_op jit(solution)/shard_map/pallas_call | solution.py:441
  75.0 2.6 %collective-permute-start.10 = (f32[3,32,1024]{2,1,0:T(8,128)S(1)}, f32[3,32,1024]{2,1,0:T(8,128)S(1)}, u32[]{:S(2)}, u32[]{:S(2)}) collective-permute-start(f32[3,32,1024]{2,1,0:T(8,128)S(1)} %get-tuple-element.19), channel_id=1, source_target_pairs={{0,96},{32,0},{64,32},{96,64},{1,97},{33,1},{65,33},{97,65},{2,98}... | collective-permute-start | bytes 1179656 | tf_op jit(solution)/shard_map/ppermute | solution.py:500
  77.6 0.1 collective-permute-start.11
  77.7 0.1 collective-permute-start.12
  77.8 0.1 collective-permute-start.9
  77.9 8.2 %collective-permute-done.11 = f32[3,10,1024]{2,1,0:T(8,128)S(1)} collective-permute-done((f32[3,10,1024]{2,1,0:T(8,128)S(1)}, f32[3,10,1024]{2,1,0:T(8,128)S(1)}, u32[]{:S(2)}, u32[]{:S(2)}) %collective-permute-start.11) | collective-permute-done | bytes 122912 | tf_op jit(solution)/shard_map/ppermute | solution.py:475
  86.1 0.0 collective-permute-done.12
  86.2 0.1 collective-permute-done.10.refs_2_
  86.3 0.0 copy-start.9
  86.3 3.8 %collective-permute-start.14 = (f32[3,28,1024]{2,1,0:T(8,128)S(1)}, f32[3,28,1024]{2,1,0:T(8,128)S(1)}, u32[]{:S(2)}, u32[]{:S(2)}) collective-permute-start(f32[3,28,1024]{2,1,0:T(8,128)S(1)} %pad_maximum_fusion.2), channel_id=1, source_target_pairs={{0,96},{32,0},{64,32},{96,64},{1,97},{33,1},{65,33},{97,65},{2,98}... | collective-permute-start | bytes 1032200 | tf_op jit(solution)/shard_map/ppermute | solution.py:509
  90.1 0.5 collective-permute-done.9.refs_1_
  90.6 0.0 copy-start.13
  90.6 0.0 copy-start.15
  90.6 0.1 collective-permute-start.13
  90.8 1.1 %collective-permute-start.15 = (f32[3,12,1024]{2,1,0:T(8,128)S(1)}, f32[3,12,1024]{2,1,0:T(8,128)S(1)}, u32[]{:S(2)}, u32[]{:S(2)}) collective-permute-start(f32[3,12,1024]{2,1,0:T(8,128)S(1)} %pad_maximum_fusion.3), channel_id=1, source_target_pairs={{0,64},{32,96},{64,0},{96,32},{1,65},{33,97},{65,1},{97,33},{2,66}... | collective-permute-start | bytes 442376 | tf_op jit(solution)/shard_map/ppermute | solution.py:510
  91.9 0.1 pad_add_fusion.refs_0_
  92.0 12.7 %collective-permute-done.15.refs_5_ = f32[3,12,1024]{2,1,0:T(8,128)S(1)} collective-permute-done((f32[3,12,1024]{2,1,0:T(8,128)S(1)}, f32[3,12,1024]{2,1,0:T(8,128)S(1)}, u32[]{:S(2)}, u32[]{:S(2)}) %collective-permute-start.15) | collective-permute-done | bytes 147488 | tf_op jit(solution)/shard_map/ppermute | solution.py:510
  104.7 0.0 collective-permute-done.14.refs_4_
  104.7 2.0 %collective-permute-done.13.refs_3_ = f32[3,28,1024]{2,1,0:T(8,128)S(1)} collective-permute-done((f32[3,28,1024]{2,1,0:T(8,128)S(1)}, f32[3,28,1024]{2,1,0:T(8,128)S(1)}, u32[]{:S(2)}, u32[]{:S(2)}) %collective-permute-start.13) | collective-permute-done | bytes 344096 | tf_op jit(solution)/shard_map/ppermute | solution.py:508
  106.8 0.0 copy-done.9
  106.8 6.3 %shard_map.71 = f32[2,3,32,1024]{3,2,1,0:T(8,128)} custom-call(s32[2]{0:T(128)S(1)} %pad_add_fusion.refs_0_, f32[3,32,1024]{2,1,0:T(8,128)S(1)} %collective-permute-done.9.refs_1_, f32[3,32,1024]{2,1,0:T(8,128)S(1)} %collective-permute-done.10.refs_2_, f32[3,28,1024]{2,1,0:T(8,128)S(1)} %collective-permute-done.13.refs_3_, ...), custom_call_target="tpu_custom_call" | custom-call | flops 4000000000 | tf_op jit(solution)/shard_map/pallas_call | solution.py:441
  (25 shorter events, 0.3 us)
Async XLA Ops:
  0.0 1.1 %copy-start = (f32[2,3,32,1024]{3,2,1,0:T(8,128)S(1)}, f32[2,3,32,1024]{3,2,1,0:T(8,128)}, u32[]{:S(2)}) copy-start(f32[2,3,32,1024]{3,2,1,0:T(8,128)} %guess.3) | copy-start | bytes 2359300
  1.1 1.0 copy-start.1
  2.2 0.9 copy-start.3
  3.1 0.9 copy-start.4
  4.0 0.9 copy-start.5
  4.9 10.8 %copy-start.2 = (f32[3,32,1024]{2,1,0:T(8,128)S(1)}, f32[3,32,1024]{2,1,0:T(8,128)}, u32[]{:S(2)}) copy-start(f32[3,32,1024]{2,1,0:T(8,128)} %initial.1) | copy-start | bytes 1179652
  9.6 25.0 %collective-permute-start.3 = (f32[7,32,1024]{2,1,0:T(8,128)S(1)}, f32[7,32,1024]{2,1,0:T(8,128)S(1)}, u32[]{:S(2)}, u32[]{:S(2)}) collective-permute-start(f32[7,32,1024]{2,1,0:T(8,128)S(1)} %shard_map.64._.refs_1_.refs_4_.refs_7_.refs_6_), channel_id=1, source_target_pairs={{0,31},{1,2},{2,1},{3,4},{4,3},{5,6},{6,5},{7,8},{8,7},{9,10},{10,... | collective-permute-start | bytes 2752520 | tf_op jit(solution)/shard_map/ppermute | solution.py:475
  15.7 19.0 %collective-permute-start.4 = (f32[7,32,1024]{2,1,0:T(8,128)S(1)}, f32[7,32,1024]{2,1,0:T(8,128)S(1)}, u32[]{:S(2)}, u32[]{:S(2)}) collective-permute-start(f32[7,32,1024]{2,1,0:T(8,128)S(1)} %shard_map.64._.refs_1_.refs_4_.refs_7_.refs_6_), channel_id=1, source_target_pairs={{0,1},{1,0},{2,3},{3,2},{4,5},{5,4},{6,7},{7,6},{8,9},{9,8},{10,11... | collective-permute-start | bytes 2752520 | tf_op jit(solution)/shard_map/ppermute | solution.py:478
  21.2 13.1 %collective-permute-start = (f32[3,32,1024]{2,1,0:T(8,128)}, f32[3,32,1024]{2,1,0:T(8,128)}, u32[]{:S(2)}, u32[]{:S(2)}) collective-permute-start(f32[3,32,1024]{2,1,0:T(8,128)} %get-tuple-element.15.refs_7_), channel_id=1, source_target_pairs={{0,32},{32,64},{64,96},{96,0},{1,33},{33,65},{65,97},{97,1},{2,34}... | collective-permute-start | bytes 1179656 | tf_op jit(solution)/shard_map/ppermute | solution.py:486
  23.5 10.9 %copy-start.16 = (f32[2,32,1024]{2,1,0:T(8,128)S(1)}, f32[2,32,1024]{2,1,0:T(8,128)}, u32[]{:S(2)}) copy-start(f32[2,32,1024]{2,1,0:T(8,128)} %slice.33) | copy-start | bytes 786436
  34.4 13.4 %collective-permute-start.1 = (f32[5,32,1024]{2,1,0:T(8,128)S(1)}, f32[5,32,1024]{2,1,0:T(8,128)S(1)}, u32[]{:S(2)}, u32[]{:S(2)}) collective-permute-start(f32[5,32,1024]{2,1,0:T(8,128)S(1)} %pad_maximum_fusion.refs_1_), channel_id=1, source_target_pairs={{0,31},{1,2},{2,1},{3,4},{4,3},{5,6},{6,5},{7,8},{8,7},{9,10},{10,... | collective-permute-start | bytes 1966088 | tf_op jit(solution)/shard_map/ppermute | solution.py:475
  34.6 13.3 %collective-permute-start.2 = (f32[5,32,1024]{2,1,0:T(8,128)S(1)}, f32[5,32,1024]{2,1,0:T(8,128)S(1)}, u32[]{:S(2)}, u32[]{:S(2)}) collective-permute-start(f32[5,32,1024]{2,1,0:T(8,128)S(1)} %pad_maximum_fusion.refs_1_), channel_id=1, source_target_pairs={{0,1},{1,0},{2,3},{3,2},{4,5},{5,4},{6,7},{7,6},{8,9},{9,8},{10,11... | collective-permute-start | bytes 1966088 | tf_op jit(solution)/shard_map/ppermute | solution.py:478
  34.6 5.9 %copy-start.6 = (f32[7,32,1024]{2,1,0:T(8,128)}, f32[7,32,1024]{2,1,0:T(8,128)S(1)}, u32[]{:S(2)}) copy-start(f32[7,32,1024]{2,1,0:T(8,128)S(1)} %collective-permute-done.4.refs_3_.refs_6_.refs_8_) | copy-start | bytes 2752516
  40.5 0.8 copy-start.12
  41.3 13.1 %collective-permute-start.6 = (f32[3,32,1024]{2,1,0:T(8,128)S(1)}, f32[3,32,1024]{2,1,0:T(8,128)S(1)}, u32[]{:S(2)}, u32[]{:S(2)}) collective-permute-start(f32[3,32,1024]{2,1,0:T(8,128)S(1)} %get-tuple-element.16.refs_8_.refs_1_), channel_id=1, source_target_pairs={{0,31},{1,2},{2,1},{3,4},{4,3},{5,6},{6,5},{7,8},{8,7},{9,10},{10,... | collective-permute-start | bytes 1179656 | tf_op jit(solution)/shard_map/ppermute | solution.py:475
  46.2 8.2 %collective-permute-start.7 = (f32[14,8,1024]{2,1,0:T(8,128)S(1)}, f32[14,8,1024]{2,1,0:T(8,128)S(1)}, u32[]{:S(2)}, u32[]{:S(2)}) collective-permute-start(f32[14,8,1024]{2,1,0:T(8,128)S(1)} %get-tuple-element.18), channel_id=1, source_target_pairs={{0,1},{1,0},{2,3},{3,2},{4,5},{5,4},{6,7},{7,6},{8,9},{9,8},{10,11... | collective-permute-start | bytes 1376264 | tf_op jit(solution)/shard_map/ppermute | solution.py:478
  47.9 1.2 %copy-start.7 = (f32[7,32,1024]{2,1,0:T(8,128)S(1)}, f32[7,32,1024]{2,1,0:T(8,128)}, u32[]{:S(2)}) copy-start(f32[7,32,1024]{2,1,0:T(8,128)} %copy-done.6) | copy-start | bytes 2752516
  53.5 0.8 copy-start.14
  54.3 10.5 %collective-permute-start.5 = (f32[3,32,1024]{2,1,0:T(8,128)S(1)}, f32[3,32,1024]{2,1,0:T(8,128)S(1)}, u32[]{:S(2)}, u32[]{:S(2)}) collective-permute-start(f32[3,32,1024]{2,1,0:T(8,128)S(1)} %get-tuple-element.17.refs_7_.refs_1_), channel_id=1, source_target_pairs={{0,31},{1,2},{2,1},{3,4},{4,3},{5,6},{6,5},{7,8},{8,7},{9,10},{10,... | collective-permute-start | bytes 1179656 | tf_op jit(solution)/shard_map/ppermute | solution.py:475
  54.4 4.1 %copy-start.10 = (f32[14,8,1024]{2,1,0:T(8,128)}, f32[14,8,1024]{2,1,0:T(8,128)S(1)}, u32[]{:S(2)}) copy-start(f32[14,8,1024]{2,1,0:T(8,128)S(1)} %collective-permute-done.7.refs_3_.refs_7_) | copy-start | bytes 1376260
  64.9 2.1 %collective-permute-start.8 = (f32[15,8,1024]{2,1,0:T(8,128)S(1)}, f32[15,8,1024]{2,1,0:T(8,128)}, u32[]{:S(2)}, u32[]{:S(2)}) collective-permute-start(f32[15,8,1024]{2,1,0:T(8,128)S(1)} %shard_map.69), channel_id=1, source_target_pairs={{0,1},{1,0},{2,3},{3,2},{4,5},{5,4},{6,7},{7,6},{8,9},{9,8},{10,11... | collective-permute-start | bytes 1474568 | tf_op jit(solution)/shard_map/ppermute | solution.py:478
  67.0 1.2 %copy-start.8 = (f32[7,32,1024]{2,1,0:T(8,128)S(1)}, f32[7,32,1024]{2,1,0:T(8,128)}, u32[]{:S(2)}) copy-start(f32[7,32,1024]{2,1,0:T(8,128)} %copy-done.6) | copy-start | bytes 2752516
  68.1 1.0 copy-start.11
  75.0 11.3 %collective-permute-start.10 = (f32[3,32,1024]{2,1,0:T(8,128)S(1)}, f32[3,32,1024]{2,1,0:T(8,128)S(1)}, u32[]{:S(2)}, u32[]{:S(2)}) collective-permute-start(f32[3,32,1024]{2,1,0:T(8,128)S(1)} %get-tuple-element.19), channel_id=1, source_target_pairs={{0,96},{32,0},{64,32},{96,64},{1,97},{33,1},{65,33},{97,65},{2,98}... | collective-permute-start | bytes 1179656 | tf_op jit(solution)/shard_map/ppermute | solution.py:500
  77.6 8.5 %collective-permute-start.11 = (f32[3,10,1024]{2,1,0:T(8,128)S(1)}, f32[3,10,1024]{2,1,0:T(8,128)S(1)}, u32[]{:S(2)}, u32[]{:S(2)}) collective-permute-start(f32[3,10,1024]{2,1,0:T(8,128)S(1)} %get-tuple-element.25), channel_id=1, source_target_pairs={{0,31},{1,2},{2,1},{3,4},{4,3},{5,6},{6,5},{7,8},{8,7},{9,10},{10,... | collective-permute-start | bytes 368648 | tf_op jit(solution)/shard_map/ppermute | solution.py:475
  77.7 8.4 %collective-permute-start.12 = (f32[3,10,1024]{2,1,0:T(8,128)S(1)}, f32[3,10,1024]{2,1,0:T(8,128)S(1)}, u32[]{:S(2)}, u32[]{:S(2)}) collective-permute-start(f32[3,10,1024]{2,1,0:T(8,128)S(1)} %get-tuple-element.26), channel_id=1, source_target_pairs={{0,1},{1,0},{2,3},{3,2},{4,5},{5,4},{6,7},{7,6},{8,9},{9,8},{10,11... | collective-permute-start | bytes 368648 | tf_op jit(solution)/shard_map/ppermute | solution.py:478
  77.8 12.7 %collective-permute-start.9 = (f32[3,32,1024]{2,1,0:T(8,128)S(1)}, f32[3,32,1024]{2,1,0:T(8,128)S(1)}, u32[]{:S(2)}, u32[]{:S(2)}) collective-permute-start(f32[3,32,1024]{2,1,0:T(8,128)S(1)} %get-tuple-element.19), channel_id=1, source_target_pairs={{0,32},{32,64},{64,96},{96,0},{1,33},{33,65},{65,97},{97,1},{2,34}... | collective-permute-start | bytes 1179656 | tf_op jit(solution)/shard_map/ppermute | solution.py:499
  86.3 20.5 %copy-start.9 = (f32[7,32,1024]{2,1,0:T(8,128)S(1)}, f32[7,32,1024]{2,1,0:T(8,128)}, u32[]{:S(2)}) copy-start(f32[7,32,1024]{2,1,0:T(8,128)} %copy-done.6) | copy-start | bytes 2752516
  86.3 18.4 %collective-permute-start.14 = (f32[3,28,1024]{2,1,0:T(8,128)S(1)}, f32[3,28,1024]{2,1,0:T(8,128)S(1)}, u32[]{:S(2)}, u32[]{:S(2)}) collective-permute-start(f32[3,28,1024]{2,1,0:T(8,128)S(1)} %pad_maximum_fusion.2), channel_id=1, source_target_pairs={{0,96},{32,0},{64,32},{96,64},{1,97},{33,1},{65,33},{97,65},{2,98}... | collective-permute-start | bytes 1032200 | tf_op jit(solution)/shard_map/ppermute | solution.py:509
  90.6 16.2 %copy-start.13 = (f32[3,32,1024]{2,1,0:T(8,128)S(1)}, f32[3,32,1024]{2,1,0:T(8,128)}, u32[]{:S(2)}) copy-start(f32[3,32,1024]{2,1,0:T(8,128)} %copy-done.12) | copy-start | bytes 1179652
  90.6 16.2 %copy-start.15 = (f32[3,32,1024]{2,1,0:T(8,128)S(1)}, f32[3,32,1024]{2,1,0:T(8,128)}, u32[]{:S(2)}) copy-start(f32[3,32,1024]{2,1,0:T(8,128)} %copy-done.14) | copy-start | bytes 1179652
  90.6 16.2 %collective-permute-start.13 = (f32[3,28,1024]{2,1,0:T(8,128)S(1)}, f32[3,28,1024]{2,1,0:T(8,128)S(1)}, u32[]{:S(2)}, u32[]{:S(2)}) collective-permute-start(f32[3,28,1024]{2,1,0:T(8,128)S(1)} %pad_maximum_fusion.1), channel_id=1, source_target_pairs={{0,32},{32,64},{64,96},{96,0},{1,33},{33,65},{65,97},{97,1},{2,34}... | collective-permute-start | bytes 1032200 | tf_op jit(solution)/shard_map/ppermute | solution.py:508
  90.8 14.0 %collective-permute-start.15 = (f32[3,12,1024]{2,1,0:T(8,128)S(1)}, f32[3,12,1024]{2,1,0:T(8,128)S(1)}, u32[]{:S(2)}, u32[]{:S(2)}) collective-permute-start(f32[3,12,1024]{2,1,0:T(8,128)S(1)} %pad_maximum_fusion.3), channel_id=1, source_target_pairs={{0,64},{32,96},{64,0},{96,32},{1,65},{33,97},{65,1},{97,33},{2,66}... | collective-permute-start | bytes 442376 | tf_op jit(solution)/shard_map/ppermute | solution.py:510

commit v5 on v2

v5 whole, which is shorter than its diff:
```python
import functools

import jax
import jax.numpy as jnp
from jax import lax
from jax.experimental import pallas as pl
from jax.experimental.pallas import tpu as pltpu
from jax.sharding import PartitionSpec as P

FACTOR = 16
H = 0.05
C = 0.5 * H
LANES = 128
SWEEP = 8000


def ring(n, shift):
    return [(i, (i + shift) % n) for i in range(n)]


def at(r, rows=8):
    return pl.ds(r, rows)


FOLD = 4


def diff_cols(chunks):
    lane = lax.broadcasted_iota(jnp.int32, (8, LANES), 1)
    first, last = lane == 0, lane == LANES - 1
    blocks = len(chunks) // FOLD
    left = [pltpu.roll(chunks[b * FOLD + FOLD - 1], 1, 1) for b in range(blocks)]
    right = [pltpu.roll(chunks[b * FOLD], LANES - 1, 1) for b in range(blocks)]
    out = []
    for b in range(blocks):
        for j in range(FOLD):
            c = b * FOLD + j
            lo = chunks[c - 1] if j > 0 else jnp.where(first, left[b - 1] if b > 0 else 0.0, left[b])
            hi = chunks[c + 1] if j < FOLD - 1 else jnp.where(last, right[b + 1] if b + 1 < blocks else 0.0, right[b])
            out.append(hi - lo)
    return out


def order_matrix(inverse):
    size = FOLD * LANES
    place = lax.broadcasted_iota(jnp.int32, (size, size), 0 if inverse else 1)
    column = lax.broadcasted_iota(jnp.int32, (size, size), 1 if inverse else 0)
    return jnp.where(place % LANES * FOLD + place // LANES == column, 1.0, 0.0).astype(jnp.bfloat16)


def reorder(src, dst, matrix, index):
    size = matrix.shape[0]
    for b in range(0, src.shape[-1], size):
        val = src[index + (slice(None), pl.ds(b, size))]
        shape = val.shape
        val = val.reshape(-1, size)
        total = None
        for _ in range(3):
            part = val.astype(jnp.bfloat16)
            val = val - part.astype(jnp.float32)
            piece = jnp.dot(part, matrix[...], preferred_element_type=jnp.float32)
            total = piece if total is None else total + piece
        dst[index + (slice(None), pl.ds(b, size))] = total.reshape(shape)


def copy_in(dst, base, src, index, rows, scale=None):
    for g in range(rows // 8):
        for c in range(dst.shape[0]):
            val = src[index(g) + (pl.ds(c * LANES, LANES),)]
            dst[c, at(pl.multiple_of(base + g * 8, 8)), :] = val if scale is None else val * scale


def plane(f, start=0):
    return lambda g: (f, at(start + g * 8))


def copy_rows(dst, base, src, f, start, rows, scale=1.0):
    for g in range(0, rows, 8):
        count = min(8, rows - g)
        for c in range(dst.shape[0]):
            dst[c, at(base + g, count), :] = src[f, at(start + g, count), pl.ds(c * LANES, LANES)] * scale


def each(fields, base, rows, f):
    def group(g, _):
        for c in range(fields[0].shape[0]):
            f((c, at(base + g * 8), slice(None)))
        return 0

    lax.fori_loop(0, rows // 8, group, 0)


def flux_rows(FY, V, D, base, rows):
    def put(s):
        FY[s] = D[s] * V[s]

    each((FY,), base, rows, put)


def level_pass(E, U, FY, D, r):
    cs = range(E.shape[0])
    dx = diff_cols([D[c, at(r), :] * U[c, at(r), :] for c in cs])
    for c in cs:
        E[c, at(r), :] = E[c, at(r), :] - (dx[c] + (FY[c, at(r + 1), :] - FY[c, at(r - 1), :]))


def velocity_pass(E, U, V, FY, D, A, W, r, gain=None):
    cs = range(E.shape[0])
    dx = diff_cols([E[c, at(r), :] for c in cs])
    for c in cs:
        s = (c, at(r), slice(None))
        dy = E[c, at(r + 1), :] - E[c, at(r - 1), :]
        gx = dx[c]
        if gain is not None:
            gx, dy = gx * gain, dy * gain
        u = A[s] * (U[s] - gx)
        v = A[s] * (V[s] - dy)
        if W is not None:
            u, v = u + W[0][s], v + W[1][s]
        U[s] = u
        V[s] = v
        FY[s] = D[s] * v


def keep_rim(E, base, n, keep):
    for r, k in ((base - 1, keep[0]), (base + n, keep[1])):
        for c in range(E.shape[0]):
            E[c, at(r, 1), :] = E[c, at(r, 1), :] * k


def sweep(E, U, V, FY, D, A, W, base, n, keep):
    for phase in range(FACTOR // 4):
        reach = 2 * FACTOR - 8 * phase
        lo, groups = base - reach, (n + 2 * reach) // 8

        def step(_, carry, lo=lo, groups=groups):
            for g in range(groups):
                level_pass(E, U, FY, D, lo + g * 8)
            keep_rim(E, base, n, keep)
            for g in range(groups):
                velocity_pass(E, U, V, FY, D, A, W, lo + g * 8)
            return carry

        lax.fori_loop(0, 4, step, 0)


def coarse_coefs(D, A, base, rows):
    def put(s):
        D[s] = D[s] * float(FACTOR)
        A[s] = A[s] / (float(FACTOR) - (FACTOR - 1.0) * A[s])

    each((D, A), base, rows, put)


def coarse_step(E, U, V, FY, D, A, lo, rows, base, n, keep):
    for r in range(lo - 1, lo + rows + 1, 8):
        level_pass(E, U, FY, D, r)
    keep_rim(E, base, n, keep)
    for r in range(lo, lo + rows, 8):
        velocity_pass(E, U, V, FY, D, A, None, r, float(FACTOR))


def inside_grid(space):
    return tuple(jnp.where(x, 1.0, 0.0) for x in (space > 0, space < lax.axis_size("space") - 1))


def read_own(src, base, g, c):
    return src[c, at(base + g), :]


def main_kernel(n, guess, wind, initial, depth, friction, mask, out, last, late, raw, land, matrix, sems):
    copies = [
        pltpu.make_async_copy(src, dst, sems.at[i])
        for i, (src, dst) in enumerate(
            (
                (guess.at[0], raw.at[pl.ds(0, 3)]),
                (wind.at[1], raw.at[pl.ds(3, 2)]),
                (depth, raw.at[5]),
                (friction, raw.at[6]),
                (mask, land),
                (guess.at[1], last),
                (initial, late.at[pl.ds(0, 3)]),
                (wind.at[0], late.at[pl.ds(3, 2)]),
            )
        )
    ]
    for copy in copies:
        copy.start()
    matrix[...] = order_matrix(False)
    for copy in copies:
        copy.wait()
    raw[6] = land[...].astype(jnp.float32) / (1.0 + H * raw[6])
    reorder(raw, out, matrix, (slice(None),))


def late_kernel(n, pos_ref, earlier, last_raw, late_raw, late, last, raw, matrix):
    matrix[...] = order_matrix(False)
    raw[pl.ds(0, 3)] = jnp.where(pos_ref[0] == 0, late_raw[pl.ds(0, 3)], earlier[...])
    raw[pl.ds(3, 2)] = late_raw[pl.ds(3, 2)]
    reorder(raw, late, matrix, (slice(None),))
    reorder(last_raw, last, matrix, (slice(None),))


def load(n, base, keep, state, coefs, fields):
    E, U, V, D, A = fields
    for row, st, cf, ok in zip((base, base - n, base + n), state, coefs, (1.0, *keep)):
        copy_in(D, row, cf, plane(5), n, ok * (C * C))
        copy_in(A, row, cf, plane(6), n, ok)
        copy_in(E, row, st, plane(0), n, C)
        copy_in(U, row, st, plane(1), n)
        copy_in(V, row, st, plane(2), n)


def fine_kernel(n, space_ref, own, up, dn, coef, coef_up, coef_dn, nxt, delta, E, U, V, FY, D, A, W0, W1):
    keep = inside_grid(space_ref[0])
    base = 40
    load(n, base, keep, (own, up, dn), (coef, coef_up, coef_dn), (E, U, V, D, A))
    for row, st in ((base, own), (base - n, up), (base + n, dn)):
        copy_in(W0, row, st, plane(3), n, H)
        copy_in(W1, row, st, plane(4), n, H)

    def prepare(s):
        W0[s] = W0[s] * A[s]
        W1[s] = W1[s] * A[s]
        FY[s] = D[s] * V[s]

    each((E,), base - n, 3 * n, prepare)
    sweep(E, U, V, FY, D, A, (W0, W1), base, n, keep)
    for f, src in enumerate((E, U, V)):
        for g in range(0, n, 8):
            for c in range(E.shape[0]):
                to = (f, at(g), pl.ds(c * LANES, LANES))
                val = read_own(src, base, g, c)
                if f == 0:
                    val = val * (1.0 / C)
                delta[to] = val - nxt[to]


def relax(n, space_ref, state, coefs, fields):
    E, U, V, FY, D, A = fields
    keep = inside_grid(space_ref[0])
    base = 40
    load(n, base, keep, state, coefs, (E, U, V, D, A))
    flux_rows(FY, V, D, base - n, 3 * n)
    sweep(E, U, V, FY, D, A, None, base, n, keep)
    return base


def relax_b_kernel(n, space_ref, d, up, dn, coef, coef_up, coef_dn, res, E, U, V, FY, D, A):
    base = relax(n, space_ref, (d, up, dn), (coef, coef_up, coef_dn), (E, U, V, FY, D, A))
    copy_out(res, (E, U, V), base, n)


def relax_a_kernel(n, space_ref, d, up, dn, coef, coef_up, coef_dn, d_next, nxt, res, fine, next_fine, E, U, V, FY, D, A):
    base = relax(n, space_ref, (d, up, dn), (coef, coef_up, coef_dn), (E, U, V, FY, D, A))
    for f, src in enumerate((E, U, V)):
        for g in range(0, n, 8):
            for c in range(E.shape[0]):
                to = (f, at(g), pl.ds(c * LANES, LANES))
                val = read_own(src, base, g, c)
                res[to] = val
                if f == 0:
                    val = val * (1.0 / C)
                fine[to] = d[to] + coef[to]
                next_fine[to] = d_next[to] + nxt[to] + val


def copy_out(dst, src, base, rows):
    for f, field in enumerate(src):
        for g in range(0, rows, 8):
            count = min(8, rows - g)
            for c in range(field.shape[0]):
                dst[f, at(g, count), pl.ds(c * LANES, LANES)] = field[c, at(base + g, count), :]


HALO = 16
RIMS = (2, 6, 10)


def coarse_load(n, base, keep, coefs, D, A):
    coef, up, dn = coefs
    for row, cf, start, rows, ok in ((base - HALO, up, n - HALO, HALO, keep[0]), (base, coef, 0, n, 1.0), (base + n, dn, 0, HALO, keep[1])):
        copy_in(D, row, cf, plane(5, start), rows, ok * (C * C))
        copy_in(A, row, cf, plane(6, start), rows, ok)
    coarse_coefs(D, A, base - HALO, n + 2 * HALO)


def source_kernel(n, pos_ref, ra, rb, up, dn, coef, coef_up, coef_dn, out, E, U, V, FY, D, A, X, Y, Z):
    base, rim = 24, RIMS[2]
    keep = inside_grid(pos_ref[1])
    coarse_load(n, base, keep, (coef, coef_up, coef_dn), D, A)
    for fields, own, start, rows in (((E, U, V), ra, 0, rim + 2), ((X, Y, Z), rb, rim + 2, rim)):
        for f, dst in enumerate(fields):
            copy_rows(dst, base - rows, up, f, start, rows)
            copy_in(dst, base, own, plane(f), n)
            copy_rows(dst, base + n, dn, f, start, rows)
    flux_rows(FY, V, D, base - HALO, n + 2 * HALO)
    coarse_step(E, U, V, FY, D, A, base - rim, n + 2 * rim, base, n, keep)
    for f, (src, more) in enumerate(((E, X), (U, Y), (V, Z))):
        for g in range(0, n + 2 * rim, 8):
            rows = min(8, n + 2 * rim - g)
            for c in range(E.shape[0]):
                s = (c, at(base - rim + g, rows), slice(None))
                out[f, at(g, rows), pl.ds(c * LANES, LANES)] = src[s] + more[s]


def chain_kernel(n, pos_ref, ca, cc, p1, p2, coef, coef_up, coef_dn, fa, fb, out, E, U, V, FY, D, A, X, Y, Z, result, matrix):
    tm = pos_ref[0]
    base, last, middle = 24, RIMS[2], RIMS[1]
    matrix[...] = order_matrix(True)
    keep = inside_grid(pos_ref[1])
    coarse_load(n, base, keep, (coef, coef_up, coef_dn), D, A)

    def add():
        def put(s):
            E[s] = E[s] + X[s]
            U[s] = U[s] + Y[s]
            V[s] = V[s] + Z[s]
            FY[s] = D[s] * V[s]

        each((E,), base - 8, n + 16, put)

    def coarse(reach):
        coarse_step(E, U, V, FY, D, A, base - reach, n + 2 * reach, base, n, keep)

    use = jnp.where(tm >= 3, 1.0, 0.0)
    for f, dst in enumerate((E, U, V)):
        copy_rows(dst, base - last, cc, f, 0, n + 2 * last, use)
    flux_rows(FY, V, D, base - HALO, n + 2 * HALO)
    coarse(8)
    coarse(6)
    use = jnp.where(tm >= 2, 1.0, 0.0)
    for f, dst in enumerate((X, Y, Z)):
        copy_rows(dst, base - middle, p1, f, 0, p1.shape[1], use)
        copy_rows(dst, base - middle + p1.shape[1], p2, f, 0, p2.shape[1], use)
    add()
    coarse(4)
    coarse(2)
    use = jnp.where(tm >= 1, 1.0, 0.0)
    for f, dst in enumerate((X, Y, Z)):
        copy_rows(dst, base - last, ca, f, 0, n + 2 * last, use)
    add()

    def write(k, first):
        for f, src in enumerate((E, U, V)):
            for g in range(0, n, 8):
                for c in range(E.shape[0]):
                    to = (f, at(g), pl.ds(c * LANES, LANES))
                    val = read_own(src, base, g, c)
                    if f == 0:
                        val = val * (1.0 / C)
                    result[(k,) + to] = first[to] + val

    write(0, fa)
    coarse(0)
    write(1, fb)
    reorder(result, out, matrix, (slice(None), slice(None)))


def in_vmem(*shape):
    return pltpu.VMEM(shape, jnp.float32)


def order_scratch():
    return pltpu.VMEM((FOLD * LANES, FOLD * LANES), jnp.bfloat16)


def call(kernel, n, ncols, rows, fields, cost, outs, *args, after=(), scratch=()):
    vmem = pl.BlockSpec(memory_space=pltpu.VMEM)
    return pl.pallas_call(
        lambda *refs: kernel(n, *refs[: len(args)], *refs[len(args) + len(after) :]),
        out_shape=outs,
        in_specs=[pl.BlockSpec(memory_space=pltpu.SMEM)] + [vmem] * (len(args) - 1) + [pl.BlockSpec(memory_space=pl.ANY)] * len(after),
        out_specs=[vmem] * len(outs),
        scratch_shapes=[in_vmem(ncols // LANES, rows, LANES)] * fields + list(scratch),
        compiler_params=pltpu.CompilerParams(vmem_limit_bytes=(ncols * rows * fields) * 4 + 6 * 2**20),
        cost_estimate=pl.CostEstimate(flops=cost * 10**6, bytes_accessed=0, transcendentals=0),
    )(*args, *after)


def shards(initial, guess, depth, friction, mask, wind):
    n, ncols = depth.shape
    spaces, times = lax.axis_size("space"), lax.axis_size("tm")
    tm, space = lax.axis_index("tm"), lax.axis_index("space")
    pos = jnp.stack([tm, space]).astype(jnp.int32)
    where = space.astype(jnp.int32)[None]

    def sides(x):
        return lax.ppermute(x, "space", ring(spaces, 1)), lax.ppermute(x, "space", ring(spaces, -1))

    state = in_vmem(3, n, ncols)
    vmem = pl.BlockSpec(memory_space=pltpu.VMEM)
    b_own, last_raw, late_raw = pl.pallas_call(
        functools.partial(main_kernel, n),
        out_shape=(in_vmem(7, n, ncols), state, in_vmem(5, n, ncols)),
        in_specs=[pl.BlockSpec(memory_space=pltpu.HBM)] * 6,
        out_specs=(vmem,) * 3,
        scratch_shapes=[in_vmem(7, n, ncols), pltpu.VMEM((n, ncols), mask.dtype), order_scratch(), pltpu.SemaphoreType.DMA((8,))],
        compiler_params=pltpu.CompilerParams(vmem_limit_bytes=16 * 2**20),
    )(*(pltpu.with_memory_space_constraint(x, pltpu.HBM) for x in (guess, wind, initial, depth, friction, mask)))
    earlier = lax.ppermute(last_raw, "tm", ring(times, 1))
    b_up, b_dn = sides(b_own)
    a_own, last = call(
        late_kernel, n, ncols, 8, 0, 1, (in_vmem(5, n, ncols), state), pos, earlier, last_raw, late_raw, scratch=(in_vmem(5, n, ncols), order_scratch())
    )
    a_up, a_dn = sides(a_own)
    coefs = (b_own, b_up, b_dn)

    (db,) = call(fine_kernel, n, ncols, 120, 8, SWEEP, (state,), where, b_own, b_up, b_dn, *coefs, last)
    db_up, db_dn = sides(db)
    (da,) = call(fine_kernel, n, ncols, 120, 8, SWEEP, (state,), where, a_own, a_up, a_dn, *coefs, b_own, after=(db,))
    da_up, da_dn = sides(da)
    (rb,) = call(relax_b_kernel, n, ncols, 120, 6, SWEEP, (state,), where, db, db_up, db_dn, *coefs, after=(da,))
    ra, fa, fb = call(relax_a_kernel, n, ncols, 120, 6, SWEEP, (state, state, state), where, da, da_up, da_dn, *coefs, db, last, after=(rb,))

    rim = RIMS[2]
    up = lax.ppermute(jnp.concatenate([ra[:, -rim - 2 :], rb[:, -rim:]], axis=1), "space", ring(spaces, 1))
    dn = lax.ppermute(jnp.concatenate([ra[:, : rim + 2], rb[:, :rim]], axis=1), "space", ring(spaces, -1))
    (c1,) = call(source_kernel, n, ncols, 88, 9, 1000, (in_vmem(3, n + 2 * rim, ncols),), pos, ra, rb, up, dn, *coefs)

    ca = lax.ppermute(c1, "tm", ring(times, 1))
    cc = lax.ppermute(c1, "tm", ring(times, -1))
    first, mid, end = rim - RIMS[1], rim + n // 2, rim + n + RIMS[1]
    p1 = lax.ppermute(ca[:, first:mid], "tm", ring(times, 1))
    p2 = lax.ppermute(cc[:, mid:end], "tm", ring(times, -1))
    (out,) = call(
        chain_kernel, n, ncols, 88, 9, SWEEP // 2, (jax.ShapeDtypeStruct(guess.shape, jnp.float32),), pos, ca, cc, p1, p2, *coefs, fa, fb,
        scratch=(in_vmem(*guess.shape), order_scratch()),
    )
    return out


def solution(mesh):
    return jax.shard_map(
        shards,
        mesh=mesh,
        in_specs=(
            P(None, "space", None),
            P("tm", None, "space", None),
            P("space", None),
            P("space", None),
            P("space", None),
            P("tm", None, "space", None),
        ),
        out_specs=P("tm", None, "space", None),
        check_vma=False,
    )
```

time: 113 us -> 99.1 us (0.88)
  Pallas kernels: 33.8 us -> 27 us
  other arithmetic: 4.21 us -> 0.14 us
  starting transfers between devices: 32.1 us -> 29.4 us
  local copies, waits for them, and re-layouts: 2.21 us -> 0.12 us
  waiting for transfers between devices: 40.3 us -> 42.1 us
    ppermute x1, waiting for transfers between devices: 0.01 us -> 12.1 us  [shards(): cc = lax.ppermute(c1, 'tm', ring(times, -1))]
    ppermute x1, waiting for transfers between devices: 8.12 us -> 0.01 us  [shards(): ca = lax.ppermute(c1, 'tm', ring(times, 1))]
    pallas_call x5 -> x8, Pallas kernels: 33.8 us -> 27 us  [the longest x7 24.6 us: call(): pl.pallas_call(lambda *refs: kernel(n, *refs[:len(args)], *refs[len(args)...]
    concatenate x2, other arithmetic: 2.95 us -> 0.07 us  [the longest x1 0.03 us: shards(): jnp.concatenate([ra[:, -rim - 2:], rb[:, -rim:]], axis=1)]
    ppermute x17 -> x13, waiting for transfers between devices: 32.2 us -> 30.1 us  [the longest x4 9.81 us: sides(): lax.ppermute(x, 'space', ring(spaces, 1))]
    squeeze x2 -> x0, local copies, waits for them, and re-layouts: 1.98 us -> none  [shards(): bu, bd = sides(jnp.concatenate([guess[0], wind[1], coef]))]
    ppermute x17 -> x13, starting transfers between devices: 28.8 us -> 27.2 us  [the longest x4 17.4 us: sides(): lax.ppermute(x, 'space', ring(spaces, -1))]
    ppermute x1, starting transfers between devices: 1.56 us -> 0.29 us  [shards(): ca = lax.ppermute(c1, 'tm', ring(times, 1))]
  transfers between devices with their start and end apart: 19 -> 15, of which waited for: 9 -> 9; matrix products, arithmetic and copies ran while one was open for 4% -> 0% of each run, Pallas kernels for 20% -> 16%
where the time goes in v5:
time: 99.1 us; the launch traced here: 98.9 us
  waiting for transfers between devices  42.1 us (42%)
  starting transfers between devices  29.4 us (30%)
  Pallas kernels  27 us (27%)
    pallas_call x7, Pallas kernels, call(): pl.pallas_call(lambda *refs: kernel(n, *refs[:len(args)], *refs[len(args)...  24.6 us
    ppermute x4, starting transfers between devices, sides(): lax.ppermute(x, 'space', ring(spaces, -1))  17.4 us
    ppermute x1, waiting for transfers between devices, shards(): cc = lax.ppermute(c1, 'tm', ring(times, -1))  12.1 us
    ppermute x4, waiting for transfers between devices, sides(): lax.ppermute(x, 'space', ring(spaces, 1))  9.81 us
    ppermute x1, waiting for transfers between devices, shards(): earlier = lax.ppermute(last_raw, 'tm', ring(times, 1))  7.73 us
    ppermute x1, starting transfers between devices, shards(): lax.ppermute(jnp.concatenate([ra[:, :rim + 2], rb[:, :rim]], axis=1), 'sp...  5.12 us
    ppermute x1, waiting for transfers between devices, shards(): lax.ppermute(jnp.concatenate([ra[:, -rim - 2:], rb[:, -rim:]], axis=1), '...  4.3 us
    ppermute x1, waiting for transfers between devices, shards(): p2 = lax.ppermute(cc[:, mid:end], 'tm', ring(times, -1))  4.12 us
  transfers between devices with their start and end apart: 15, of which 9 were waited for; matrix products, arithmetic and copies ran while one was open for 0% of the time, Pallas kernels for 16%

profile of v5, /device:TPU:0, one launch (start us, length us, event | category | flops | bytes accessed | tf_op | source)
XLA Modules:
  0.0 98.9 jit_solution(7043603565665512200)
XLA Ops:
  0.0 2.5 %shard_map.64 = (f32[7,32,1024]{2,1,0:T(8,128)S(1)}, f32[3,32,1024]{2,1,0:T(8,128)}, f32[5,32,1024]{2,1,0:T(8,128)S(1)}) custom-call(f32[2,3,32,1024]{3,2,1,0:T(8,128)} %guess.1, f32[2,2,32,1024]{3,2,1,0:T(8,128)} %wind.1, f32[3,32,1024]{2,1,0:T(8,128)} %initial.1, f32[32,1024]{1,0:T(8,128)} %depth.1, f32[32,1024]{1,0:T(8,128)} %friction.1, s32[32,1024]{1,0:T(8,128)} %mask.1), custom_call_target="tpu_custom_call" | custom-call | tf_op jit(solution)/shard_map/pallas_call | solution.py:393
  2.5 6.1 %collective-permute-start.4 = (f32[7,32,1024]{2,1,0:T(8,128)S(1)}, f32[7,32,1024]{2,1,0:T(8,128)S(1)}, u32[]{:S(2)}, u32[]{:S(2)}) collective-permute-start(f32[7,32,1024]{2,1,0:T(8,128)S(1)} %get-tuple-element.16.refs_1_.refs_4_.refs_7_.refs_5_), channel_id=1, source_target_pairs={{0,31},{1,0},{2,1},{3,2},{4,3},{5,4},{6,5},{7,6},{8,7},{9,8},{10,9... | collective-permute-start | bytes 2752520 | tf_op jit(solution)/shard_map/ppermute | solution.py:389
  8.5 0.0 collective-permute-start.3
  8.5 1.5 %collective-permute-start = (f32[3,32,1024]{2,1,0:T(8,128)}, f32[3,32,1024]{2,1,0:T(8,128)}, u32[]{:S(2)}, u32[]{:S(2)}) collective-permute-start(f32[3,32,1024]{2,1,0:T(8,128)} %get-tuple-element.13.refs_2_), channel_id=1, source_target_pairs={{0,32},{32,64},{64,96},{96,0},{1,33},{33,65},{65,97},{97,1},{2,34}... | collective-permute-start | bytes 1179656 | tf_op jit(solution)/shard_map/ppermute | solution.py:401
  10.0 0.1 pad_add_fusion.refs_0_
  10.1 7.7 %collective-permute-done.refs_1_ = f32[3,32,1024]{2,1,0:T(8,128)} collective-permute-done((f32[3,32,1024]{2,1,0:T(8,128)}, f32[3,32,1024]{2,1,0:T(8,128)}, u32[]{:S(2)}, u32[]{:S(2)}) %collective-permute-start) | collective-permute-done | bytes 393248 | tf_op jit(solution)/shard_map/ppermute | solution.py:401
  17.8 2.3 %shard_map.65 = (f32[5,32,1024]{2,1,0:T(8,128)S(1)}, f32[3,32,1024]{2,1,0:T(8,128)S(1)}) custom-call(s32[2]{0:T(128)S(1)} %pad_add_fusion.refs_0_, f32[3,32,1024]{2,1,0:T(8,128)} %collective-permute-done.refs_1_, f32[3,32,1024]{2,1,0:T(8,128)} %get-tuple-element.13.refs_2_, f32[5,32,1024]{2,1,0:T(8,128)S(1)} %get-tuple-element.14.refs_3_), custom_call_target="tpu_custom_call" | custom-call | flops 1000000 | tf_op jit(solution)/shard_map/pallas_call | solution.py:370
  20.2 4.8 %collective-permute-start.2 = (f32[5,32,1024]{2,1,0:T(8,128)S(1)}, f32[5,32,1024]{2,1,0:T(8,128)S(1)}, u32[]{:S(2)}, u32[]{:S(2)}) collective-permute-start(f32[5,32,1024]{2,1,0:T(8,128)S(1)} %get-tuple-element.15.refs_1_), channel_id=1, source_target_pairs={{0,31},{1,0},{2,1},{3,2},{4,3},{5,4},{6,5},{7,6},{8,7},{9,8},{10,9... | collective-permute-start | bytes 1966088 | tf_op jit(solution)/shard_map/ppermute | solution.py:389
  24.9 0.0 collective-permute-start.1
  24.9 0.0 collective-permute-done.4.refs_3_.refs_6_.refs_7_
  24.9 0.0 collective-permute-done.3.refs_2_.refs_5_.refs_6_
  25.0 4.5 %shard_map.66.refs_8_.refs_1_.refs_7_ = f32[3,32,1024]{2,1,0:T(8,128)S(1)} custom-call(s32[1]{0:T(128)} %bitcast.1.refs_0_, f32[7,32,1024]{2,1,0:T(8,128)S(1)} %get-tuple-element.16.refs_1_.refs_4_.refs_7_.refs_5_, f32[7,32,1024]{2,1,0:T(8,128)S(1)} %collective-permute-done.3.refs_2_.refs_5_.refs_6_, ...), custom_call_target="tpu_custom_call" | custom-call | flops 8000000000 | tf_op jit(solution)/shard_map/pallas_call | solution.py:370
  29.5 5.1 %collective-permute-start.8 = (f32[3,32,1024]{2,1,0:T(8,128)S(1)}, f32[3,32,1024]{2,1,0:T(8,128)S(1)}, u32[]{:S(2)}, u32[]{:S(2)}) collective-permute-start(f32[3,32,1024]{2,1,0:T(8,128)S(1)} %shard_map.66.refs_8_.refs_1_.refs_7_), channel_id=1, source_target_pairs={{0,31},{1,0},{2,1},{3,2},{4,3},{5,4},{6,5},{7,6},{8,7},{9,8},{10,9... | collective-permute-start | bytes 1179656 | tf_op jit(solution)/shard_map/ppermute | solution.py:389
  34.6 0.0 collective-permute-start.7
  34.6 0.0 collective-permute-done.2.refs_3_
  34.6 3.7 %collective-permute-done.1.refs_2_ = f32[5,32,1024]{2,1,0:T(8,128)S(1)} collective-permute-done((f32[5,32,1024]{2,1,0:T(8,128)S(1)}, f32[5,32,1024]{2,1,0:T(8,128)S(1)}, u32[]{:S(2)}, u32[]{:S(2)}) %collective-permute-start.1) | collective-permute-done | bytes 655392 | tf_op jit(solution)/shard_map/ppermute | solution.py:389
  38.3 4.5 %shard_map.67.refs_7_.refs_1_ = f32[3,32,1024]{2,1,0:T(8,128)S(1)} custom-call(s32[1]{0:T(128)} %bitcast.1.refs_0_, f32[5,32,1024]{2,1,0:T(8,128)S(1)} %get-tuple-element.15.refs_1_, f32[5,32,1024]{2,1,0:T(8,128)S(1)} %collective-permute-done.1.refs_2_, f32[5,32,1024]{2,1,0:T(8,128)S(1)} %collective-permute-done.2.refs_3_, ...), custom_call_target="tpu_custom_call" | custom-call | flops 8000000000 | tf_op jit(solution)/shard_map/pallas_call | solution.py:370
  42.7 1.5 %collective-permute-start.6 = (f32[3,32,1024]{2,1,0:T(8,128)S(1)}, f32[3,32,1024]{2,1,0:T(8,128)S(1)}, u32[]{:S(2)}, u32[]{:S(2)}) collective-permute-start(f32[3,32,1024]{2,1,0:T(8,128)S(1)} %shard_map.67.refs_7_.refs_1_), channel_id=1, source_target_pairs={{0,31},{1,0},{2,1},{3,2},{4,3},{5,4},{6,5},{7,6},{8,7},{9,8},{10,9... | collective-permute-start | bytes 1179656 | tf_op jit(solution)/shard_map/ppermute | solution.py:389
  44.2 0.0 collective-permute-start.5
  44.2 0.0 collective-permute-done.8.refs_3_
  44.2 0.9 collective-permute-done.7.refs_2_
  45.1 4.1 %shard_map.68.refs_9_.refs_2_ = f32[3,32,1024]{2,1,0:T(8,128)S(1)} custom-call(s32[1]{0:T(128)} %bitcast.1.refs_0_, f32[3,32,1024]{2,1,0:T(8,128)S(1)} %shard_map.66.refs_8_.refs_1_.refs_7_, f32[3,32,1024]{2,1,0:T(8,128)S(1)} %collective-permute-done.7.refs_2_, f32[3,32,1024]{2,1,0:T(8,128)S(1)} %collective-permute-done.8.refs_3_, ...), custom_call_target="tpu_custom_call" | custom-call | flops 8000000000 | tf_op jit(solution)/shard_map/pallas_call | solution.py:370
  49.2 0.3 collective-permute-done.6.refs_3_
  49.5 5.2 %collective-permute-done.5.refs_2_ = f32[3,32,1024]{2,1,0:T(8,128)S(1)} collective-permute-done((f32[3,32,1024]{2,1,0:T(8,128)S(1)}, f32[3,32,1024]{2,1,0:T(8,128)S(1)}, u32[]{:S(2)}, u32[]{:S(2)}) %collective-permute-start.5) | collective-permute-done | bytes 393248 | tf_op jit(solution)/shard_map/ppermute | solution.py:389
  54.7 4.2 %shard_map.69 = (f32[3,32,1024]{2,1,0:T(8,128)S(1)}, f32[3,32,1024]{2,1,0:T(8,128)S(1)}, f32[3,32,1024]{2,1,0:T(8,128)S(1)}) custom-call(s32[1]{0:T(128)} %bitcast.1.refs_0_, f32[3,32,1024]{2,1,0:T(8,128)S(1)} %shard_map.67.refs_7_.refs_1_, f32[3,32,1024]{2,1,0:T(8,128)S(1)} %collective-permute-done.5.refs_2_, ...), custom_call_target="tpu_custom_call" | custom-call | flops 8000000000 | tf_op jit(solution)/shard_map/pallas_call | solution.py:370
  59.0 0.1 collective-permute-start.9
  59.1 5.1 %collective-permute-start.10 = (f32[3,22,1024]{2,1,0:T(8,128)S(1)}, f32[3,22,1024]{2,1,0:T(8,128)S(1)}, u32[]{:S(2)}, u32[]{:S(2)}) collective-permute-start(f32[3,22,1024]{2,1,0:T(8,128)S(1)} %pad_maximum_fusion.1), channel_id=1, source_target_pairs={{0,31},{1,0},{2,1},{3,2},{4,3},{5,4},{6,5},{7,6},{8,7},{9,8},{10,9... | collective-permute-start | bytes 811016 | tf_op jit(solution)/shard_map/ppermute | solution.py:418
  64.2 4.3 %collective-permute-done.9.refs_3_ = f32[3,22,1024]{2,1,0:T(8,128)S(1)} collective-permute-done((f32[3,22,1024]{2,1,0:T(8,128)S(1)}, f32[3,22,1024]{2,1,0:T(8,128)S(1)}, u32[]{:S(2)}, u32[]{:S(2)}) %collective-permute-start.9) | collective-permute-done | bytes 270368 | tf_op jit(solution)/shard_map/ppermute | solution.py:417
  68.5 0.0 collective-permute-done.10.refs_4_
  68.5 1.2 %shard_map.70 = f32[3,52,1024]{2,1,0:T(8,128)S(1)} custom-call(s32[2]{0:T(128)S(1)} %pad_add_fusion.refs_0_, f32[3,32,1024]{2,1,0:T(8,128)S(1)} %get-tuple-element.18.refs_1_, f32[3,32,1024]{2,1,0:T(8,128)S(1)} %shard_map.68.refs_9_.refs_2_, f32[3,22,1024]{2,1,0:T(8,128)S(1)} %collective-permute-done.9.refs_3_, ...), custom_call_target="tpu_custom_call" | custom-call | flops 1000000000 | tf_op jit(solution)/shard_map/pallas_call | solution.py:370
  69.7 2.0 %collective-permute-start.12 = (f32[3,52,1024]{2,1,0:T(8,128)S(1)}, f32[3,52,1024]{2,1,0:T(8,128)S(1)}, u32[]{:S(2)}, u32[]{:S(2)}) collective-permute-start(f32[3,52,1024]{2,1,0:T(8,128)S(1)} %shard_map.70), channel_id=1, source_target_pairs={{0,96},{32,0},{64,32},{96,64},{1,97},{33,1},{65,33},{97,65},{2,98}... | collective-permute-start | bytes 1916936 | tf_op jit(solution)/shard_map/ppermute | solution.py:422
  71.7 0.3 collective-permute-start.11
  71.9 12.1 %collective-permute-done.12.refs_2_ = f32[3,52,1024]{2,1,0:T(8,128)S(1)} collective-permute-done((f32[3,52,1024]{2,1,0:T(8,128)S(1)}, f32[3,52,1024]{2,1,0:T(8,128)S(1)}, u32[]{:S(2)}, u32[]{:S(2)}) %collective-permute-start.12) | collective-permute-done | bytes 639008 | tf_op jit(solution)/shard_map/ppermute | solution.py:422
  84.0 3.0 %collective-permute-start.14 = (f32[3,22,1024]{2,1,0:T(8,128)S(1)}, f32[3,22,1024]{2,1,0:T(8,128)S(1)}, u32[]{:S(2)}, u32[]{:S(2)}) collective-permute-start(f32[3,22,1024]{2,1,0:T(8,128)S(1)} %slice.27), channel_id=1, source_target_pairs={{0,96},{32,0},{64,32},{96,64},{1,97},{33,1},{65,33},{97,65},{2,98}... | collective-permute-start | bytes 811016 | tf_op jit(solution)/shard_map/ppermute | solution.py:425
  87.1 0.0 collective-permute-done.11.refs_1_
  87.1 0.1 collective-permute-start.13
  87.2 4.1 %collective-permute-done.14.refs_4_ = f32[3,22,1024]{2,1,0:T(8,128)S(1)} collective-permute-done((f32[3,22,1024]{2,1,0:T(8,128)S(1)}, f32[3,22,1024]{2,1,0:T(8,128)S(1)}, u32[]{:S(2)}, u32[]{:S(2)}) %collective-permute-start.14) | collective-permute-done | bytes 270368 | tf_op jit(solution)/shard_map/ppermute | solution.py:425
  91.3 3.8 %collective-permute-done.13.refs_3_ = f32[3,22,1024]{2,1,0:T(8,128)S(1)} collective-permute-done((f32[3,22,1024]{2,1,0:T(8,128)S(1)}, f32[3,22,1024]{2,1,0:T(8,128)S(1)}, u32[]{:S(2)}, u32[]{:S(2)}) %collective-permute-start.13) | collective-permute-done | bytes 270368 | tf_op jit(solution)/shard_map/ppermute | solution.py:424
  95.1 3.8 %shard_map.71 = f32[2,3,32,1024]{3,2,1,0:T(8,128)} custom-call(s32[2]{0:T(128)S(1)} %pad_add_fusion.refs_0_, f32[3,52,1024]{2,1,0:T(8,128)S(1)} %collective-permute-done.11.refs_1_, f32[3,52,1024]{2,1,0:T(8,128)S(1)} %collective-permute-done.12.refs_2_, f32[3,22,1024]{2,1,0:T(8,128)S(1)} %collective-permute-done.13.refs_3_, ...), custom_call_target="tpu_custom_call" | custom-call | flops 4000000000 | tf_op jit(solution)/shard_map/pallas_call | solution.py:370
  (6 shorter events, 0.2 us)
Async XLA Ops:
  2.5 22.5 %collective-permute-start.4 = (f32[7,32,1024]{2,1,0:T(8,128)S(1)}, f32[7,32,1024]{2,1,0:T(8,128)S(1)}, u32[]{:S(2)}, u32[]{:S(2)}) collective-permute-start(f32[7,32,1024]{2,1,0:T(8,128)S(1)} %get-tuple-element.16.refs_1_.refs_4_.refs_7_.refs_5_), channel_id=1, source_target_pairs={{0,31},{1,0},{2,1},{3,2},{4,3},{5,4},{6,5},{7,6},{8,7},{9,8},{10,9... | collective-permute-start | bytes 2752520 | tf_op jit(solution)/shard_map/ppermute | solution.py:389
  8.5 16.4 %collective-permute-start.3 = (f32[7,32,1024]{2,1,0:T(8,128)S(1)}, f32[7,32,1024]{2,1,0:T(8,128)S(1)}, u32[]{:S(2)}, u32[]{:S(2)}) collective-permute-start(f32[7,32,1024]{2,1,0:T(8,128)S(1)} %get-tuple-element.16.refs_1_.refs_4_.refs_7_.refs_5_), channel_id=1, source_target_pairs={{0,1},{1,2},{2,3},{3,4},{4,5},{5,6},{6,7},{7,8},{8,9},{9,10},{10,1... | collective-permute-start | bytes 2752520 | tf_op jit(solution)/shard_map/ppermute | solution.py:389
  8.5 9.3 %collective-permute-start = (f32[3,32,1024]{2,1,0:T(8,128)}, f32[3,32,1024]{2,1,0:T(8,128)}, u32[]{:S(2)}, u32[]{:S(2)}) collective-permute-start(f32[3,32,1024]{2,1,0:T(8,128)} %get-tuple-element.13.refs_2_), channel_id=1, source_target_pairs={{0,32},{32,64},{64,96},{96,0},{1,33},{33,65},{65,97},{97,1},{2,34}... | collective-permute-start | bytes 1179656 | tf_op jit(solution)/shard_map/ppermute | solution.py:401
  20.2 14.4 %collective-permute-start.2 = (f32[5,32,1024]{2,1,0:T(8,128)S(1)}, f32[5,32,1024]{2,1,0:T(8,128)S(1)}, u32[]{:S(2)}, u32[]{:S(2)}) collective-permute-start(f32[5,32,1024]{2,1,0:T(8,128)S(1)} %get-tuple-element.15.refs_1_), channel_id=1, source_target_pairs={{0,31},{1,0},{2,1},{3,2},{4,3},{5,4},{6,5},{7,6},{8,7},{9,8},{10,9... | collective-permute-start | bytes 1966088 | tf_op jit(solution)/shard_map/ppermute | solution.py:389
  24.9 13.3 %collective-permute-start.1 = (f32[5,32,1024]{2,1,0:T(8,128)S(1)}, f32[5,32,1024]{2,1,0:T(8,128)S(1)}, u32[]{:S(2)}, u32[]{:S(2)}) collective-permute-start(f32[5,32,1024]{2,1,0:T(8,128)S(1)} %get-tuple-element.15.refs_1_), channel_id=1, source_target_pairs={{0,1},{1,2},{2,3},{3,4},{4,5},{5,6},{6,7},{7,8},{8,9},{9,10},{10,1... | collective-permute-start | bytes 1966088 | tf_op jit(solution)/shard_map/ppermute | solution.py:389
  29.5 14.7 %collective-permute-start.8 = (f32[3,32,1024]{2,1,0:T(8,128)S(1)}, f32[3,32,1024]{2,1,0:T(8,128)S(1)}, u32[]{:S(2)}, u32[]{:S(2)}) collective-permute-start(f32[3,32,1024]{2,1,0:T(8,128)S(1)} %shard_map.66.refs_8_.refs_1_.refs_7_), channel_id=1, source_target_pairs={{0,31},{1,0},{2,1},{3,2},{4,3},{5,4},{6,5},{7,6},{8,7},{9,8},{10,9... | collective-permute-start | bytes 1179656 | tf_op jit(solution)/shard_map/ppermute | solution.py:389
  34.6 10.5 %collective-permute-start.7 = (f32[3,32,1024]{2,1,0:T(8,128)S(1)}, f32[3,32,1024]{2,1,0:T(8,128)S(1)}, u32[]{:S(2)}, u32[]{:S(2)}) collective-permute-start(f32[3,32,1024]{2,1,0:T(8,128)S(1)} %shard_map.66.refs_8_.refs_1_.refs_7_), channel_id=1, source_target_pairs={{0,1},{1,2},{2,3},{3,4},{4,5},{5,6},{6,7},{7,8},{8,9},{9,10},{10,1... | collective-permute-start | bytes 1179656 | tf_op jit(solution)/shard_map/ppermute | solution.py:389
  42.7 6.7 %collective-permute-start.6 = (f32[3,32,1024]{2,1,0:T(8,128)S(1)}, f32[3,32,1024]{2,1,0:T(8,128)S(1)}, u32[]{:S(2)}, u32[]{:S(2)}) collective-permute-start(f32[3,32,1024]{2,1,0:T(8,128)S(1)} %shard_map.67.refs_7_.refs_1_), channel_id=1, source_target_pairs={{0,31},{1,0},{2,1},{3,2},{4,3},{5,4},{6,5},{7,6},{8,7},{9,8},{10,9... | collective-permute-start | bytes 1179656 | tf_op jit(solution)/shard_map/ppermute | solution.py:389
  44.2 10.5 %collective-permute-start.5 = (f32[3,32,1024]{2,1,0:T(8,128)S(1)}, f32[3,32,1024]{2,1,0:T(8,128)S(1)}, u32[]{:S(2)}, u32[]{:S(2)}) collective-permute-start(f32[3,32,1024]{2,1,0:T(8,128)S(1)} %shard_map.67.refs_7_.refs_1_), channel_id=1, source_target_pairs={{0,1},{1,2},{2,3},{3,4},{4,5},{5,6},{6,7},{7,8},{8,9},{9,10},{10,1... | collective-permute-start | bytes 1179656 | tf_op jit(solution)/shard_map/ppermute | solution.py:389
  59.0 9.5 %collective-permute-start.9 = (f32[3,22,1024]{2,1,0:T(8,128)S(1)}, f32[3,22,1024]{2,1,0:T(8,128)S(1)}, u32[]{:S(2)}, u32[]{:S(2)}) collective-permute-start(f32[3,22,1024]{2,1,0:T(8,128)S(1)} %pad_maximum_fusion), channel_id=1, source_target_pairs={{0,1},{1,2},{2,3},{3,4},{4,5},{5,6},{6,7},{7,8},{8,9},{9,10},{10,1... | collective-permute-start | bytes 811016 | tf_op jit(solution)/shard_map/ppermute | solution.py:417
  59.1 9.4 %collective-permute-start.10 = (f32[3,22,1024]{2,1,0:T(8,128)S(1)}, f32[3,22,1024]{2,1,0:T(8,128)S(1)}, u32[]{:S(2)}, u32[]{:S(2)}) collective-permute-start(f32[3,22,1024]{2,1,0:T(8,128)S(1)} %pad_maximum_fusion.1), channel_id=1, source_target_pairs={{0,31},{1,0},{2,1},{3,2},{4,3},{5,4},{6,5},{7,6},{8,7},{9,8},{10,9... | collective-permute-start | bytes 811016 | tf_op jit(solution)/shard_map/ppermute | solution.py:418
  69.7 14.3 %collective-permute-start.12 = (f32[3,52,1024]{2,1,0:T(8,128)S(1)}, f32[3,52,1024]{2,1,0:T(8,128)S(1)}, u32[]{:S(2)}, u32[]{:S(2)}) collective-permute-start(f32[3,52,1024]{2,1,0:T(8,128)S(1)} %shard_map.70), channel_id=1, source_target_pairs={{0,96},{32,0},{64,32},{96,64},{1,97},{33,1},{65,33},{97,65},{2,98}... | collective-permute-start | bytes 1916936 | tf_op jit(solution)/shard_map/ppermute | solution.py:422
  71.7 15.4 %collective-permute-start.11 = (f32[3,52,1024]{2,1,0:T(8,128)S(1)}, f32[3,52,1024]{2,1,0:T(8,128)S(1)}, u32[]{:S(2)}, u32[]{:S(2)}) collective-permute-start(f32[3,52,1024]{2,1,0:T(8,128)S(1)} %shard_map.70), channel_id=1, source_target_pairs={{0,32},{32,64},{64,96},{96,0},{1,33},{33,65},{65,97},{97,1},{2,34}... | collective-permute-start | bytes 1916936 | tf_op jit(solution)/shard_map/ppermute | solution.py:421
  84.0 7.3 %collective-permute-start.14 = (f32[3,22,1024]{2,1,0:T(8,128)S(1)}, f32[3,22,1024]{2,1,0:T(8,128)S(1)}, u32[]{:S(2)}, u32[]{:S(2)}) collective-permute-start(f32[3,22,1024]{2,1,0:T(8,128)S(1)} %slice.27), channel_id=1, source_target_pairs={{0,96},{32,0},{64,32},{96,64},{1,97},{33,1},{65,33},{97,65},{2,98}... | collective-permute-start | bytes 811016 | tf_op jit(solution)/shard_map/ppermute | solution.py:425
  87.1 8.0 %collective-permute-start.13 = (f32[3,22,1024]{2,1,0:T(8,128)S(1)}, f32[3,22,1024]{2,1,0:T(8,128)S(1)}, u32[]{:S(2)}, u32[]{:S(2)}) collective-permute-start(f32[3,22,1024]{2,1,0:T(8,128)S(1)} %slice.26), channel_id=1, source_target_pairs={{0,32},{32,64},{64,96},{96,0},{1,33},{33,65},{65,97},{97,1},{2,34}... | collective-permute-start | bytes 811016 | tf_op jit(solution)/shard_map/ppermute | solution.py:424

commit v6 on v5

--- a/solution.py
+++ b/solution.py
@@ -160,15 +160,16 @@
         velocity_pass(E, U, V, FY, D, A, None, r, float(FACTOR))
 
 
-def inside_grid(space):
-    return tuple(jnp.where(x, 1.0, 0.0) for x in (space > 0, space < lax.axis_size("space") - 1))
+def place(space):
+    keep = tuple(jnp.where(x, 1.0, 0.0) for x in (space > 0, space < lax.axis_size("space") - 1))
+    return lax.rem(space, 2) == 0, keep, keep[0] * keep[1]
 
 
 def read_own(src, base, g, c):
     return src[c, at(base + g), :]
 
 
-def main_kernel(n, guess, wind, initial, depth, friction, mask, out, last, late, raw, land, matrix, sems):
+def main_kernel(n, guess, wind, initial, depth, friction, mask, out, last, start, raw, land, matrix, sems):
     copies = [
         pltpu.make_async_copy(src, dst, sems.at[i])
         for i, (src, dst) in enumerate(
@@ -178,9 +179,9 @@
                 (depth, raw.at[5]),
                 (friction, raw.at[6]),
                 (mask, land),
+                (wind.at[0], raw.at[pl.ds(7, 2)]),
                 (guess.at[1], last),
-                (initial, late.at[pl.ds(0, 3)]),
-                (wind.at[0], late.at[pl.ds(3, 2)]),
+                (initial, start),
             )
         )
     ]
@@ -193,31 +194,35 @@
     reorder(raw, out, matrix, (slice(None),))
 
 
-def late_kernel(n, pos_ref, earlier, last_raw, late_raw, late, last, raw, matrix):
+def last_kernel(n, _, last_raw, last, matrix):
     matrix[...] = order_matrix(False)
-    raw[pl.ds(0, 3)] = jnp.where(pos_ref[0] == 0, late_raw[pl.ds(0, 3)], earlier[...])
-    raw[pl.ds(3, 2)] = late_raw[pl.ds(3, 2)]
-    reorder(raw, late, matrix, (slice(None),))
     reorder(last_raw, last, matrix, (slice(None),))
 
 
-def load(n, base, keep, state, coefs, fields):
+def late_kernel(n, pos_ref, earlier, start, out, raw, matrix):
+    matrix[...] = order_matrix(False)
+    raw[...] = jnp.where(pos_ref[0] == 0, start[...], earlier[...])
+    reorder(raw, out, matrix, (slice(None),))
+
+
+def load(n, base, space, state, coefs, fields, wind=(), first=0):
     E, U, V, D, A = fields
-    for row, st, cf, ok in zip((base, base - n, base + n), state, coefs, (1.0, *keep)):
+    even, _, inside = place(space)
+    rows = (base, jnp.where(even, base - n, base + n), jnp.where(even, base + n, base - n))
+    for row, st, cf, ok in zip(rows, state, coefs, (1.0, inside, 1.0)):
         copy_in(D, row, cf, plane(5), n, ok * (C * C))
         copy_in(A, row, cf, plane(6), n, ok)
         copy_in(E, row, st, plane(0), n, C)
         copy_in(U, row, st, plane(1), n)
         copy_in(V, row, st, plane(2), n)
-
-
-def fine_kernel(n, space_ref, own, up, dn, coef, coef_up, coef_dn, nxt, delta, E, U, V, FY, D, A, W0, W1):
-    keep = inside_grid(space_ref[0])
+        for k, dst in enumerate(wind):
+            copy_in(dst, row, cf, plane(first + k), n, H)
+
+
+def fine_kernel(wind, n, space_ref, own, across, beside, coef, coef_a, coef_b, nxt, delta, E, U, V, FY, D, A, W0, W1):
+    _, keep, _ = place(space_ref[0])
     base = 40
-    load(n, base, keep, (own, up, dn), (coef, coef_up, coef_dn), (E, U, V, D, A))
-    for row, st in ((base, own), (base - n, up), (base + n, dn)):
-        copy_in(W0, row, st, plane(3), n, H)
-        copy_in(W1, row, st, plane(4), n, H)
+    load(n, base, space_ref[0], (own, across, beside), (coef, coef_a, coef_b), (E, U, V, D, A), (W0, W1), wind)
 
     def prepare(s):
         W0[s] = W0[s] * A[s]
@@ -238,21 +243,21 @@
 
 def relax(n, space_ref, state, coefs, fields):
     E, U, V, FY, D, A = fields
-    keep = inside_grid(space_ref[0])
+    _, keep, _ = place(space_ref[0])
     base = 40
-    load(n, base, keep, state, coefs, (E, U, V, D, A))
+    load(n, base, space_ref[0], state, coefs, (E, U, V, D, A))
     flux_rows(FY, V, D, base - n, 3 * n)
     sweep(E, U, V, FY, D, A, None, base, n, keep)
     return base
 
 
-def relax_b_kernel(n, space_ref, d, up, dn, coef, coef_up, coef_dn, res, E, U, V, FY, D, A):
-    base = relax(n, space_ref, (d, up, dn), (coef, coef_up, coef_dn), (E, U, V, FY, D, A))
+def relax_b_kernel(n, space_ref, d, up, dn, coef, coef_a, coef_b, res, E, U, V, FY, D, A):
+    base = relax(n, space_ref, (d, up, dn), (coef, coef_a, coef_b), (E, U, V, FY, D, A))
     copy_out(res, (E, U, V), base, n)
 
 
-def relax_a_kernel(n, space_ref, d, up, dn, coef, coef_up, coef_dn, d_next, nxt, res, fine, next_fine, E, U, V, FY, D, A):
-    base = relax(n, space_ref, (d, up, dn), (coef, coef_up, coef_dn), (E, U, V, FY, D, A))
+def relax_a_kernel(n, space_ref, d, up, dn, coef, coef_a, coef_b, d_next, nxt, res, fine, next_fine, E, U, V, FY, D, A):
+    base = relax(n, space_ref, (d, up, dn), (coef, coef_a, coef_b), (E, U, V, FY, D, A))
     for f, src in enumerate((E, U, V)):
         for g in range(0, n, 8):
             for c in range(E.shape[0]):
@@ -277,18 +282,26 @@
 RIMS = (2, 6, 10)
 
 
-def coarse_load(n, base, keep, coefs, D, A):
-    coef, up, dn = coefs
-    for row, cf, start, rows, ok in ((base - HALO, up, n - HALO, HALO, keep[0]), (base, coef, 0, n, 1.0), (base + n, dn, 0, HALO, keep[1])):
-        copy_in(D, row, cf, plane(5, start), rows, ok * (C * C))
-        copy_in(A, row, cf, plane(6, start), rows, ok)
+def coarse_load(n, base, space, coefs, D, A):
+    coef, coef_a, coef_b = coefs
+    even, _, inside = place(space)
+    for cond, up, dn, ok_up, ok_dn in ((even, coef_a, coef_b, inside, 1.0), (jnp.logical_not(even), coef_b, coef_a, 1.0, inside)):
+
+        @pl.when(cond)
+        def _(up=up, dn=dn, ok_up=ok_up, ok_dn=ok_dn):
+            for f, dst, k in ((5, D, C * C), (6, A, 1.0)):
+                copy_in(dst, base - HALO, up, plane(f, n - HALO), HALO, ok_up * k)
+                copy_in(dst, base + n, dn, plane(f), HALO, ok_dn * k)
+
+    copy_in(D, base, coef, plane(5), n, C * C)
+    copy_in(A, base, coef, plane(6), n)
     coarse_coefs(D, A, base - HALO, n + 2 * HALO)
 
 
-def source_kernel(n, pos_ref, ra, rb, up, dn, coef, coef_up, coef_dn, out, E, U, V, FY, D, A, X, Y, Z):
+def source_kernel(n, pos_ref, ra, rb, up, dn, coef, coef_a, coef_b, out, E, U, V, FY, D, A, X, Y, Z):
     base, rim = 24, RIMS[2]
-    keep = inside_grid(pos_ref[1])
-    coarse_load(n, base, keep, (coef, coef_up, coef_dn), D, A)
+    _, keep, _ = place(pos_ref[1])
+    coarse_load(n, base, pos_ref[1], (coef, coef_a, coef_b), D, A)
     for fields, own, start, rows in (((E, U, V), ra, 0, rim + 2), ((X, Y, Z), rb, rim + 2, rim)):
         for f, dst in enumerate(fields):
             copy_rows(dst, base - rows, up, f, start, rows)
@@ -304,12 +317,12 @@
                 out[f, at(g, rows), pl.ds(c * LANES, LANES)] = src[s] + more[s]
 
 
-def chain_kernel(n, pos_ref, ca, cc, p1, p2, coef, coef_up, coef_dn, fa, fb, out, E, U, V, FY, D, A, X, Y, Z, result, matrix):
+def chain_kernel(n, pos_ref, ca, cc, p1, p2, coef, coef_a, coef_b, fa, fb, out, E, U, V, FY, D, A, X, Y, Z, result, matrix):
     tm = pos_ref[0]
     base, last, middle = 24, RIMS[2], RIMS[1]
     matrix[...] = order_matrix(True)
-    keep = inside_grid(pos_ref[1])
-    coarse_load(n, base, keep, (coef, coef_up, coef_dn), D, A)
+    _, keep, _ = place(pos_ref[1])
+    coarse_load(n, base, pos_ref[1], (coef, coef_a, coef_b), D, A)
 
     def add():
         def put(s):
@@ -384,38 +397,53 @@
     tm, space = lax.axis_index("tm"), lax.axis_index("space")
     pos = jnp.stack([tm, space]).astype(jnp.int32)
     where = space.astype(jnp.int32)[None]
+    even = space % 2 == 0
+
+    def across(x, ends_meet=False):
+        if ends_meet:
+            return lax.ppermute(x, "space", [(i, (i - 1 if i % 2 == 0 else i + 1) % spaces) for i in range(spaces)])
+        pairs = []
+        for t in range(times):
+            for i in range(spaces):
+                other = t * spaces + (i - 1 if i % 2 == 0 else i + 1)
+                pairs.append((t * spaces + i, (t ^ 1) * spaces + i if i in (0, spaces - 1) else other))
+        return lax.ppermute(x, ("tm", "space"), pairs)
+
+    def beside(x):
+        return lax.ppermute(x, "space", [(i, i ^ 1) for i in range(spaces)])
 
     def sides(x):
-        return lax.ppermute(x, "space", ring(spaces, 1)), lax.ppermute(x, "space", ring(spaces, -1))
+        return across(x), beside(x)
 
     state = in_vmem(3, n, ncols)
     vmem = pl.BlockSpec(memory_space=pltpu.VMEM)
-    b_own, last_raw, late_raw = pl.pallas_call(
+    b_own, last_raw, start = pl.pallas_call(
         functools.partial(main_kernel, n),
-        out_shape=(in_vmem(7, n, ncols), state, in_vmem(5, n, ncols)),
+        out_shape=(in_vmem(9, n, ncols), state, state),
         in_specs=[pl.BlockSpec(memory_space=pltpu.HBM)] * 6,
         out_specs=(vmem,) * 3,
-        scratch_shapes=[in_vmem(7, n, ncols), pltpu.VMEM((n, ncols), mask.dtype), order_scratch(), pltpu.SemaphoreType.DMA((8,))],
+        scratch_shapes=[in_vmem(9, n, ncols), pltpu.VMEM((n, ncols), mask.dtype), order_scratch(), pltpu.SemaphoreType.DMA((8,))],
         compiler_params=pltpu.CompilerParams(vmem_limit_bytes=16 * 2**20),
     )(*(pltpu.with_memory_space_constraint(x, pltpu.HBM) for x in (guess, wind, initial, depth, friction, mask)))
     earlier = lax.ppermute(last_raw, "tm", ring(times, 1))
-    b_up, b_dn = sides(b_own)
-    a_own, last = call(
-        late_kernel, n, ncols, 8, 0, 1, (in_vmem(5, n, ncols), state), pos, earlier, last_raw, late_raw, scratch=(in_vmem(5, n, ncols), order_scratch())
-    )
-    a_up, a_dn = sides(a_own)
-    coefs = (b_own, b_up, b_dn)
-
-    (db,) = call(fine_kernel, n, ncols, 120, 8, SWEEP, (state,), where, b_own, b_up, b_dn, *coefs, last)
-    db_up, db_dn = sides(db)
-    (da,) = call(fine_kernel, n, ncols, 120, 8, SWEEP, (state,), where, a_own, a_up, a_dn, *coefs, b_own, after=(db,))
-    da_up, da_dn = sides(da)
-    (rb,) = call(relax_b_kernel, n, ncols, 120, 6, SWEEP, (state,), where, db, db_up, db_dn, *coefs, after=(da,))
-    ra, fa, fb = call(relax_a_kernel, n, ncols, 120, 6, SWEEP, (state, state, state), where, da, da_up, da_dn, *coefs, db, last, after=(rb,))
+    coefs = (b_own, across(b_own, ends_meet=True), beside(b_own))
+    (last,) = call(last_kernel, n, ncols, 8, 0, 1, (state,), where, last_raw, scratch=(order_scratch(),))
+    (a_own,) = call(late_kernel, n, ncols, 8, 0, 1, (state,), pos, earlier, start, scratch=(state, order_scratch()))
+    a_a, a_b = sides(a_own)
+
+    fine_b, fine_a = functools.partial(fine_kernel, 3), functools.partial(fine_kernel, 7)
+    (db,) = call(fine_b, n, ncols, 120, 8, SWEEP, (state,), where, *coefs, *coefs, last)
+    db_a, db_b = sides(db)
+    (da,) = call(fine_a, n, ncols, 120, 8, SWEEP, (state,), where, a_own, a_a, a_b, *coefs, b_own, after=(db,))
+    da_a, da_b = sides(da)
+    (rb,) = call(relax_b_kernel, n, ncols, 120, 6, SWEEP, (state,), where, db, db_a, db_b, *coefs, after=(da,))
+    ra, fa, fb = call(relax_a_kernel, n, ncols, 120, 6, SWEEP, (state, state, state), where, da, da_a, da_b, *coefs, db, last, after=(rb,))
 
     rim = RIMS[2]
-    up = lax.ppermute(jnp.concatenate([ra[:, -rim - 2 :], rb[:, -rim:]], axis=1), "space", ring(spaces, 1))
-    dn = lax.ppermute(jnp.concatenate([ra[:, : rim + 2], rb[:, :rim]], axis=1), "space", ring(spaces, -1))
+    end = jnp.concatenate([ra[:, -rim - 2 :], rb[:, -rim:]], axis=1)
+    top = jnp.concatenate([ra[:, : rim + 2], rb[:, :rim]], axis=1)
+    rim_a, rim_b = across(jnp.where(even, top, end)), beside(jnp.where(even, end, top))
+    up, dn = jnp.where(even, rim_a, rim_b), jnp.where(even, rim_b, rim_a)
     (c1,) = call(source_kernel, n, ncols, 88, 9, 1000, (in_vmem(3, n + 2 * rim, ncols),), pos, ra, rb, up, dn, *coefs)
 
     ca = lax.ppermute(c1, "tm", ring(times, 1))

time: 99.1 us -> 90.4 us (0.912)
  starting transfers between devices: 29.4 us -> 17.2 us
  local copies, waits for them, and re-layouts: 0.12 us -> 1.86 us
  Pallas kernels: 27 us -> 28.3 us
    ppermute x1, waiting for transfers between devices: 0.01 us -> 15.4 us  [shards(): ca = lax.ppermute(c1, 'tm', ring(times, 1))]
    ppermute x10, starting transfers between devices: 22.6 us -> 9.02 us  [the longest x1 6.01 us: across(): lax.ppermute(x, 'space', [(i, (i - 1 if i % 2 == 0 else i + 1) % spaces)...]
    ppermute x1, waiting for transfers between devices: 12.1 us -> 0.01 us  [shards(): cc = lax.ppermute(c1, 'tm', ring(times, -1))]
    ppermute x1, waiting for transfers between devices: 4.12 us -> 0.01 us  [shards(): p2 = lax.ppermute(cc[:, mid:end], 'tm', ring(times, -1))]
    ppermute x10, waiting for transfers between devices: 14.4 us -> 10.9 us  [the longest x4 9.72 us: across(): return lax.ppermute(x, ('tm', 'space'), pairs)]
    ppermute x1, waiting for transfers between devices: 3.8 us -> 6.06 us  [shards(): p1 = lax.ppermute(ca[:, first:mid], 'tm', ring(times, 1))]
    ppermute x1, waiting for transfers between devices: 7.73 us -> 9.79 us  [shards(): earlier = lax.ppermute(last_raw, 'tm', ring(times, 1))]
    unnamed x0 -> x4, local copies, waits for them, and re-layouts: none -> 1.74 us
  transfers between devices with their start and end apart: 15 -> 15, of which waited for: 9 -> 8; matrix products, arithmetic and copies ran while one was open for 0% -> 0% of each run, Pallas kernels for 16% -> 18%
where the time goes in v6:
time: 90.4 us; the launch traced here: 89.9 us
  waiting for transfers between devices  42.2 us (47%)
  Pallas kernels  28.3 us (31%)
  starting transfers between devices  17.2 us (19%)
  local copies, waits for them, and re-layouts  1.86 us (2%)
    pallas_call x8, Pallas kernels, call(): pl.pallas_call(lambda *refs: kernel(n, *refs[:len(args)], *refs[len(args)...  25.6 us
    ppermute x1, waiting for transfers between devices, shards(): ca = lax.ppermute(c1, 'tm', ring(times, 1))  15.4 us
    ppermute x1, waiting for transfers between devices, shards(): earlier = lax.ppermute(last_raw, 'tm', ring(times, 1))  9.79 us
    ppermute x4, waiting for transfers between devices, across(): return lax.ppermute(x, ('tm', 'space'), pairs)  9.72 us
    ppermute x1, waiting for transfers between devices, shards(): p1 = lax.ppermute(ca[:, first:mid], 'tm', ring(times, 1))  6.06 us
    ppermute x1, starting transfers between devices, across(): lax.ppermute(x, 'space', [(i, (i - 1 if i % 2 == 0 else i + 1) % spaces)...  6.01 us
    ppermute x1, starting transfers between devices, shards(): p2 = lax.ppermute(cc[:, mid:end], 'tm', ring(times, -1))  3.28 us
    ppermute x1, starting transfers between devices, shards(): cc = lax.ppermute(c1, 'tm', ring(times, -1))  2.95 us
  transfers between devices with their start and end apart: 15, of which 8 were waited for; matrix products, arithmetic and copies ran while one was open for 0% of the time, Pallas kernels for 18%

profile of v6, /device:TPU:0, one launch (start us, length us, event | category | flops | bytes accessed | tf_op | source)
XLA Modules:
  0.0 89.9 jit_solution(349857117109917599)
XLA Ops:
  0.0 2.7 %shard_map.64 = (f32[9,32,1024]{2,1,0:T(8,128)S(1)}, f32[3,32,1024]{2,1,0:T(8,128)}, f32[3,32,1024]{2,1,0:T(8,128)S(1)}) custom-call(f32[2,3,32,1024]{3,2,1,0:T(8,128)} %guess.1, f32[2,2,32,1024]{3,2,1,0:T(8,128)} %wind.1, f32[3,32,1024]{2,1,0:T(8,128)} %initial.1, f32[32,1024]{1,0:T(8,128)} %depth.1, f32[32,1024]{1,0:T(8,128)} %friction.1, s32[32,1024]{1,0:T(8,128)} %mask.1), custom_call_target="tpu_custom_call" | custom-call | tf_op jit(solution)/shard_map/pallas_call | solution.py:420
  2.7 0.0 copy-start
  2.7 0.7 copy-done
  3.4 6.0 %collective-permute-start.3 = (f32[9,32,1024]{2,1,0:T(8,128)S(1)}, f32[9,32,1024]{2,1,0:T(8,128)S(1)}, u32[]{:S(2)}, u32[]{:S(2)}) collective-permute-start(f32[9,32,1024]{2,1,0:T(8,128)S(1)} %get-tuple-element.13.refs_1_.refs_4_.refs_7_.refs_5_), channel_id=1, source_target_pairs={{0,31},{1,2},{2,1},{3,4},{4,3},{5,6},{6,5},{7,8},{8,7},{9,10},{10,... | collective-permute-start | bytes 3538952 | tf_op jit(solution)/shard_map/ppermute | solution.py:404
  9.5 0.0 collective-permute-start.4
  9.5 1.5 %collective-permute-start = (f32[3,32,1024]{2,1,0:T(8,128)}, f32[3,32,1024]{2,1,0:T(8,128)}, u32[]{:S(2)}, u32[]{:S(2)}) collective-permute-start(f32[3,32,1024]{2,1,0:T(8,128)} %get-tuple-element.11.refs_1_), channel_id=1, source_target_pairs={{0,32},{32,64},{64,96},{96,0},{1,33},{33,65},{65,97},{97,1},{2,34}... | collective-permute-start | bytes 1179656 | tf_op jit(solution)/shard_map/ppermute | solution.py:428
  11.0 1.7 %shard_map.66.refs_7_.refs_8_ = f32[3,32,1024]{2,1,0:T(8,128)S(1)} custom-call(s32[1]{0:T(128)} %bitcast.1.refs_0_, f32[3,32,1024]{2,1,0:T(8,128)} %get-tuple-element.11.refs_1_), custom_call_target="tpu_custom_call" | custom-call | flops 1000000 | tf_op jit(solution)/shard_map/pallas_call | solution.py:383
  12.6 0.1 pad_add_fusion.refs_0_
  12.7 9.8 %collective-permute-done.refs_1_ = f32[3,32,1024]{2,1,0:T(8,128)} collective-permute-done((f32[3,32,1024]{2,1,0:T(8,128)}, f32[3,32,1024]{2,1,0:T(8,128)}, u32[]{:S(2)}, u32[]{:S(2)}) %collective-permute-start) | collective-permute-done | bytes 393248 | tf_op jit(solution)/shard_map/ppermute | solution.py:428
  22.5 0.0 copy-start.1
  22.5 1.0 %copy-done.1 = f32[3,32,1024]{2,1,0:T(8,128)S(1)} copy-done((f32[3,32,1024]{2,1,0:T(8,128)S(1)}, f32[3,32,1024]{2,1,0:T(8,128)}, u32[]{:S(2)}) %copy-start.1) | copy-done | bytes 393240
  23.5 1.7 %shard_map.65.refs_1_ = f32[3,32,1024]{2,1,0:T(8,128)S(1)} custom-call(s32[2]{0:T(128)S(1)} %pad_add_fusion.refs_0_, f32[3,32,1024]{2,1,0:T(8,128)} %collective-permute-done.refs_1_, f32[3,32,1024]{2,1,0:T(8,128)S(1)} %copy-done.1), custom_call_target="tpu_custom_call" | custom-call | flops 1000000 | tf_op jit(solution)/shard_map/pallas_call | solution.py:383
  25.2 0.4 collective-permute-start.1
  25.6 0.0 collective-permute-start.2
  25.6 0.0 collective-permute-done.3.refs_2_.refs_5_.refs_6_
  25.6 0.0 collective-permute-done.4.refs_3_.refs_6_.refs_7_
  25.6 4.5 %shard_map.67.refs_8_.refs_1_.refs_7_ = f32[3,32,1024]{2,1,0:T(8,128)S(1)} custom-call(s32[1]{0:T(128)} %bitcast.1.refs_0_, f32[9,32,1024]{2,1,0:T(8,128)S(1)} %get-tuple-element.13.refs_1_.refs_4_.refs_7_.refs_5_, f32[9,32,1024]{2,1,0:T(8,128)S(1)} %collective-permute-done.3.refs_2_.refs_5_.refs_6_, ...), custom_call_target="tpu_custom_call" | custom-call | flops 8000000000 | tf_op jit(solution)/shard_map/pallas_call | solution.py:383
  30.1 1.8 %collective-permute-start.7 = (f32[3,32,1024]{2,1,0:T(8,128)S(1)}, f32[3,32,1024]{2,1,0:T(8,128)S(1)}, u32[]{:S(2)}, u32[]{:S(2)}) collective-permute-start(f32[3,32,1024]{2,1,0:T(8,128)S(1)} %shard_map.67.refs_8_.refs_1_.refs_7_), channel_id=1, source_target_pairs={{0,32},{1,2},{2,1},{3,4},{4,3},{5,6},{6,5},{7,8},{8,7},{9,10},{10,... | collective-permute-start | bytes 1179656 | tf_op jit(solution)/shard_map/ppermute | solution.py:410
  31.9 0.0 collective-permute-start.8
  31.9 1.1 %collective-permute-done.1.refs_2_ = f32[3,32,1024]{2,1,0:T(8,128)S(1)} collective-permute-done((f32[3,32,1024]{2,1,0:T(8,128)S(1)}, f32[3,32,1024]{2,1,0:T(8,128)S(1)}, u32[]{:S(2)}, u32[]{:S(2)}) %collective-permute-start.1) | collective-permute-done | bytes 393248 | tf_op jit(solution)/shard_map/ppermute | solution.py:410
  33.0 0.0 collective-permute-done.2.refs_3_
  33.1 4.5 %shard_map.68.refs_7_.refs_1_ = f32[3,32,1024]{2,1,0:T(8,128)S(1)} custom-call(s32[1]{0:T(128)} %bitcast.1.refs_0_, f32[3,32,1024]{2,1,0:T(8,128)S(1)} %shard_map.65.refs_1_, f32[3,32,1024]{2,1,0:T(8,128)S(1)} %collective-permute-done.1.refs_2_, f32[3,32,1024]{2,1,0:T(8,128)S(1)} %collective-permute-done.2.refs_3_, ...), custom_call_target="tpu_custom_call" | custom-call | flops 8000000000 | tf_op jit(solution)/shard_map/pallas_call | solution.py:383
  37.5 0.4 collective-permute-start.5
  37.9 0.0 collective-permute-start.6
  37.9 0.1 collective-permute-done.7.refs_2_
  38.0 0.0 collective-permute-done.8.refs_3_
  38.0 4.1 %shard_map.69.refs_9_.refs_2_ = f32[3,32,1024]{2,1,0:T(8,128)S(1)} custom-call(s32[1]{0:T(128)} %bitcast.1.refs_0_, f32[3,32,1024]{2,1,0:T(8,128)S(1)} %shard_map.67.refs_8_.refs_1_.refs_7_, f32[3,32,1024]{2,1,0:T(8,128)S(1)} %collective-permute-done.7.refs_2_, f32[3,32,1024]{2,1,0:T(8,128)S(1)} %collective-permute-done.8.refs_3_, ...), custom_call_target="tpu_custom_call" | custom-call | flops 8000000000 | tf_op jit(solution)/shard_map/pallas_call | solution.py:383
  42.1 3.3 %collective-permute-done.5.refs_2_ = f32[3,32,1024]{2,1,0:T(8,128)S(1)} collective-permute-done((f32[3,32,1024]{2,1,0:T(8,128)S(1)}, f32[3,32,1024]{2,1,0:T(8,128)S(1)}, u32[]{:S(2)}, u32[]{:S(2)}) %collective-permute-start.5) | collective-permute-done | bytes 393248 | tf_op jit(solution)/shard_map/ppermute | solution.py:410
  45.4 0.0 collective-permute-done.6.refs_3_
  45.4 4.2 %shard_map.70 = (f32[3,32,1024]{2,1,0:T(8,128)S(1)}, f32[3,32,1024]{2,1,0:T(8,128)S(1)}, f32[3,32,1024]{2,1,0:T(8,128)S(1)}) custom-call(s32[1]{0:T(128)} %bitcast.1.refs_0_, f32[3,32,1024]{2,1,0:T(8,128)S(1)} %shard_map.68.refs_7_.refs_1_, f32[3,32,1024]{2,1,0:T(8,128)S(1)} %collective-permute-done.5.refs_2_, ...), custom_call_target="tpu_custom_call" | custom-call | flops 8000000000 | tf_op jit(solution)/shard_map/pallas_call | solution.py:383
  49.6 0.1 fusion
  49.7 0.1 collective-permute-start.10
  49.8 0.4 collective-permute-start.9
  50.2 1.2 %collective-permute-done.10 = f32[3,22,1024]{2,1,0:T(8,128)S(1)} collective-permute-done((f32[3,22,1024]{2,1,0:T(8,128)S(1)}, f32[3,22,1024]{2,1,0:T(8,128)S(1)}, u32[]{:S(2)}, u32[]{:S(2)}) %collective-permute-start.10) | collective-permute-done | bytes 270368 | tf_op jit(solution)/shard_map/ppermute | solution.py:413
  51.4 5.2 %collective-permute-done.9 = f32[3,22,1024]{2,1,0:T(8,128)S(1)} collective-permute-done((f32[3,22,1024]{2,1,0:T(8,128)S(1)}, f32[3,22,1024]{2,1,0:T(8,128)S(1)}, u32[]{:S(2)}, u32[]{:S(2)}) %collective-permute-start.9) | collective-permute-done | bytes 270368 | tf_op jit(solution)/shard_map/ppermute | solution.py:410
  56.7 1.2 %shard_map.71 = f32[3,52,1024]{2,1,0:T(8,128)S(1)} custom-call(s32[2]{0:T(128)S(1)} %pad_add_fusion.refs_0_, f32[3,32,1024]{2,1,0:T(8,128)S(1)} %get-tuple-element.14.refs_1_, f32[3,32,1024]{2,1,0:T(8,128)S(1)} %shard_map.69.refs_9_.refs_2_, f32[3,22,1024]{2,1,0:T(8,128)S(1)} %get-tuple-element.20.refs_3_, f32[3,22,1024]{2,1,0:T(8,128)S(1)} %get-tuple-element.19.refs_4_, ...), custom_call_target="tpu_custom_call" | custom-call | flops 1000000000 | tf_op jit(solution)/shard_map/pallas_call | solution.py:383
  57.8 0.4 collective-permute-start.11
  58.2 2.9 %collective-permute-start.12 = (f32[3,52,1024]{2,1,0:T(8,128)S(1)}, f32[3,52,1024]{2,1,0:T(8,128)S(1)}, u32[]{:S(2)}, u32[]{:S(2)}) collective-permute-start(f32[3,52,1024]{2,1,0:T(8,128)S(1)} %shard_map.71), channel_id=1, source_target_pairs={{0,96},{32,0},{64,32},{96,64},{1,97},{33,1},{65,33},{97,65},{2,98}... | collective-permute-start | bytes 1916936 | tf_op jit(solution)/shard_map/ppermute | solution.py:450
  61.1 15.4 %collective-permute-done.11.refs_1_ = f32[3,52,1024]{2,1,0:T(8,128)S(1)} collective-permute-done((f32[3,52,1024]{2,1,0:T(8,128)S(1)}, f32[3,52,1024]{2,1,0:T(8,128)S(1)}, u32[]{:S(2)}, u32[]{:S(2)}) %collective-permute-start.11) | collective-permute-done | bytes 639008 | tf_op jit(solution)/shard_map/ppermute | solution.py:449
  76.6 0.1 collective-permute-start.13
  76.7 0.0 collective-permute-done.12.refs_2_
  76.7 3.3 %collective-permute-start.14 = (f32[3,22,1024]{2,1,0:T(8,128)S(1)}, f32[3,22,1024]{2,1,0:T(8,128)S(1)}, u32[]{:S(2)}, u32[]{:S(2)}) collective-permute-start(f32[3,22,1024]{2,1,0:T(8,128)S(1)} %slice.27), channel_id=1, source_target_pairs={{0,96},{32,0},{64,32},{96,64},{1,97},{33,1},{65,33},{97,65},{2,98}... | collective-permute-start | bytes 811016 | tf_op jit(solution)/shard_map/ppermute | solution.py:453
  80.0 6.1 %collective-permute-done.13.refs_3_ = f32[3,22,1024]{2,1,0:T(8,128)S(1)} collective-permute-done((f32[3,22,1024]{2,1,0:T(8,128)S(1)}, f32[3,22,1024]{2,1,0:T(8,128)S(1)}, u32[]{:S(2)}, u32[]{:S(2)}) %collective-permute-start.13) | collective-permute-done | bytes 270368 | tf_op jit(solution)/shard_map/ppermute | solution.py:452
  86.1 0.0 collective-permute-done.14.refs_4_
  86.1 3.9 %shard_map.72 = f32[2,3,32,1024]{3,2,1,0:T(8,128)} custom-call(s32[2]{0:T(128)S(1)} %pad_add_fusion.refs_0_, f32[3,52,1024]{2,1,0:T(8,128)S(1)} %collective-permute-done.11.refs_1_, f32[3,52,1024]{2,1,0:T(8,128)S(1)} %collective-permute-done.12.refs_2_, f32[3,22,1024]{2,1,0:T(8,128)S(1)} %collective-permute-done.13.refs_3_, ...), custom_call_target="tpu_custom_call" | custom-call | flops 4000000000 | tf_op jit(solution)/shard_map/pallas_call | solution.py:383
  (5 shorter events, 0.2 us)
Async XLA Ops:
  2.7 0.8 copy-start
  3.4 22.1 %collective-permute-start.3 = (f32[9,32,1024]{2,1,0:T(8,128)S(1)}, f32[9,32,1024]{2,1,0:T(8,128)S(1)}, u32[]{:S(2)}, u32[]{:S(2)}) collective-permute-start(f32[9,32,1024]{2,1,0:T(8,128)S(1)} %get-tuple-element.13.refs_1_.refs_4_.refs_7_.refs_5_), channel_id=1, source_target_pairs={{0,31},{1,2},{2,1},{3,4},{4,3},{5,6},{6,5},{7,8},{8,7},{9,10},{10,... | collective-permute-start | bytes 3538952 | tf_op jit(solution)/shard_map/ppermute | solution.py:404
  9.5 16.1 %collective-permute-start.4 = (f32[9,32,1024]{2,1,0:T(8,128)S(1)}, f32[9,32,1024]{2,1,0:T(8,128)S(1)}, u32[]{:S(2)}, u32[]{:S(2)}) collective-permute-start(f32[9,32,1024]{2,1,0:T(8,128)S(1)} %get-tuple-element.13.refs_1_.refs_4_.refs_7_.refs_5_), channel_id=1, source_target_pairs={{0,1},{1,0},{2,3},{3,2},{4,5},{5,4},{6,7},{7,6},{8,9},{9,8},{10,11... | collective-permute-start | bytes 3538952 | tf_op jit(solution)/shard_map/ppermute | solution.py:413
  9.5 13.1 %collective-permute-start = (f32[3,32,1024]{2,1,0:T(8,128)}, f32[3,32,1024]{2,1,0:T(8,128)}, u32[]{:S(2)}, u32[]{:S(2)}) collective-permute-start(f32[3,32,1024]{2,1,0:T(8,128)} %get-tuple-element.11.refs_1_), channel_id=1, source_target_pairs={{0,32},{32,64},{64,96},{96,0},{1,33},{33,65},{65,97},{97,1},{2,34}... | collective-permute-start | bytes 1179656 | tf_op jit(solution)/shard_map/ppermute | solution.py:428
  22.5 1.0 %copy-start.1 = (f32[3,32,1024]{2,1,0:T(8,128)S(1)}, f32[3,32,1024]{2,1,0:T(8,128)}, u32[]{:S(2)}) copy-start(f32[3,32,1024]{2,1,0:T(8,128)} %copy-done) | copy-start | bytes 1179652
  25.2 7.9 %collective-permute-start.1 = (f32[3,32,1024]{2,1,0:T(8,128)S(1)}, f32[3,32,1024]{2,1,0:T(8,128)S(1)}, u32[]{:S(2)}, u32[]{:S(2)}) collective-permute-start(f32[3,32,1024]{2,1,0:T(8,128)S(1)} %shard_map.65.refs_1_), channel_id=1, source_target_pairs={{0,32},{1,2},{2,1},{3,4},{4,3},{5,6},{6,5},{7,8},{8,7},{9,10},{10,... | collective-permute-start | bytes 1179656 | tf_op jit(solution)/shard_map/ppermute | solution.py:410
  25.6 7.5 %collective-permute-start.2 = (f32[3,32,1024]{2,1,0:T(8,128)S(1)}, f32[3,32,1024]{2,1,0:T(8,128)S(1)}, u32[]{:S(2)}, u32[]{:S(2)}) collective-permute-start(f32[3,32,1024]{2,1,0:T(8,128)S(1)} %shard_map.65.refs_1_), channel_id=1, source_target_pairs={{0,1},{1,0},{2,3},{3,2},{4,5},{5,4},{6,7},{7,6},{8,9},{9,8},{10,11... | collective-permute-start | bytes 1179656 | tf_op jit(solution)/shard_map/ppermute | solution.py:413
  30.1 7.9 %collective-permute-start.7 = (f32[3,32,1024]{2,1,0:T(8,128)S(1)}, f32[3,32,1024]{2,1,0:T(8,128)S(1)}, u32[]{:S(2)}, u32[]{:S(2)}) collective-permute-start(f32[3,32,1024]{2,1,0:T(8,128)S(1)} %shard_map.67.refs_8_.refs_1_.refs_7_), channel_id=1, source_target_pairs={{0,32},{1,2},{2,1},{3,4},{4,3},{5,6},{6,5},{7,8},{8,7},{9,10},{10,... | collective-permute-start | bytes 1179656 | tf_op jit(solution)/shard_map/ppermute | solution.py:410
  31.9 6.0 %collective-permute-start.8 = (f32[3,32,1024]{2,1,0:T(8,128)S(1)}, f32[3,32,1024]{2,1,0:T(8,128)S(1)}, u32[]{:S(2)}, u32[]{:S(2)}) collective-permute-start(f32[3,32,1024]{2,1,0:T(8,128)S(1)} %shard_map.67.refs_8_.refs_1_.refs_7_), channel_id=1, source_target_pairs={{0,1},{1,0},{2,3},{3,2},{4,5},{5,4},{6,7},{7,6},{8,9},{9,8},{10,11... | collective-permute-start | bytes 1179656 | tf_op jit(solution)/shard_map/ppermute | solution.py:413
  37.5 7.9 %collective-permute-start.5 = (f32[3,32,1024]{2,1,0:T(8,128)S(1)}, f32[3,32,1024]{2,1,0:T(8,128)S(1)}, u32[]{:S(2)}, u32[]{:S(2)}) collective-permute-start(f32[3,32,1024]{2,1,0:T(8,128)S(1)} %shard_map.68.refs_7_.refs_1_), channel_id=1, source_target_pairs={{0,32},{1,2},{2,1},{3,4},{4,3},{5,6},{6,5},{7,8},{8,7},{9,10},{10,... | collective-permute-start | bytes 1179656 | tf_op jit(solution)/shard_map/ppermute | solution.py:410
  37.9 7.5 %collective-permute-start.6 = (f32[3,32,1024]{2,1,0:T(8,128)S(1)}, f32[3,32,1024]{2,1,0:T(8,128)S(1)}, u32[]{:S(2)}, u32[]{:S(2)}) collective-permute-start(f32[3,32,1024]{2,1,0:T(8,128)S(1)} %shard_map.68.refs_7_.refs_1_), channel_id=1, source_target_pairs={{0,1},{1,0},{2,3},{3,2},{4,5},{5,4},{6,7},{7,6},{8,9},{9,8},{10,11... | collective-permute-start | bytes 1179656 | tf_op jit(solution)/shard_map/ppermute | solution.py:413
  49.7 1.7 %collective-permute-start.10 = (f32[3,22,1024]{2,1,0:T(8,128)S(1)}, f32[3,22,1024]{2,1,0:T(8,128)S(1)}, u32[]{:S(2)}, u32[]{:S(2)}) collective-permute-start(f32[3,22,1024]{2,1,0:T(8,128)S(1)} %get-tuple-element.17), channel_id=1, source_target_pairs={{0,1},{1,0},{2,3},{3,2},{4,5},{5,4},{6,7},{7,6},{8,9},{9,8},{10,11... | collective-permute-start | bytes 811016 | tf_op jit(solution)/shard_map/ppermute | solution.py:413
  49.8 6.8 %collective-permute-start.9 = (f32[3,22,1024]{2,1,0:T(8,128)S(1)}, f32[3,22,1024]{2,1,0:T(8,128)S(1)}, u32[]{:S(2)}, u32[]{:S(2)}) collective-permute-start(f32[3,22,1024]{2,1,0:T(8,128)S(1)} %get-tuple-element.18), channel_id=1, source_target_pairs={{0,32},{1,2},{2,1},{3,4},{4,3},{5,6},{6,5},{7,8},{8,7},{9,10},{10,... | collective-permute-start | bytes 811016 | tf_op jit(solution)/shard_map/ppermute | solution.py:410
  57.8 18.7 %collective-permute-start.11 = (f32[3,52,1024]{2,1,0:T(8,128)S(1)}, f32[3,52,1024]{2,1,0:T(8,128)S(1)}, u32[]{:S(2)}, u32[]{:S(2)}) collective-permute-start(f32[3,52,1024]{2,1,0:T(8,128)S(1)} %shard_map.71), channel_id=1, source_target_pairs={{0,32},{32,64},{64,96},{96,0},{1,33},{33,65},{65,97},{97,1},{2,34}... | collective-permute-start | bytes 1916936 | tf_op jit(solution)/shard_map/ppermute | solution.py:449
  58.2 18.5 %collective-permute-start.12 = (f32[3,52,1024]{2,1,0:T(8,128)S(1)}, f32[3,52,1024]{2,1,0:T(8,128)S(1)}, u32[]{:S(2)}, u32[]{:S(2)}) collective-permute-start(f32[3,52,1024]{2,1,0:T(8,128)S(1)} %shard_map.71), channel_id=1, source_target_pairs={{0,96},{32,0},{64,32},{96,64},{1,97},{33,1},{65,33},{97,65},{2,98}... | collective-permute-start | bytes 1916936 | tf_op jit(solution)/shard_map/ppermute | solution.py:450
  76.6 9.5 %collective-permute-start.13 = (f32[3,22,1024]{2,1,0:T(8,128)S(1)}, f32[3,22,1024]{2,1,0:T(8,128)S(1)}, u32[]{:S(2)}, u32[]{:S(2)}) collective-permute-start(f32[3,22,1024]{2,1,0:T(8,128)S(1)} %slice.26), channel_id=1, source_target_pairs={{0,32},{32,64},{64,96},{96,0},{1,33},{33,65},{65,97},{97,1},{2,34}... | collective-permute-start | bytes 811016 | tf_op jit(solution)/shard_map/ppermute | solution.py:452
  76.7 9.3 %collective-permute-start.14 = (f32[3,22,1024]{2,1,0:T(8,128)S(1)}, f32[3,22,1024]{2,1,0:T(8,128)S(1)}, u32[]{:S(2)}, u32[]{:S(2)}) collective-permute-start(f32[3,22,1024]{2,1,0:T(8,128)S(1)} %slice.27), channel_id=1, source_target_pairs={{0,96},{32,0},{64,32},{96,64},{1,97},{33,1},{65,33},{97,65},{2,98}... | collective-permute-start | bytes 811016 | tf_op jit(solution)/shard_map/ppermute | solution.py:453

commit v7 on v6

--- a/solution.py
+++ b/solution.py
@@ -169,7 +169,7 @@
     return src[c, at(base + g), :]
 
 
-def main_kernel(n, guess, wind, initial, depth, friction, mask, out, last, start, raw, land, matrix, sems):
+def main_kernel(n, guess, wind, depth, friction, mask, out, last, raw, land, matrix, sems):
     copies = [
         pltpu.make_async_copy(src, dst, sems.at[i])
         for i, (src, dst) in enumerate(
@@ -181,7 +181,6 @@
                 (mask, land),
                 (wind.at[0], raw.at[pl.ds(7, 2)]),
                 (guess.at[1], last),
-                (initial, start),
             )
         )
     ]
@@ -194,15 +193,19 @@
     reorder(raw, out, matrix, (slice(None),))
 
 
-def last_kernel(n, _, last_raw, last, matrix):
+def last_kernel(last_raw, initial, last, start, raw, matrix, sem):
+    copy = pltpu.make_async_copy(initial, raw, sem)
+    copy.start()
     matrix[...] = order_matrix(False)
     reorder(last_raw, last, matrix, (slice(None),))
-
-
-def late_kernel(n, pos_ref, earlier, start, out, raw, matrix):
+    copy.wait()
+    reorder(raw, start, matrix, (slice(None),))
+
+
+def late_kernel(n, pos_ref, earlier, start, out, matrix):
     matrix[...] = order_matrix(False)
-    raw[...] = jnp.where(pos_ref[0] == 0, start[...], earlier[...])
-    reorder(raw, out, matrix, (slice(None),))
+    reorder(earlier, out, matrix, (slice(None),))
+    out[...] = jnp.where(pos_ref[0] == 0, start[...], out[...])
 
 
 def load(n, base, space, state, coefs, fields, wind=(), first=0):
@@ -417,18 +420,31 @@
 
     state = in_vmem(3, n, ncols)
     vmem = pl.BlockSpec(memory_space=pltpu.VMEM)
-    b_own, last_raw, start = pl.pallas_call(
+    hbm = pl.BlockSpec(memory_space=pltpu.HBM)
+    params = pltpu.CompilerParams(vmem_limit_bytes=16 * 2**20)
+
+    def in_hbm(*args):
+        return [pltpu.with_memory_space_constraint(x, pltpu.HBM) for x in args]
+
+    b_own, last_raw = pl.pallas_call(
         functools.partial(main_kernel, n),
-        out_shape=(in_vmem(9, n, ncols), state, state),
-        in_specs=[pl.BlockSpec(memory_space=pltpu.HBM)] * 6,
-        out_specs=(vmem,) * 3,
-        scratch_shapes=[in_vmem(9, n, ncols), pltpu.VMEM((n, ncols), mask.dtype), order_scratch(), pltpu.SemaphoreType.DMA((8,))],
-        compiler_params=pltpu.CompilerParams(vmem_limit_bytes=16 * 2**20),
-    )(*(pltpu.with_memory_space_constraint(x, pltpu.HBM) for x in (guess, wind, initial, depth, friction, mask)))
+        out_shape=(in_vmem(9, n, ncols), state),
+        in_specs=[hbm] * 5,
+        out_specs=(vmem,) * 2,
+        scratch_shapes=[in_vmem(9, n, ncols), pltpu.VMEM((n, ncols), mask.dtype), order_scratch(), pltpu.SemaphoreType.DMA((7,))],
+        compiler_params=params,
+    )(*in_hbm(guess, wind, depth, friction, mask))
     earlier = lax.ppermute(last_raw, "tm", ring(times, 1))
     coefs = (b_own, across(b_own, ends_meet=True), beside(b_own))
-    (last,) = call(last_kernel, n, ncols, 8, 0, 1, (state,), where, last_raw, scratch=(order_scratch(),))
-    (a_own,) = call(late_kernel, n, ncols, 8, 0, 1, (state,), pos, earlier, start, scratch=(state, order_scratch()))
+    last, start = pl.pallas_call(
+        last_kernel,
+        out_shape=(state, state),
+        in_specs=[vmem, hbm],
+        out_specs=(vmem,) * 2,
+        scratch_shapes=[state, order_scratch(), pltpu.SemaphoreType.DMA],
+        compiler_params=params,
+    )(last_raw, *in_hbm(initial))
+    (a_own,) = call(late_kernel, n, ncols, 8, 0, 1, (state,), pos, earlier, start, scratch=(order_scratch(),))
     a_a, a_b = sides(a_own)
 
     fine_b, fine_a = functools.partial(fine_kernel, 3), functools.partial(fine_kernel, 7)

time: 90.4 us -> 89.7 us (level)
  waiting for transfers between devices: 42.2 us -> 39.7 us
  Pallas kernels: 28.3 us -> 29.3 us
    pallas_call x0 -> x1, Pallas kernels: none -> 2.67 us  [shards(): pl.pallas_call(last_kernel, out_shape=(state, state), in_specs=[vmem, hbm...]
    ppermute x1, waiting for transfers between devices: 9.79 us -> 7.31 us  [shards(): earlier = lax.ppermute(last_raw, 'tm', ring(times, 1))]
    pallas_call x8 -> x7, Pallas kernels: 25.6 us -> 24 us  [call(): pl.pallas_call(lambda *refs: kernel(n, *refs[:len(args)], *refs[len(args)...]
    unnamed x4 -> x8, local copies, waits for them, and re-layouts: 1.74 us -> 2.49 us
  transfers between devices with their start and end apart: 15 -> 15, of which waited for: 8 -> 7; matrix products, arithmetic and copies ran while one was open for 0% -> 0% of each run, Pallas kernels for 18% -> 20%
where the time goes in v7:
time: 89.7 us; the launch traced here: 89.2 us
  waiting for transfers between devices  39.7 us (44%)
  Pallas kernels  29.3 us (33%)
  starting transfers between devices  17.2 us (19%)
  local copies, waits for them, and re-layouts  2.61 us (3%)
    pallas_call x7, Pallas kernels, call(): pl.pallas_call(lambda *refs: kernel(n, *refs[:len(args)], *refs[len(args)...  24 us
    ppermute x1, waiting for transfers between devices, shards(): ca = lax.ppermute(c1, 'tm', ring(times, 1))  15.4 us
    ppermute x4, waiting for transfers between devices, across(): return lax.ppermute(x, ('tm', 'space'), pairs)  9.7 us
    ppermute x1, waiting for transfers between devices, shards(): earlier = lax.ppermute(last_raw, 'tm', ring(times, 1))  7.31 us
    ppermute x1, starting transfers between devices, across(): lax.ppermute(x, 'space', [(i, (i - 1 if i % 2 == 0 else i + 1) % spaces)...  6.09 us
    ppermute x1, waiting for transfers between devices, shards(): p1 = lax.ppermute(ca[:, first:mid], 'tm', ring(times, 1))  6.06 us
    ppermute x1, starting transfers between devices, shards(): p2 = lax.ppermute(cc[:, mid:end], 'tm', ring(times, -1))  3.28 us
    ppermute x1, starting transfers between devices, shards(): cc = lax.ppermute(c1, 'tm', ring(times, -1))  2.95 us
  transfers between devices with their start and end apart: 15, of which 7 were waited for; matrix products, arithmetic and copies ran while one was open for 0% of the time, Pallas kernels for 20%

profile of v7, /device:TPU:0, one launch (start us, length us, event | category | flops | bytes accessed | tf_op | source)
XLA Modules:
  0.0 89.2 jit_solution(10968584210820411767)
XLA Ops:
  0.0 2.6 %shard_map.64 = (f32[9,32,1024]{2,1,0:T(8,128)S(1)}, f32[3,32,1024]{2,1,0:T(8,128)}) custom-call(f32[2,3,32,1024]{3,2,1,0:T(8,128)} %guess.1, f32[2,2,32,1024]{3,2,1,0:T(8,128)} %wind.1, f32[32,1024]{1,0:T(8,128)} %depth.1, f32[32,1024]{1,0:T(8,128)} %friction.1, s32[32,1024]{1,0:T(8,128)} %mask.1), custom_call_target="tpu_custom_call" | custom-call | tf_op jit(solution)/shard_map/pallas_call | solution.py:429
  2.6 6.1 %collective-permute-start.3 = (f32[9,32,1024]{2,1,0:T(8,128)S(1)}, f32[9,32,1024]{2,1,0:T(8,128)S(1)}, u32[]{:S(2)}, u32[]{:S(2)}) collective-permute-start(f32[9,32,1024]{2,1,0:T(8,128)S(1)} %get-tuple-element.14.refs_1_.refs_4_.refs_7_.refs_5_), channel_id=1, source_target_pairs={{0,31},{1,2},{2,1},{3,4},{4,3},{5,6},{6,5},{7,8},{8,7},{9,10},{10,... | collective-permute-start | bytes 3538952 | tf_op jit(solution)/shard_map/ppermute | solution.py:407
  8.7 0.0 collective-permute-start.4
  8.7 1.5 %collective-permute-start = (f32[3,32,1024]{2,1,0:T(8,128)}, f32[3,32,1024]{2,1,0:T(8,128)}, u32[]{:S(2)}, u32[]{:S(2)}) collective-permute-start(f32[3,32,1024]{2,1,0:T(8,128)} %get-tuple-element.12.last_raw), channel_id=1, source_target_pairs={{0,32},{32,64},{64,96},{96,0},{1,33},{33,65},{65,97},{97,1},{2,34}... | collective-permute-start | bytes 1179656 | tf_op jit(solution)/shard_map/ppermute | solution.py:437
  10.2 2.7 %shard_map.65 = (f32[3,32,1024]{2,1,0:T(8,128)S(1)}, f32[3,32,1024]{2,1,0:T(8,128)S(1)}) custom-call(f32[3,32,1024]{2,1,0:T(8,128)} %get-tuple-element.12.last_raw, f32[3,32,1024]{2,1,0:T(8,128)} %initial.1), custom_call_target="tpu_custom_call" | custom-call | tf_op jit(solution)/shard_map/pallas_call | solution.py:439
  12.8 0.0 copy-start
  12.8 0.8 copy-done
  13.6 0.0 copy-start.2
  13.6 0.7 copy-done.2
  14.3 0.1 pad_add_fusion.refs_0_
  14.4 7.3 %collective-permute-done.refs_1_ = f32[3,32,1024]{2,1,0:T(8,128)} collective-permute-done((f32[3,32,1024]{2,1,0:T(8,128)}, f32[3,32,1024]{2,1,0:T(8,128)}, u32[]{:S(2)}, u32[]{:S(2)}) %collective-permute-start) | collective-permute-done | bytes 393248 | tf_op jit(solution)/shard_map/ppermute | solution.py:437
  21.7 0.0 copy-start.1
  21.7 1.0 %copy-done.1 = f32[3,32,1024]{2,1,0:T(8,128)S(1)} copy-done((f32[3,32,1024]{2,1,0:T(8,128)S(1)}, f32[3,32,1024]{2,1,0:T(8,128)}, u32[]{:S(2)}) %copy-start.1) | copy-done | bytes 393240
  22.7 0.0 copy-start.3
  22.7 1.7 %shard_map.66.refs_1_ = f32[3,32,1024]{2,1,0:T(8,128)S(1)} custom-call(s32[2]{0:T(128)S(1)} %pad_add_fusion.refs_0_, f32[3,32,1024]{2,1,0:T(8,128)} %collective-permute-done.refs_1_, f32[3,32,1024]{2,1,0:T(8,128)S(1)} %copy-done.1), custom_call_target="tpu_custom_call" | custom-call | flops 1000000 | tf_op jit(solution)/shard_map/pallas_call | solution.py:386
  24.4 0.4 collective-permute-start.1
  24.8 0.0 collective-permute-start.2
  24.8 0.0 collective-permute-done.3.refs_2_.refs_5_.refs_6_
  24.8 0.0 collective-permute-done.4.refs_3_.refs_6_.refs_7_
  24.8 0.0 copy-done.3
  24.8 4.5 %shard_map.67.refs_8_.refs_1_.refs_7_ = f32[3,32,1024]{2,1,0:T(8,128)S(1)} custom-call(s32[1]{0:T(128)} %bitcast.1.refs_0_, f32[9,32,1024]{2,1,0:T(8,128)S(1)} %get-tuple-element.14.refs_1_.refs_4_.refs_7_.refs_5_, f32[9,32,1024]{2,1,0:T(8,128)S(1)} %collective-permute-done.3.refs_2_.refs_5_.refs_6_, ...), custom_call_target="tpu_custom_call" | custom-call | flops 8000000000 | tf_op jit(solution)/shard_map/pallas_call | solution.py:386
  29.3 1.8 %collective-permute-start.7 = (f32[3,32,1024]{2,1,0:T(8,128)S(1)}, f32[3,32,1024]{2,1,0:T(8,128)S(1)}, u32[]{:S(2)}, u32[]{:S(2)}) collective-permute-start(f32[3,32,1024]{2,1,0:T(8,128)S(1)} %shard_map.67.refs_8_.refs_1_.refs_7_), channel_id=1, source_target_pairs={{0,32},{1,2},{2,1},{3,4},{4,3},{5,6},{6,5},{7,8},{8,7},{9,10},{10,... | collective-permute-start | bytes 1179656 | tf_op jit(solution)/shard_map/ppermute | solution.py:413
  31.1 0.0 collective-permute-start.8
  31.1 1.1 %collective-permute-done.1.refs_2_ = f32[3,32,1024]{2,1,0:T(8,128)S(1)} collective-permute-done((f32[3,32,1024]{2,1,0:T(8,128)S(1)}, f32[3,32,1024]{2,1,0:T(8,128)S(1)}, u32[]{:S(2)}, u32[]{:S(2)}) %collective-permute-start.1) | collective-permute-done | bytes 393248 | tf_op jit(solution)/shard_map/ppermute | solution.py:413
  32.3 0.0 collective-permute-done.2.refs_3_
  32.3 4.5 %shard_map.68.refs_7_.refs_1_ = f32[3,32,1024]{2,1,0:T(8,128)S(1)} custom-call(s32[1]{0:T(128)} %bitcast.1.refs_0_, f32[3,32,1024]{2,1,0:T(8,128)S(1)} %shard_map.66.refs_1_, f32[3,32,1024]{2,1,0:T(8,128)S(1)} %collective-permute-done.1.refs_2_, f32[3,32,1024]{2,1,0:T(8,128)S(1)} %collective-permute-done.2.refs_3_, ...), custom_call_target="tpu_custom_call" | custom-call | flops 8000000000 | tf_op jit(solution)/shard_map/pallas_call | solution.py:386
  36.8 0.4 collective-permute-start.5
  37.2 0.0 collective-permute-start.6
  37.2 0.0 collective-permute-done.7.refs_2_
  37.2 0.0 collective-permute-done.8.refs_3_
  37.2 4.1 %shard_map.69.refs_9_.refs_2_ = f32[3,32,1024]{2,1,0:T(8,128)S(1)} custom-call(s32[1]{0:T(128)} %bitcast.1.refs_0_, f32[3,32,1024]{2,1,0:T(8,128)S(1)} %shard_map.67.refs_8_.refs_1_.refs_7_, f32[3,32,1024]{2,1,0:T(8,128)S(1)} %collective-permute-done.7.refs_2_, f32[3,32,1024]{2,1,0:T(8,128)S(1)} %collective-permute-done.8.refs_3_, ...), custom_call_target="tpu_custom_call" | custom-call | flops 8000000000 | tf_op jit(solution)/shard_map/pallas_call | solution.py:386
  41.3 3.3 %collective-permute-done.5.refs_2_ = f32[3,32,1024]{2,1,0:T(8,128)S(1)} collective-permute-done((f32[3,32,1024]{2,1,0:T(8,128)S(1)}, f32[3,32,1024]{2,1,0:T(8,128)S(1)}, u32[]{:S(2)}, u32[]{:S(2)}) %collective-permute-start.5) | collective-permute-done | bytes 393248 | tf_op jit(solution)/shard_map/ppermute | solution.py:413
  44.6 0.0 collective-permute-done.6.refs_3_
  44.7 4.2 %shard_map.70 = (f32[3,32,1024]{2,1,0:T(8,128)S(1)}, f32[3,32,1024]{2,1,0:T(8,128)S(1)}, f32[3,32,1024]{2,1,0:T(8,128)S(1)}) custom-call(s32[1]{0:T(128)} %bitcast.1.refs_0_, f32[3,32,1024]{2,1,0:T(8,128)S(1)} %shard_map.68.refs_7_.refs_1_, f32[3,32,1024]{2,1,0:T(8,128)S(1)} %collective-permute-done.5.refs_2_, ...), custom_call_target="tpu_custom_call" | custom-call | flops 8000000000 | tf_op jit(solution)/shard_map/pallas_call | solution.py:386
  48.9 0.1 fusion
  49.0 0.1 collective-permute-start.10
  49.1 0.4 collective-permute-start.9
  49.4 1.2 %collective-permute-done.10 = f32[3,22,1024]{2,1,0:T(8,128)S(1)} collective-permute-done((f32[3,22,1024]{2,1,0:T(8,128)S(1)}, f32[3,22,1024]{2,1,0:T(8,128)S(1)}, u32[]{:S(2)}, u32[]{:S(2)}) %collective-permute-start.10) | collective-permute-done | bytes 270368 | tf_op jit(solution)/shard_map/ppermute | solution.py:416
  50.6 5.2 %collective-permute-done.9 = f32[3,22,1024]{2,1,0:T(8,128)S(1)} collective-permute-done((f32[3,22,1024]{2,1,0:T(8,128)S(1)}, f32[3,22,1024]{2,1,0:T(8,128)S(1)}, u32[]{:S(2)}, u32[]{:S(2)}) %collective-permute-start.9) | collective-permute-done | bytes 270368 | tf_op jit(solution)/shard_map/ppermute | solution.py:413
  55.9 1.2 %shard_map.71 = f32[3,52,1024]{2,1,0:T(8,128)S(1)} custom-call(s32[2]{0:T(128)S(1)} %pad_add_fusion.refs_0_, f32[3,32,1024]{2,1,0:T(8,128)S(1)} %get-tuple-element.16.refs_1_, f32[3,32,1024]{2,1,0:T(8,128)S(1)} %shard_map.69.refs_9_.refs_2_, f32[3,22,1024]{2,1,0:T(8,128)S(1)} %get-tuple-element.22.refs_3_, f32[3,22,1024]{2,1,0:T(8,128)S(1)} %get-tuple-element.21.refs_4_, ...), custom_call_target="tpu_custom_call" | custom-call | flops 1000000000 | tf_op jit(solution)/shard_map/pallas_call | solution.py:386
  57.1 0.4 collective-permute-start.11
  57.4 3.0 %collective-permute-start.12 = (f32[3,52,1024]{2,1,0:T(8,128)S(1)}, f32[3,52,1024]{2,1,0:T(8,128)S(1)}, u32[]{:S(2)}, u32[]{:S(2)}) collective-permute-start(f32[3,52,1024]{2,1,0:T(8,128)S(1)} %shard_map.71), channel_id=1, source_target_pairs={{0,96},{32,0},{64,32},{96,64},{1,97},{33,1},{65,33},{97,65},{2,98}... | collective-permute-start | bytes 1916936 | tf_op jit(solution)/shard_map/ppermute | solution.py:466
  60.4 15.4 %collective-permute-done.11.refs_1_ = f32[3,52,1024]{2,1,0:T(8,128)S(1)} collective-permute-done((f32[3,52,1024]{2,1,0:T(8,128)S(1)}, f32[3,52,1024]{2,1,0:T(8,128)S(1)}, u32[]{:S(2)}, u32[]{:S(2)}) %collective-permute-start.11) | collective-permute-done | bytes 639008 | tf_op jit(solution)/shard_map/ppermute | solution.py:465
  75.9 0.1 collective-permute-start.13
  75.9 0.0 collective-permute-done.12.refs_2_
  76.0 3.3 %collective-permute-start.14 = (f32[3,22,1024]{2,1,0:T(8,128)S(1)}, f32[3,22,1024]{2,1,0:T(8,128)S(1)}, u32[]{:S(2)}, u32[]{:S(2)}) collective-permute-start(f32[3,22,1024]{2,1,0:T(8,128)S(1)} %slice.27), channel_id=1, source_target_pairs={{0,96},{32,0},{64,32},{96,64},{1,97},{33,1},{65,33},{97,65},{2,98}... | collective-permute-start | bytes 811016 | tf_op jit(solution)/shard_map/ppermute | solution.py:469
  79.3 6.1 %collective-permute-done.13.refs_3_ = f32[3,22,1024]{2,1,0:T(8,128)S(1)} collective-permute-done((f32[3,22,1024]{2,1,0:T(8,128)S(1)}, f32[3,22,1024]{2,1,0:T(8,128)S(1)}, u32[]{:S(2)}, u32[]{:S(2)}) %collective-permute-start.13) | collective-permute-done | bytes 270368 | tf_op jit(solution)/shard_map/ppermute | solution.py:468
  85.3 0.0 collective-permute-done.14.refs_4_
  85.3 3.9 %shard_map.72 = f32[2,3,32,1024]{3,2,1,0:T(8,128)} custom-call(s32[2]{0:T(128)S(1)} %pad_add_fusion.refs_0_, f32[3,52,1024]{2,1,0:T(8,128)S(1)} %collective-permute-done.11.refs_1_, f32[3,52,1024]{2,1,0:T(8,128)S(1)} %collective-permute-done.12.refs_2_, f32[3,22,1024]{2,1,0:T(8,128)S(1)} %collective-permute-done.13.refs_3_, ...), custom_call_target="tpu_custom_call" | custom-call | flops 4000000000 | tf_op jit(solution)/shard_map/pallas_call | solution.py:386
  (5 shorter events, 0.2 us)
Async XLA Ops:
  2.6 22.2 %collective-permute-start.3 = (f32[9,32,1024]{2,1,0:T(8,128)S(1)}, f32[9,32,1024]{2,1,0:T(8,128)S(1)}, u32[]{:S(2)}, u32[]{:S(2)}) collective-permute-start(f32[9,32,1024]{2,1,0:T(8,128)S(1)} %get-tuple-element.14.refs_1_.refs_4_.refs_7_.refs_5_), channel_id=1, source_target_pairs={{0,31},{1,2},{2,1},{3,4},{4,3},{5,6},{6,5},{7,8},{8,7},{9,10},{10,... | collective-permute-start | bytes 3538952 | tf_op jit(solution)/shard_map/ppermute | solution.py:407
  8.7 16.1 %collective-permute-start.4 = (f32[9,32,1024]{2,1,0:T(8,128)S(1)}, f32[9,32,1024]{2,1,0:T(8,128)S(1)}, u32[]{:S(2)}, u32[]{:S(2)}) collective-permute-start(f32[9,32,1024]{2,1,0:T(8,128)S(1)} %get-tuple-element.14.refs_1_.refs_4_.refs_7_.refs_5_), channel_id=1, source_target_pairs={{0,1},{1,0},{2,3},{3,2},{4,5},{5,4},{6,7},{7,6},{8,9},{9,8},{10,11... | collective-permute-start | bytes 3538952 | tf_op jit(solution)/shard_map/ppermute | solution.py:416
  8.7 13.1 %collective-permute-start = (f32[3,32,1024]{2,1,0:T(8,128)}, f32[3,32,1024]{2,1,0:T(8,128)}, u32[]{:S(2)}, u32[]{:S(2)}) collective-permute-start(f32[3,32,1024]{2,1,0:T(8,128)} %get-tuple-element.12.last_raw), channel_id=1, source_target_pairs={{0,32},{32,64},{64,96},{96,0},{1,33},{33,65},{65,97},{97,1},{2,34}... | collective-permute-start | bytes 1179656 | tf_op jit(solution)/shard_map/ppermute | solution.py:437
  12.8 0.8 copy-start
  13.6 0.7 copy-start.2
  21.7 1.0 %copy-start.1 = (f32[3,32,1024]{2,1,0:T(8,128)S(1)}, f32[3,32,1024]{2,1,0:T(8,128)}, u32[]{:S(2)}) copy-start(f32[3,32,1024]{2,1,0:T(8,128)} %copy-done) | copy-start | bytes 1179652
  22.7 2.1 %copy-start.3 = (f32[3,32,1024]{2,1,0:T(8,128)S(1)}, f32[3,32,1024]{2,1,0:T(8,128)}, u32[]{:S(2)}) copy-start(f32[3,32,1024]{2,1,0:T(8,128)} %copy-done.2) | copy-start | bytes 1179652
  24.4 7.9 %collective-permute-start.1 = (f32[3,32,1024]{2,1,0:T(8,128)S(1)}, f32[3,32,1024]{2,1,0:T(8,128)S(1)}, u32[]{:S(2)}, u32[]{:S(2)}) collective-permute-start(f32[3,32,1024]{2,1,0:T(8,128)S(1)} %shard_map.66.refs_1_), channel_id=1, source_target_pairs={{0,32},{1,2},{2,1},{3,4},{4,3},{5,6},{6,5},{7,8},{8,7},{9,10},{10,... | collective-permute-start | bytes 1179656 | tf_op jit(solution)/shard_map/ppermute | solution.py:413
  24.8 7.5 %collective-permute-start.2 = (f32[3,32,1024]{2,1,0:T(8,128)S(1)}, f32[3,32,1024]{2,1,0:T(8,128)S(1)}, u32[]{:S(2)}, u32[]{:S(2)}) collective-permute-start(f32[3,32,1024]{2,1,0:T(8,128)S(1)} %shard_map.66.refs_1_), channel_id=1, source_target_pairs={{0,1},{1,0},{2,3},{3,2},{4,5},{5,4},{6,7},{7,6},{8,9},{9,8},{10,11... | collective-permute-start | bytes 1179656 | tf_op jit(solution)/shard_map/ppermute | solution.py:416
  29.3 7.9 %collective-permute-start.7 = (f32[3,32,1024]{2,1,0:T(8,128)S(1)}, f32[3,32,1024]{2,1,0:T(8,128)S(1)}, u32[]{:S(2)}, u32[]{:S(2)}) collective-permute-start(f32[3,32,1024]{2,1,0:T(8,128)S(1)} %shard_map.67.refs_8_.refs_1_.refs_7_), channel_id=1, source_target_pairs={{0,32},{1,2},{2,1},{3,4},{4,3},{5,6},{6,5},{7,8},{8,7},{9,10},{10,... | collective-permute-start | bytes 1179656 | tf_op jit(solution)/shard_map/ppermute | solution.py:413
  31.1 6.0 %collective-permute-start.8 = (f32[3,32,1024]{2,1,0:T(8,128)S(1)}, f32[3,32,1024]{2,1,0:T(8,128)S(1)}, u32[]{:S(2)}, u32[]{:S(2)}) collective-permute-start(f32[3,32,1024]{2,1,0:T(8,128)S(1)} %shard_map.67.refs_8_.refs_1_.refs_7_), channel_id=1, source_target_pairs={{0,1},{1,0},{2,3},{3,2},{4,5},{5,4},{6,7},{7,6},{8,9},{9,8},{10,11... | collective-permute-start | bytes 1179656 | tf_op jit(solution)/shard_map/ppermute | solution.py:416
  36.8 7.9 %collective-permute-start.5 = (f32[3,32,1024]{2,1,0:T(8,128)S(1)}, f32[3,32,1024]{2,1,0:T(8,128)S(1)}, u32[]{:S(2)}, u32[]{:S(2)}) collective-permute-start(f32[3,32,1024]{2,1,0:T(8,128)S(1)} %shard_map.68.refs_7_.refs_1_), channel_id=1, source_target_pairs={{0,32},{1,2},{2,1},{3,4},{4,3},{5,6},{6,5},{7,8},{8,7},{9,10},{10,... | collective-permute-start | bytes 1179656 | tf_op jit(solution)/shard_map/ppermute | solution.py:413
  37.2 7.5 %collective-permute-start.6 = (f32[3,32,1024]{2,1,0:T(8,128)S(1)}, f32[3,32,1024]{2,1,0:T(8,128)S(1)}, u32[]{:S(2)}, u32[]{:S(2)}) collective-permute-start(f32[3,32,1024]{2,1,0:T(8,128)S(1)} %shard_map.68.refs_7_.refs_1_), channel_id=1, source_target_pairs={{0,1},{1,0},{2,3},{3,2},{4,5},{5,4},{6,7},{7,6},{8,9},{9,8},{10,11... | collective-permute-start | bytes 1179656 | tf_op jit(solution)/shard_map/ppermute | solution.py:416
  49.0 1.7 %collective-permute-start.10 = (f32[3,22,1024]{2,1,0:T(8,128)S(1)}, f32[3,22,1024]{2,1,0:T(8,128)S(1)}, u32[]{:S(2)}, u32[]{:S(2)}) collective-permute-start(f32[3,22,1024]{2,1,0:T(8,128)S(1)} %get-tuple-element.19), channel_id=1, source_target_pairs={{0,1},{1,0},{2,3},{3,2},{4,5},{5,4},{6,7},{7,6},{8,9},{9,8},{10,11... | collective-permute-start | bytes 811016 | tf_op jit(solution)/shard_map/ppermute | solution.py:416
  49.1 6.8 %collective-permute-start.9 = (f32[3,22,1024]{2,1,0:T(8,128)S(1)}, f32[3,22,1024]{2,1,0:T(8,128)S(1)}, u32[]{:S(2)}, u32[]{:S(2)}) collective-permute-start(f32[3,22,1024]{2,1,0:T(8,128)S(1)} %get-tuple-element.20), channel_id=1, source_target_pairs={{0,32},{1,2},{2,1},{3,4},{4,3},{5,6},{6,5},{7,8},{8,7},{9,10},{10,... | collective-permute-start | bytes 811016 | tf_op jit(solution)/shard_map/ppermute | solution.py:413
  57.1 18.7 %collective-permute-start.11 = (f32[3,52,1024]{2,1,0:T(8,128)S(1)}, f32[3,52,1024]{2,1,0:T(8,128)S(1)}, u32[]{:S(2)}, u32[]{:S(2)}) collective-permute-start(f32[3,52,1024]{2,1,0:T(8,128)S(1)} %shard_map.71), channel_id=1, source_target_pairs={{0,32},{32,64},{64,96},{96,0},{1,33},{33,65},{65,97},{97,1},{2,34}... | collective-permute-start | bytes 1916936 | tf_op jit(solution)/shard_map/ppermute | solution.py:465
  57.4 18.5 %collective-permute-start.12 = (f32[3,52,1024]{2,1,0:T(8,128)S(1)}, f32[3,52,1024]{2,1,0:T(8,128)S(1)}, u32[]{:S(2)}, u32[]{:S(2)}) collective-permute-start(f32[3,52,1024]{2,1,0:T(8,128)S(1)} %shard_map.71), channel_id=1, source_target_pairs={{0,96},{32,0},{64,32},{96,64},{1,97},{33,1},{65,33},{97,65},{2,98}... | collective-permute-start | bytes 1916936 | tf_op jit(solution)/shard_map/ppermute | solution.py:466
  75.9 9.5 %collective-permute-start.13 = (f32[3,22,1024]{2,1,0:T(8,128)S(1)}, f32[3,22,1024]{2,1,0:T(8,128)S(1)}, u32[]{:S(2)}, u32[]{:S(2)}) collective-permute-start(f32[3,22,1024]{2,1,0:T(8,128)S(1)} %slice.26), channel_id=1, source_target_pairs={{0,32},{32,64},{64,96},{96,0},{1,33},{33,65},{65,97},{97,1},{2,34}... | collective-permute-start | bytes 811016 | tf_op jit(solution)/shard_map/ppermute | solution.py:468
  76.0 9.3 %collective-permute-start.14 = (f32[3,22,1024]{2,1,0:T(8,128)S(1)}, f32[3,22,1024]{2,1,0:T(8,128)S(1)}, u32[]{:S(2)}, u32[]{:S(2)}) collective-permute-start(f32[3,22,1024]{2,1,0:T(8,128)S(1)} %slice.27), channel_id=1, source_target_pairs={{0,96},{32,0},{64,32},{96,64},{1,97},{33,1},{65,33},{97,65},{2,98}... | collective-permute-start | bytes 811016 | tf_op jit(solution)/shard_map/ppermute | solution.py:469
